TPU v7x, 256 devices: a whole 4x4x8 slice. The times are simulated.
256 devices in a mesh: store: 4 (over y_hi, core), req: 8 (over z), tp: 8 (over y_lo, x).
Axes of the slice: x: 4, y: 4 (y_hi: 2, y_lo: 2; y = y_hi * 2 + y_lo), z: 8, core: 2. Of those that a mesh axis runs over, the one named last changes fastest.
Arguments:
- hidden: bfloat16 [4096, 9216], P('store', 'req'), may hold values from -6 to 6
- row_counts: int32 [4], replicated, may hold values from 128 to 1024, as said below
- ln_gain: float32 [9216], P('req'), may hold values from 0.1 to 1.9
- ln_bias: float32 [9216], P('req'), may hold values from -3 to 3
- key_weight: bfloat16 [9216, 5120], P('req', 'tp'), may hold values from -0.0625 to 0.0625
- value_weight: bfloat16 [9216, 5120], P('req', 'tp'), may hold values from -0.0625 to 0.0625
- suffix_q: bfloat16 [128, 128, 5120], P(('store', 'req'), None, 'tp'), may hold values from -192 to 192
- suffix_k: bfloat16 [128, 128, 5120], P(('store', 'req'), None, 'tp'), may hold values from -4.6 to 4.6
- suffix_v: bfloat16 [128, 128, 5120], P(('store', 'req'), None, 'tp'), may hold values from -6 to 6
- suffix_lengths: int32 [128], P(('store', 'req')), may hold values from 1 to 128, 8192 in all
Outputs:
- context: bfloat16 [128, 128, 5120], P(('store', 'req'), None, 'tp')
Inputs may be any that keep to these rules, and one draw needn't show every extreme that they name: Owner o holds transcript rows in its first row_counts[o] slots; each count is a multiple of 128, the counts sum to 2048, and one owner is full with 1024. Request r's suffix fills its first suffix_lengths[r] slots; the lengths sum to 8192.
All inputs are finite; a program needn't handle non-finite values. No bound on the sum of `suffix_lengths` on one device may be relied on, other than what follows from the above.
Results may differ from a plain program's by a relative error of at most 0.0039.
Values may be sent and summed in bfloat16 or wider, within the bound.
No kernel may reach another device: no remote copies, remote signals or barrier semaphores. Data moves between devices by JAX's collectives and lax.ppermute only.
A program may use at most 128 MiB of HBM per device.

v0:
```python
import math

import jax
import jax.numpy as jnp
from jax import lax
from jax.sharding import PartitionSpec as P

D = 9216
HD = 128


epsilon = 1e-05


def per_device(
    hidden,
    row_counts,
    ln_gain,
    ln_bias,
    key_weight,
    value_weight,
    suffix_q,
    suffix_k,
    suffix_v,
    suffix_lengths,
):
    capacity = hidden.shape[0]
    owners = lax.axis_size("store")
    width_dev = key_weight.shape[1]
    heads_dev = width_dev // HD
    requests = suffix_q.shape[0]
    positions = suffix_q.shape[1]
    query_rows = requests * positions
    score_scale = 1.0 / math.sqrt(HD)
    owner_ids = jnp.arange(owners, dtype=jnp.int32)

    def live_stored(first_row, row_count):
        row_ids = first_row + jnp.arange(row_count, dtype=jnp.int32)
        holder = row_ids // capacity
        limit = jnp.sum(
            jnp.where(holder[:, None] == owner_ids[None, :], row_counts[None, :], 0), axis=1
        )
        return row_ids - holder * capacity < limit

    widened = hidden.astype(jnp.float32)
    row_sums, row_squares = lax.psum(
        (jnp.sum(widened, axis=1), jnp.sum(widened * widened, axis=1)), "req"
    )
    row_mean = row_sums / D
    row_var = row_squares / D - row_mean * row_mean
    normed = (
        (widened - row_mean[:, None]) * lax.rsqrt(row_var + epsilon)[:, None] * ln_gain + ln_bias
    ).astype(jnp.bfloat16)
    query_heads = suffix_q.reshape(requests, positions, heads_dev, HD)
    key_heads = suffix_k.reshape(requests, positions, heads_dev, HD)
    value_heads = suffix_v.reshape(requests, positions, heads_dev, HD)
    own_scores = (
        jnp.einsum("rqhd,rkhd->rqhk", query_heads, key_heads, preferred_element_type=jnp.float32)
        * score_scale
    )
    causal = jnp.arange(positions)[None, :] <= jnp.arange(positions)[:, None]
    own_scores = jnp.where(causal[None, :, None, :], own_scores, -jnp.inf)
    top_own = jnp.max(own_scores, axis=-1)
    own_weights = jnp.exp(own_scores - top_own[..., None]).astype(jnp.bfloat16)
    own_totals = jnp.sum(own_weights, axis=-1, dtype=jnp.float32)
    own_context = jnp.einsum(
        "rqhk,rkhd->rqhd", own_weights, value_heads, preferred_element_type=jnp.float32
    )
    start_state = (
        top_own.reshape(query_rows, heads_dev),
        own_totals.reshape(query_rows, heads_dev),
        own_context.reshape(query_rows, heads_dev, HD),
    )
    queries = suffix_q.reshape(query_rows, heads_dev, HD)
    key_part = jnp.dot(normed, key_weight, preferred_element_type=jnp.float32)
    value_part = jnp.dot(normed, value_weight, preferred_element_type=jnp.float32)
    key_values = lax.psum_scatter(
        jnp.concatenate([key_part, value_part], axis=1), "req", scatter_dimension=0, tiled=True
    ).astype(jnp.bfloat16)
    shard_rows = lax.all_gather(key_values, ("store", "req"), axis=0, tiled=True)
    row_total = shard_rows.shape[0]
    block_rows = math.gcd(row_total, 512)
    blocks = shard_rows.reshape(row_total // block_rows, block_rows, 2 * width_dev)
    offsets = block_rows * jnp.arange(row_total // block_rows, dtype=jnp.int32)

    def one_block(state, block_item):
        key_value, offset = block_item
        key_block = key_value[:, :width_dev].reshape(block_rows, heads_dev, HD)
        value_block = key_value[:, width_dev:].reshape(block_rows, heads_dev, HD)
        scores = (
            jnp.einsum("qhd,khd->qhk", queries, key_block, preferred_element_type=jnp.float32)
            * score_scale
        )
        scores = jnp.where(live_stored(offset, block_rows)[None, None, :], scores, -jnp.inf)
        top_now, totals, context = state
        top_next = jnp.maximum(top_now, jnp.max(scores, axis=-1))
        factor = jnp.exp(top_now - top_next)
        weights = jnp.exp(scores - top_next[..., None]).astype(jnp.bfloat16)
        totals = totals * factor + jnp.sum(weights, axis=-1, dtype=jnp.float32)
        context = context * factor[..., None] + jnp.einsum(
            "qhk,khd->qhd", weights, value_block, preferred_element_type=jnp.float32
        )
        return ((top_next, totals, context), None)

    state_next, ignored = lax.scan(one_block, start_state, (blocks, offsets))
    top_end, totals, context = state_next
    result = context / totals[..., None]
    live_queries = (jnp.arange(positions)[None, :] < suffix_lengths[:, None]).reshape(query_rows)
    result = jnp.where(live_queries[:, None, None], result, 0.0).astype(jnp.bfloat16)
    return result.reshape(requests, positions, width_dev)


def solution(mesh):
    in_specs = (
        P("store", "req"),
        P(),
        P("req"),
        P("req"),
        P("req", "tp"),
        P("req", "tp"),
        P(("store", "req"), None, "tp"),
        P(("store", "req"), None, "tp"),
        P(("store", "req"), None, "tp"),
        P(("store", "req")),
    )
    out_specs = P(("store", "req"), None, "tp")
    return jax.shard_map(
        per_device, mesh=mesh, in_specs=in_specs, out_specs=out_specs, check_vma=False
    )
```

profile of v0, /device:TPU:1, one launch (start us, length us, event | category | flops | bytes accessed | tf_op | source)
XLA Modules:
  0.0 301.5 jit_solution(8942424238306026077)
XLA Ops:
  6.5 2.6 convert_reduce_fusion.1
  9.1 17.5 %all-reduce = (f32[1024]{0:T(1024)S(1)}, f32[1024]{0:T(1024)S(1)}) all-reduce(f32[1024]{0:T(1024)S(1)} %get-tuple-element.173, f32[1024]{0:T(1024)S(1)} %get-tuple-element.172), channel_id=1, replica_groups=mesh['store'=4,'req'=8,'tp'=8] {'req'}, use_global_device_ids=true, to_apply=%region_5.6 | all-reduce | flops 2048 | bytes 16384 | tf_op jit(solution)/shard_map/psum | solution.py:46
  26.7 4.0 %fusion.17 = f32[1024,640]{0,1:T(8,128)S(1)} fusion(bf16[1152,640]{1,0:T(8,128)(2,1)S(1)} %copy-done, bf16[1024,1152]{1,0:T(8,128)(2,1)} %param.12, f32[1152]{0:T(1024)} %param.15, f32[1152]{0:T(1024)} %param.14, f32[1024]{0:T(1024)S(1)} %get-tuple-element.199, f32[1024]{0:T(1024)S(1)} %get-tuple-element.198), kind=kOutput, calls=%fused_computation.47 | convolution fusion | flops 1517027328 | bytes 6472704 | tf_op jit(solution)/shard_map/dot_general | solution.py:76
  30.8 2.3 fusion.19
  33.1 3.0 pad_maximum_fusion
  36.3 66.9 %reduce-scatter.2.cloned.1.call-done = f32[128,1280]{0,1:T(8,128)} async-done(((f32[1024,1280]{0,1:T(8,128)}), f32[128,1280]{0,1:T(8,128)}) %reduce-scatter.2.cloned.1.call-update) | async-done | bytes 655376 | tf_op jit(solution)/shard_map/reduce_scatter | solution.py:77
  103.2 1.8 convert_element_type.34
  105.4 1.7 reshape.131
  107.2 1.4 copy.50
  108.6 1.4 copy.54
  111.0 1.2 copy.57
  112.3 1.7 copy.59
  114.0 1.3 copy.61
  115.4 1.6 convert_reduce_fusion.2
  117.0 106.5 %all-gather.2.cloned.1.call-done = bf16[4096,1280]{0,1:T(8,128)(2,1)} async-done(((bf16[128,1280]{0,1:T(8,128)(2,1)}), bf16[4096,1280]{0,1:T(8,128)(2,1)}) %all-gather.2.cloned.1.call-update) | async-done | bytes 10485776 | tf_op jit(solution)/shard_map/all_gather | solution.py:80
  223.6 8.8 %copy.73 = bf16[160,8,8,512]{3,2,0,1:T(8,128)(2,1)} copy(bf16[160,8,8,512]{3,2,1,0:T(8,128)(2,1)} %bitcast.72) | data formatting | bytes 20971520 | tf_op jit(solution)/shard_map/reshape | solution.py:83
  232.4 60.4 %while.17 = (s32[]{:T(128)}, f32[512,5]{0,1:T(8,128)S(1)}, f32[512,5]{0,1:T(8,128)S(1)}, f32[512,5,128]{0,2,1:T(8,128)S(1)}, s32[8]{0:T(128)S(1)}, /*index=5*/s3...) while((s32[]{:T(128)}, f32[512,5]{0,1:T(8,128)S(1)}, ...), condition=%wide.region_11.12_spmd.clone, body=%wide.region_7.11_spmd.clone.sunk | while | flops 688812032 | bytes 25733252 | solution.py:105
  233.0 0.7 add_select_fusion.2
  233.7 0.7 subtract_compare_fusion.2
  234.4 1.4 dynamic-slice_bitcast_fusion.2
  235.9 1.2 bitcast_reduce_fusion.2
  237.2 1.2 convert_reduce_fusion.4
  238.4 1.5 fusion.42
  240.5 0.7 add_select_fusion.2
  241.3 0.7 subtract_compare_fusion.2
  241.9 1.4 dynamic-slice_bitcast_fusion.2
  243.4 1.3 bitcast_reduce_fusion.2
  244.7 1.2 convert_reduce_fusion.4
  245.9 1.5 fusion.42
  248.1 0.7 add_select_fusion.2
  248.8 0.7 subtract_compare_fusion.2
  249.5 1.4 dynamic-slice_bitcast_fusion.2
  251.0 1.3 bitcast_reduce_fusion.2
  252.3 1.2 convert_reduce_fusion.4
  253.5 1.5 fusion.42
  255.6 0.7 add_select_fusion.2
  256.4 0.7 subtract_compare_fusion.2
  257.0 1.4 dynamic-slice_bitcast_fusion.2
  258.5 1.3 bitcast_reduce_fusion.2
  259.8 1.2 convert_reduce_fusion.4
  261.0 1.5 fusion.42
  263.2 0.7 add_select_fusion.2
  263.9 0.7 subtract_compare_fusion.2
  264.6 1.4 dynamic-slice_bitcast_fusion.2
  266.1 1.3 bitcast_reduce_fusion.2
  267.4 1.2 convert_reduce_fusion.4
  268.6 1.5 fusion.42
  270.7 0.7 add_select_fusion.2
  271.5 0.7 subtract_compare_fusion.2
  272.1 1.4 dynamic-slice_bitcast_fusion.2
  273.7 1.3 bitcast_reduce_fusion.2
  274.9 1.2 convert_reduce_fusion.4
  276.1 1.5 fusion.42
  279.0 0.7 subtract_compare_fusion.2
  279.7 1.4 dynamic-slice_bitcast_fusion.2
  281.2 1.3 bitcast_reduce_fusion.2
  282.5 1.2 convert_reduce_fusion.4
  283.7 1.5 fusion.42
  286.6 0.7 subtract_compare_fusion.2
  287.3 1.4 dynamic-slice_bitcast_fusion.2
  288.8 1.3 bitcast_reduce_fusion.2
  290.0 1.2 convert_reduce_fusion.4
  291.2 1.5 fusion.42
  293.1 1.5 copy.62
  (81 shorter events, 9.6 us)
Async XLA Ops:
  6.5 20.1 %copy-start = (bf16[1152,640]{1,0:T(8,128)(2,1)S(1)}, bf16[1152,640]{1,0:T(8,128)(2,1)}, u32[]{:S(2)}) copy-start(bf16[1152,640]{1,0:T(8,128)(2,1)} %param.17) | copy-start | bytes 4423684
  6.5 96.7 %reduce-scatter.2.cloned.1.call-start = ((), (), s32[]{:S(2)}) async-start(), calls=%async_computation.1 | async-start | bytes 5898240 | tf_op jit(solution)/shard_map/reduce_scatter | solution.py:77
  26.6 4.1 %copy-start.3 = (bf16[1024,1152]{1,0:T(8,128)(2,1)S(1)}, bf16[1024,1152]{1,0:T(8,128)(2,1)}, u32[]{:S(2)}) copy-start(bf16[1024,1152]{1,0:T(8,128)(2,1)} %param.12) | copy-start | bytes 7077892
  26.7 4.1 %copy-start.5 = (bf16[1152,640]{1,0:T(8,128)(2,1)S(1)}, bf16[1152,640]{1,0:T(8,128)(2,1)}, u32[]{:S(2)}) copy-start(bf16[1152,640]{1,0:T(8,128)(2,1)} %param.16) | copy-start | bytes 4423684
  26.7 4.1 %copy-start.6 = (f32[1152]{0:T(1024)S(1)}, f32[1152]{0:T(1024)}, u32[]{:S(2)}) copy-start(f32[1152]{0:T(1024)} %param.15) | copy-start | bytes 13828
  26.7 4.1 %copy-start.7 = (f32[1152]{0:T(1024)S(1)}, f32[1152]{0:T(1024)}, u32[]{:S(2)}) copy-start(f32[1152]{0:T(1024)} %param.14) | copy-start | bytes 13828
  36.1 69.0 %copy-start.2 = (bf16[4,128,640]{2,1,0:T(8,128)(2,1)S(1)}, bf16[4,128,640]{2,1,0:T(8,128)(2,1)}, u32[]{:S(2)}) copy-start(bf16[4,128,640]{2,1,0:T(8,128)(2,1)} %param.18) | copy-start | bytes 1966084
  36.1 187.5 %all-gather.2.cloned.1.call-start = ((), (), s32[]{:S(2)}) async-start(), calls=%async_computation.2 | async-start | bytes 10813440 | tf_op jit(solution)/shard_map/all_gather | solution.py:80
  110.4 1.9 copy-start.1
  112.3 4.6 %copy-start.8 = (s32[4]{0:T(128)S(1)}, s32[4]{0:T(128)}, u32[]{:S(2)}) copy-start(s32[4]{0:T(128)} %param.21) | copy-start | bytes 52
  223.5 8.8 %copy-start.4 = (s32[4]{0:T(128)S(1)}, s32[4]{0:T(128)}, u32[]{:S(2)}) copy-start(s32[4]{0:T(128)} %param.13) | copy-start | bytes 52
Sparse Core Ops, SparseCore 0:
  36.2 66.9 reduce-scatter.1
  105.8 117.7 all-gather.1
where the time goes:
time: 302 us; the launch traced here: 301 us
  waiting for transfers between devices  173 us (57%)
  local copies, waits for them, and re-layouts  36.3 us (12%)
  other arithmetic  29.9 us (10%)
  matrix products  29.7 us (10%)
  blocking collectives  17.5 us (6%)
  between operations  13.6 us (5%)
    all_gather x1, waiting for transfers between devices, per_device(): lax.all_gather(key_values, ('store', 'req'), axis=0, tiled=True)  107 us
    reduce_scatter x1, waiting for transfers between devices, per_device(): lax.psum_scatter(jnp.concatenate([key_part, value_part], axis=1), 'req',...  66.9 us
    psum x1, blocking collectives, per_device(): lax.psum((jnp.sum(widened, axis=1), jnp.sum(widened * widened, axis=1)),...  17.5 us
    dot_general x8, matrix products, one_block(): jnp.einsum('qhk,khd->qhd', weights, value_block, preferred_element_type=j...  12.3 us
    squeeze x8, local copies, waits for them, and re-layouts, per_device(): state_next, ignored = lax.scan(one_block, start_state, (blocks, offsets))  11.3 us
    dot_general x8, matrix products, one_block(): jnp.einsum('qhd,khd->qhk', queries, key_block, preferred_element_type=jnp...  10 us
    reduce_sum x8, other arithmetic, one_block(): totals = totals * factor + jnp.sum(weights, axis=-1, dtype=jnp.float32)  9.4 us
    reshape x1, local copies, waits for them, and re-layouts, per_device(): shard_rows.reshape(row_total // block_rows, block_rows, 2 * width_dev)  8.83 us
  transfers between devices with their start and end apart: 2, of which 2 were waited for; matrix products, arithmetic and copies ran while one was open for 4% of the time, Pallas kernels for 0%

commit v1 on v0

v1 whole, which is shorter than its diff:
```python
import functools
import math

import jax
import jax.numpy as jnp
from jax import lax
from jax.experimental import pallas as pl
from jax.experimental.pallas import tpu as pltpu
from jax.sharding import PartitionSpec as P

HD = 128
UNIT = 128
MOST_UNITS = 14
SPAN = 16 * MOST_UNITS
TAIL = 8
epsilon = 1e-05
MIB = 1 << 20


def projection_kernel(
    counts, hidden, hidden_other, gain, bias, key_weight, value_weight, *rest
):
    parts, (rows_in, semaphores) = rest[:5], rest[5:]
    store = lax.axis_index("store")
    me = lax.axis_index("req")
    core = lax.rem(store, 2)
    first_count = counts[store - core]
    second_count = counts[store - core + 1]
    share = (first_count + second_count) // 8
    width = hidden.shape[1]
    cols = key_weight.shape[1]
    weights = (key_weight, value_weight)

    def copies(act):
        for side, source in enumerate((hidden, hidden_other)):
            first = (core + side) % 2 == 0
            count = jnp.where(first, first_count, second_count)
            base = jnp.where(first, 0, first_count)
            for unit in range(source.shape[0] // UNIT):

                @pl.when(unit * UNIT < count)
                def _():
                    at = pl.multiple_of(base + unit * UNIT, UNIT)
                    act(
                        pltpu.make_async_copy(
                            source.at[pl.ds(unit * UNIT, UNIT)],
                            rows_in.at[pl.ds(at, UNIT)],
                            semaphores.at[side, unit],
                        )
                    )

    copies(lambda copy: copy.start())

    row_id = lax.broadcasted_iota(jnp.int32, (16, width), 0)
    affine = jnp.where(row_id == 2, gain[...], jnp.where(row_id == 3, bias[...], 0.0))
    pieces = []
    left = affine
    for _ in range(3):
        piece = left.astype(jnp.bfloat16)
        pieces.append(piece)
        left = left - piece.astype(jnp.float32)
    affine_sums = [
        sum(
            jnp.dot(piece, weight[...], preferred_element_type=jnp.float32) for piece in pieces
        )
        for weight in weights
    ]
    copies(lambda copy: copy.wait())

    tail_row = lax.broadcasted_iota(jnp.int32, (TAIL, cols), 0)
    lane = lax.broadcasted_iota(jnp.int32, (128, 128), 1)

    def project(part, steps, halves):
        target = lax.rem(me + jnp.where(core == 0, steps, 8 - steps), 8)
        start = pl.multiple_of(target * share, 16)
        wide = rows_in[pl.ds(start, SPAN), :].astype(jnp.float32)
        row_sum = jnp.sum(wide, axis=1, keepdims=True)
        row_square = jnp.sum(wide * wide, axis=1, keepdims=True)
        centre = row_sum * (1.0 / width)
        scaled = ((wide - centre) * gain[...]).astype(jnp.bfloat16)
        flipped = []
        for at in range(0, SPAN, 128):
            count = min(128, SPAN - at)
            column = jnp.where(
                lane[:count] == 0,
                row_sum[at : at + count],
                jnp.where(lane[:count] == 1, row_square[at : at + count], 0.0),
            )
            if count < 128:
                column = jnp.concatenate(
                    [column, jnp.zeros((128 - count, 128), jnp.float32)], axis=0
                )
            flipped.append(jnp.transpose(column)[:TAIL])
        flipped = jnp.concatenate(flipped, axis=1)
        for half, at in halves:
            affine_sum = affine_sums[half]
            part[0:SPAN, at : at + cols] = (
                jnp.dot(scaled, weights[half][...], preferred_element_type=jnp.float32)
                + centre * affine_sum[2:3]
            )
            tail = jnp.where(
                jnp.logical_or(tail_row == 2, tail_row == 3), affine_sum[0:TAIL], 0.0
            )
            part[SPAN : SPAN + TAIL, at : at + cols] = tail
            part[SPAN : SPAN + TAIL, at : at + 256] = jnp.where(
                tail_row[:, :256] < 2, flipped, tail[:, :256]
            )

    for k in (0, 4):
        for half in range(2):

            @pl.when(core == half)
            def _():
                project(parts[k], 4 - k, ((half, 0),))

    for k in (1, 2, 3):
        project(parts[k], 4 - k, ((0, 0), (1, cols)))


def project_rows(counts, hidden, hidden_other, gain, bias, key_weight, value_weight):
    width = hidden.shape[1]
    cols = key_weight.shape[1]
    vmem = pl.BlockSpec(memory_space=pltpu.VMEM)
    hbm = pl.BlockSpec(memory_space=pl.ANY)
    return pl.pallas_call(
        projection_kernel,
        out_shape=[
            jax.ShapeDtypeStruct((SPAN + TAIL, n * cols), jnp.float32) for n in (1, 2, 2, 2, 1)
        ],
        in_specs=[pl.BlockSpec(memory_space=pltpu.SMEM), hbm, hbm] + [vmem] * 4,
        out_specs=[vmem] * 5,
        scratch_shapes=[
            pltpu.VMEM((MOST_UNITS * UNIT, width), jnp.bfloat16),
            pltpu.SemaphoreType.DMA((2, hidden.shape[0] // UNIT)),
        ],
        compiler_params=pltpu.CompilerParams(vmem_limit_bytes=40 * MIB),
        cost_estimate=pl.CostEstimate(
            flops=8 * SPAN * width * 2 * cols, bytes_accessed=12 * MIB, transcendentals=0
        ),
    )(counts, hidden, hidden_other, gain, bias, key_weight, value_weight)


def attention_kernel(begin, end, pair_count, *refs):
    refs = list(refs)
    if end:
        lengths = refs.pop(0)
    q = refs.pop(0)
    if begin:
        own_k, own_v = refs.pop(0), refs.pop(0)
    else:
        state = refs.pop(0)
    blocks = refs[: 4 * pair_count]
    out = refs[-1]
    requests, positions, _ = q.shape
    rows = requests * positions
    rate = math.log2(math.e) / math.sqrt(HD)
    first_core = lax.rem(lax.axis_index("store"), 2) == 0

    def scores_of(queries, block):
        return lax.dot_general(
            queries, block, (((1,), (1,)), ((), ())), preferred_element_type=jnp.float32
        )

    def weigh(scores, top, block):
        weights = jnp.exp2((scores - top) * rate).astype(jnp.bfloat16)
        both = jnp.concatenate([block, jnp.ones(block.shape, jnp.bfloat16)], axis=1)
        return jnp.dot(weights, both, preferred_element_type=jnp.float32)

    if begin:
        row = lax.broadcasted_iota(jnp.int32, (positions, positions), 0)
        column = lax.broadcasted_iota(jnp.int32, (positions, positions), 1)
        tops, sums = [], []
        for r in range(requests):
            scores = jnp.where(column <= row, scores_of(q[r], own_k[r]), -jnp.inf)
            top = jnp.max(scores, axis=1, keepdims=True)
            tops.append(top)
            sums.append(weigh(scores, top, own_v[r]))
        top = jnp.concatenate(tops, axis=0)
        total = jnp.concatenate(sums, axis=0)
    else:
        right = state[0, :, HD:]
        top = right[:, HD // 2 : HD // 2 + 1]
        total = jnp.concatenate(
            [state[0, :, :HD], jnp.broadcast_to(right[:, 0:1], (rows, HD))], axis=1
        )
    queries = q[...].reshape(rows, HD)

    def pick(i):
        return jnp.where(first_core, blocks[2 * i][...], blocks[2 * i + 1][...])

    for i in range(pair_count):
        scores = scores_of(queries, pick(2 * i))
        top_next = jnp.maximum(top, jnp.max(scores, axis=1, keepdims=True))
        factor = jnp.exp2((top - top_next) * rate)
        total = total * factor + weigh(scores, top_next, pick(2 * i + 1))
        top = top_next
    if end:
        result = total[:, :HD] / total[:, HD:]
        place = lax.broadcasted_iota(jnp.int32, (positions, HD), 0)
        for r in range(requests):
            part = result[r * positions : (r + 1) * positions]
            out[r] = jnp.where(place < lengths[r], part, 0.0).astype(jnp.bfloat16)
    else:
        lane = lax.broadcasted_iota(jnp.int32, (rows, HD), 1)
        out[0, :, :HD] = total[:, :HD]
        out[0, :, HD:] = jnp.where(lane < HD // 2, total[:, HD:], top)


def attend(q, pairs, suffix=None, state=None, lengths=None):
    requests, positions, width = q.shape
    rows = requests * positions
    heads = width // HD
    whole = pl.BlockSpec((requests, positions, HD), lambda h: (0, 0, h))
    carried = pl.BlockSpec((1, rows, 2 * HD), lambda h: (h, 0, 0))
    specs, operands = [], []
    if lengths is not None:
        specs.append(pl.BlockSpec(memory_space=pltpu.SMEM))
        operands.append(lengths)
    specs.append(whole)
    operands.append(q)
    if suffix is not None:
        specs += [whole] * 2
        operands += list(suffix)
    else:
        specs.append(carried)
        operands.append(state)
    key_rows = positions if suffix is not None else 0
    for pair in pairs:
        key_rows += pair[0][0].shape[0]
        for array, at in pair:
            specs.append(pl.BlockSpec((array.shape[0], HD), lambda h, at=at: (0, at + h)))
            operands.append(array)
    if lengths is not None:
        out_shape, out_spec = jax.ShapeDtypeStruct(q.shape, jnp.bfloat16), whole
    else:
        out_shape, out_spec = jax.ShapeDtypeStruct((heads, rows, 2 * HD), jnp.float32), carried
    return pl.pallas_call(
        functools.partial(
            attention_kernel, suffix is not None, lengths is not None, len(pairs)
        ),
        grid=(heads,),
        out_shape=out_shape,
        in_specs=specs,
        out_specs=out_spec,
        compiler_params=pltpu.CompilerParams(vmem_limit_bytes=40 * MIB),
        cost_estimate=pl.CostEstimate(
            flops=4 * rows * key_rows * width,
            bytes_accessed=6 * MIB,
            transcendentals=rows * key_rows * heads,
        ),
    )(*operands)


def per_device(
    hidden,
    row_counts,
    ln_gain,
    ln_bias,
    key_weight,
    value_weight,
    suffix_q,
    suffix_k,
    suffix_v,
    suffix_lengths,
):
    cols = key_weight.shape[1]
    heads = cols // HD
    store = lax.axis_index("store")
    first_core = store % 2 == 0
    stores = lax.axis_size("store")
    ring = lax.axis_size("req")
    depth = ring * key_weight.shape[0]
    around = [
        (s * ring + z, s * ring + (z + (1 if s % 2 == 0 else ring - 1)) % ring)
        for s in range(stores)
        for z in range(ring)
    ]
    across = [(s, s + 1 - 2 * (s % 2)) for s in range(stores)]
    far = [(s, (s + 2) % 4) for s in range(stores)]

    def step(array):
        return lax.ppermute(array, ("store", "req"), around)

    def swap(array):
        return lax.ppermute(array, "store", across)

    def ordered(mine, other):
        return jnp.where(
            first_core,
            jnp.concatenate([mine, other], axis=1),
            jnp.concatenate([other, mine], axis=1),
        )

    parts = project_rows(
        row_counts,
        hidden,
        swap(hidden),
        ln_gain[None, :],
        ln_bias[None, :],
        key_weight,
        value_weight,
    )
    state = attend(suffix_q, [], suffix=(suffix_k, suffix_v))

    moving = step(parts[0])
    moving = parts[1] + ordered(moving, jnp.zeros_like(moving))
    moving = step(moving) + parts[2]
    moving = step(moving) + parts[3]
    moving = step(moving) + ordered(parts[4], jnp.zeros_like(parts[4]))
    left, right = moving[:, :cols], moving[:, cols:]
    total = jnp.where(first_core, left, right) + swap(jnp.where(first_core, right, left))
    mean = total[SPAN, :SPAN] / depth
    var = total[SPAN + 1, :SPAN] / depth - mean * mean
    rows = (total[:SPAN] - mean[:, None] * total[SPAN + 2][None, :]) * lax.rsqrt(var + epsilon)[
        :, None
    ] + total[SPAN + 3][None, :]
    rows = rows.astype(jnp.bfloat16)

    rows_far = lax.ppermute(rows, "store", far)
    pair = lax.dynamic_slice(row_counts, (store // 2 * 2,), (2,))
    shared = (pair[0] + pair[1]) // ring
    mine = jnp.pad(rows, ((0, 256), (0, 0)))
    mine = lax.dynamic_update_slice(mine, rows_far, (shared, 0))[:256]

    other = swap(mine)
    r0 = step(mine)
    x0 = swap(r0)
    r1 = step(ordered(r0, other))
    x1 = swap(r1)
    r2 = step(r1)
    x2 = swap(r2)
    r3 = step(r2)
    x3 = swap(r3)

    def up(k, half):
        arrays = ((r0, x0), (r1, x1), (r2, x2), (r3, x3))[k]
        at = half * heads if k > 0 else 0
        return ((arrays[0], at), (arrays[1], at))

    def down(k, half):
        return up(k, half)[::-1]

    state = attend(
        suffix_q,
        [
            ((mine, 0), (other, 0), (other, 0), (mine, 0)),
            up(0, 0) + up(1, 1),
            down(1, 0) + down(0, 1),
        ],
        state=state,
    )
    state = attend(suffix_q, [up(1, 0) + up(2, 1), down(2, 0) + down(1, 1)], state=state)
    return attend(
        suffix_q,
        [up(2, 0) + up(3, 1), down(3, 0) + down(2, 1), up(3, 0) + down(3, 1)],
        state=state,
        lengths=suffix_lengths,
    )


def solution(mesh):
    in_specs = (
        P("store", "req"),
        P(),
        P("req"),
        P("req"),
        P("req", "tp"),
        P("req", "tp"),
        P(("store", "req"), None, "tp"),
        P(("store", "req"), None, "tp"),
        P(("store", "req"), None, "tp"),
        P(("store", "req")),
    )
    out_specs = P(("store", "req"), None, "tp")
    return jax.shard_map(
        per_device, mesh=mesh, in_specs=in_specs, out_specs=out_specs, check_vma=False
    )
```

time: 302 us -> 189 us (0.63)
  waiting for transfers between devices: 173 us -> 83.7 us
  Pallas kernels: 0 us -> 48.5 us
  starting transfers between devices: 0.22 us -> 42.6 us
  matrix products: 29.7 us -> 0 us
  other arithmetic: 29.9 us -> 2.69 us
  local copies, waits for them, and re-layouts: 36.3 us -> 9.99 us
  blocking collectives: 17.5 us -> 0 us
  between operations: 13.6 us -> 1.53 us
    all_gather x1 -> x0, waiting for transfers between devices: 107 us -> none  [per_device(): lax.all_gather(key_values, ('store', 'req'), axis=0, tiled=True)]
    ppermute x0 -> x16, waiting for transfers between devices: none -> 83.7 us  [the longest x8 72.6 us: step(): return lax.ppermute(array, ('store', 'req'), around)]
    reduce_scatter x1 -> x0, waiting for transfers between devices: 66.9 us -> none  [per_device(): lax.psum_scatter(jnp.concatenate([key_part, value_part], axis=1), 'req',...]
    pallas_call x0 -> x5, Pallas kernels: none -> 48.5 us  [the longest x4 41.1 us: attend(): pl.pallas_call(functools.partial(attention_kernel, suffix is not None, le...]
    ppermute x0 -> x16, starting transfers between devices: none -> 42.6 us  [the longest x7 21.1 us: swap(): return lax.ppermute(array, 'store', across)]
    dot_general x20 -> x0, matrix products: 29.7 us -> none  [the longest x8 12.3 us: one_block(): jnp.einsum('qhk,khd->qhd', weights, value_block, preferred_element_type=j...]
    psum x1 -> x0, blocking collectives: 17.5 us -> none  [per_device(): lax.psum((jnp.sum(widened, axis=1), jnp.sum(widened * widened, axis=1)),...]
    reduce_sum x18 -> x0, other arithmetic: 14.2 us -> none  [the longest x8 9.4 us: one_block(): totals = totals * factor + jnp.sum(weights, axis=-1, dtype=jnp.float32)]
  transfers between devices with their start and end apart: 2 -> 16, of which waited for: 2 -> 12; matrix products, arithmetic and copies ran while one was open for 4% -> 1% of each run, Pallas kernels for 0% -> 15%
where the time goes in v1:
time: 189 us
  waiting for transfers between devices  83.7 us (44%)
  Pallas kernels  48.5 us (26%)
  starting transfers between devices  42.6 us (23%)
  local copies, waits for them, and re-layouts  9.99 us (5%)
  other arithmetic  2.69 us (1%)
    ppermute x8, waiting for transfers between devices, step(): return lax.ppermute(array, ('store', 'req'), around)  72.6 us
    pallas_call x4, Pallas kernels, attend(): pl.pallas_call(functools.partial(attention_kernel, suffix is not None, le...  41.1 us
    ppermute x7, starting transfers between devices, swap(): return lax.ppermute(array, 'store', across)  21.1 us
    ppermute x8, starting transfers between devices, step(): return lax.ppermute(array, ('store', 'req'), around)  19 us
    pallas_call x1, Pallas kernels, project_rows(): pl.pallas_call(projection_kernel, out_shape=[jax.ShapeDtypeStruct((SPAN +...  7.46 us
    unnamed x20, local copies, waits for them, and re-layouts  6.13 us
    ppermute x7, waiting for transfers between devices, swap(): return lax.ppermute(array, 'store', across)  5.87 us
    ppermute x1, waiting for transfers between devices, per_device(): rows_far = lax.ppermute(rows, 'store', far)  5.3 us
  transfers between devices with their start and end apart: 16, of which 12 were waited for; matrix products, arithmetic and copies ran while one was open for 1% of the time, Pallas kernels for 15%

profile of v1, /device:TPU:1, one launch (start us, length us, event | category | flops | bytes accessed | tf_op | source)
XLA Modules:
  0.0 189.0 jit_solution(17884126436552054338)
XLA Ops:
  0.0 3.2 %collective-permute-start = (bf16[1024,1152]{1,0:T(8,128)(2,1)}, bf16[1024,1152]{1,0:T(8,128)(2,1)S(1)}, u32[]{:S(2)}, u32[]{:S(2)}) collective-permute-start(bf16[1024,1152]{1,0:T(8,128)(2,1)} %hidden.1), channel_id=1, source_target_pairs={{0,64},{64,0},{128,192},{192,128},{1,65},{65,1},{129,193},{193,129... | collective-permute-start | bytes 7077896 | tf_op jit(solution)/shard_map/ppermute | solution.py:285
  3.2 0.7 broadcast_in_dim.8.gain
  3.9 0.7 broadcast_in_dim.9.bias
  4.6 3.0 %collective-permute-done.hidden_other = bf16[1024,1152]{1,0:T(8,128)(2,1)S(1)} collective-permute-done((bf16[1024,1152]{1,0:T(8,128)(2,1)}, bf16[1024,1152]{1,0:T(8,128)(2,1)S(1)}, u32[]{:S(2)}, u32[]{:S(2)}) %collective-permute-start) | collective-permute-done | bytes 2359328 | tf_op jit(solution)/shard_map/ppermute | solution.py:285
  7.6 1.7 copy-done.5
  9.3 1.4 copy-done.6
  10.7 1.4 copy-done.7
  12.0 0.7 copy-done.8
  12.7 7.5 %shard_map.101 = (f32[232,640]{1,0:T(8,128)}, f32[232,1280]{1,0:T(8,128)S(1)}, f32[232,1280]{1,0:T(8,128)S(1)}, f32[232,1280]{1,0:T(8,128)S(1)}, f32[232,640]{1,0:T(8,128)S(1)}) custom-call(s32[4]{0:T(128)S(1)} %copy-done.8, bf16[1024,1152]{1,0:T(8,128)(2,1)S(1)} %copy-done.5, bf16[1024,1152]{1,0:T(8,128)(2,1)S(1)} %collective-permute-done.hidden_other, ...), custom_call_target="tpu_custom_call" | custom-call | flops 2642411520 | bytes 12582912 | tf_op jit(solution)/shard_map/pallas_call | solution.py:125
  20.1 0.0 copy-start.1
  20.2 1.0 copy-done.1
  21.2 3.9 %collective-permute-start.1 = (f32[232,640]{1,0:T(8,128)}, f32[232,640]{1,0:T(8,128)}, u32[]{:S(2)}, u32[]{:S(2)}) collective-permute-start(f32[232,640]{1,0:T(8,128)} %get-tuple-element.11), channel_id=1, source_target_pairs={{0,8},{8,16},{16,24},{24,32},{32,40},{40,48},{48,56},{56,0},{64,12... | collective-permute-start | bytes 1781768 | tf_op jit(solution)/shard_map/ppermute | solution.py:282
  25.1 7.2 %collective-permute-done.1 = f32[232,640]{1,0:T(8,128)} collective-permute-done((f32[232,640]{1,0:T(8,128)}, f32[232,640]{1,0:T(8,128)}, u32[]{:S(2)}, u32[]{:S(2)}) %collective-permute-start.1) | collective-permute-done | bytes 593952 | tf_op jit(solution)/shard_map/ppermute | solution.py:282
  32.2 1.7 select_add_fusion.1
  34.0 3.2 %collective-permute-start.2 = (f32[232,1280]{1,0:T(8,128)S(1)}, f32[232,1280]{1,0:T(8,128)S(1)}, u32[]{:S(2)}, u32[]{:S(2)}) collective-permute-start(f32[232,1280]{1,0:T(8,128)S(1)} %select_add_fusion.1), channel_id=1, source_target_pairs={{0,8},{8,16},{16,24},{24,32},{32,40},{40,48},{48,56},{56,0},{64,12... | collective-permute-start | bytes 3563528 | tf_op jit(solution)/shard_map/ppermute | solution.py:282
  37.2 13.2 %collective-permute-done.2 = f32[232,1280]{1,0:T(8,128)S(1)} collective-permute-done((f32[232,1280]{1,0:T(8,128)S(1)}, f32[232,1280]{1,0:T(8,128)S(1)}, u32[]{:S(2)}, u32[]{:S(2)}) %collective-permute-start.2) | collective-permute-done | bytes 1187872 | tf_op jit(solution)/shard_map/ppermute | solution.py:282
  50.4 0.2 add.65
  50.6 3.2 %collective-permute-start.3 = (f32[232,1280]{1,0:T(8,128)S(1)}, f32[232,1280]{1,0:T(8,128)S(1)}, u32[]{:S(2)}, u32[]{:S(2)}) collective-permute-start(f32[232,1280]{1,0:T(8,128)S(1)} %add.65), channel_id=1, source_target_pairs={{0,8},{8,16},{16,24},{24,32},{32,40},{40,48},{48,56},{56,0},{64,12... | collective-permute-start | bytes 3563528 | tf_op jit(solution)/shard_map/ppermute | solution.py:282
  53.7 13.2 %collective-permute-done.3 = f32[232,1280]{1,0:T(8,128)S(1)} collective-permute-done((f32[232,1280]{1,0:T(8,128)S(1)}, f32[232,1280]{1,0:T(8,128)S(1)}, u32[]{:S(2)}, u32[]{:S(2)}) %collective-permute-start.3) | collective-permute-done | bytes 1187872 | tf_op jit(solution)/shard_map/ppermute | solution.py:282
  67.0 0.2 add.66
  67.1 3.2 %collective-permute-start.4 = (f32[232,1280]{1,0:T(8,128)S(1)}, f32[232,1280]{1,0:T(8,128)S(1)}, u32[]{:S(2)}, u32[]{:S(2)}) collective-permute-start(f32[232,1280]{1,0:T(8,128)S(1)} %add.66), channel_id=1, source_target_pairs={{0,8},{8,16},{16,24},{24,32},{32,40},{40,48},{48,56},{56,0},{64,12... | collective-permute-start | bytes 3563528 | tf_op jit(solution)/shard_map/ppermute | solution.py:282
  70.3 13.2 %collective-permute-done.4 = f32[232,1280]{1,0:T(8,128)S(1)} collective-permute-done((f32[232,1280]{1,0:T(8,128)S(1)}, f32[232,1280]{1,0:T(8,128)S(1)}, u32[]{:S(2)}, u32[]{:S(2)}) %collective-permute-start.4) | collective-permute-done | bytes 1187872 | tf_op jit(solution)/shard_map/ppermute | solution.py:282
  83.6 0.2 select_add_fusion
  83.8 0.1 slice_select_fusion
  83.8 0.0 copy-start.9
  83.8 5.2 %collective-permute-start.5 = (f32[232,640]{1,0:T(8,128)S(1)}, f32[232,640]{1,0:T(8,128)S(1)}, u32[]{:S(2)}, u32[]{:S(2)}) collective-permute-start(f32[232,640]{1,0:T(8,128)S(1)} %slice_select_fusion), channel_id=1, source_target_pairs={{0,64},{64,0},{128,192},{192,128},{1,65},{65,1},{129,193},{193,129... | collective-permute-start | bytes 1781768 | tf_op jit(solution)/shard_map/ppermute | solution.py:285
  89.0 1.6 collective-permute-done.5
  90.7 0.1 select_add_fusion.2
  90.8 0.2 fusion.2
  91.0 2.5 %collective-permute-start.6 = (bf16[224,640]{1,0:T(8,128)(2,1)S(1)}, bf16[224,640]{1,0:T(8,128)(2,1)S(1)}, u32[]{:S(2)}, u32[]{:S(2)}) collective-permute-start(bf16[224,640]{1,0:T(8,128)(2,1)S(1)} %fusion.2), channel_id=1, source_target_pairs={{0,128},{64,192},{128,0},{192,64},{1,129},{65,193},{129,1},{193,65... | collective-permute-start | bytes 860168 | tf_op jit(solution)/shard_map/ppermute | solution.py:319
  93.5 0.0 copy-done.9
  93.5 0.1 dynamic_slice.3
  93.5 0.6 fusion.3
  95.4 0.1 pad.8
  95.5 0.0 copy-start
  95.5 0.0 copy-start.2
  95.5 0.0 copy-start.3
  95.5 5.3 %collective-permute-done.6 = bf16[224,640]{1,0:T(8,128)(2,1)S(1)} collective-permute-done((bf16[224,640]{1,0:T(8,128)(2,1)S(1)}, bf16[224,640]{1,0:T(8,128)(2,1)S(1)}, u32[]{:S(2)}, u32[]{:S(2)}) %collective-permute-start.6) | collective-permute-done | bytes 286752 | tf_op jit(solution)/shard_map/ppermute | solution.py:319
  100.8 1.7 dynamic_update_slice.3
  102.6 1.3 collective-permute-start.7
  103.8 0.0 collective-permute-start.8
  103.8 1.3 collective-permute-done.7.refs_3_.refs_4_
  105.1 5.0 %collective-permute-done.8.refs_6_.refs_13_ = bf16[256,640]{1,0:T(8,128)(2,1)S(1)} collective-permute-done((bf16[256,640]{1,0:T(8,128)(2,1)S(1)}, bf16[256,640]{1,0:T(8,128)(2,1)S(1)}, u32[]{:S(2)}, u32[]{:S(2)}) %collective-permute-start.8) | collective-permute-done | bytes 327712 | tf_op jit(solution)/shard_map/ppermute | solution.py:282
  110.1 0.2 maximum_select_fusion
  110.2 1.0 collective-permute-start.10
  111.2 8.8 %collective-permute-done.10.refs_8_.refs_11_.refs_2_.refs_9_ = bf16[256,1280]{1,0:T(8,128)(2,1)S(1)} collective-permute-done((bf16[256,1280]{1,0:T(8,128)(2,1)S(1)}, bf16[256,1280]{1,0:T(8,128)(2,1)S(1)}, u32[]{:S(2)}, u32[]{:S(2)}) %collective-permute-start.10) | collective-permute-done | bytes 655392 | tf_op jit(solution)/shard_map/ppermute | solution.py:282
  120.0 1.8 collective-permute-start.12
  121.9 7.9 %collective-permute-done.12.refs_4_.refs_7_.refs_3_.refs_10_ = bf16[256,1280]{1,0:T(8,128)(2,1)S(1)} collective-permute-done((bf16[256,1280]{1,0:T(8,128)(2,1)S(1)}, bf16[256,1280]{1,0:T(8,128)(2,1)S(1)}, u32[]{:S(2)}, u32[]{:S(2)}) %collective-permute-start.12) | collective-permute-done | bytes 655392 | tf_op jit(solution)/shard_map/ppermute | solution.py:282
  129.8 2.7 %collective-permute-start.14 = (bf16[256,1280]{1,0:T(8,128)(2,1)S(1)}, bf16[256,1280]{1,0:T(8,128)(2,1)S(1)}, u32[]{:S(2)}, u32[]{:S(2)}) collective-permute-start(bf16[256,1280]{1,0:T(8,128)(2,1)S(1)} %collective-permute-done.12.refs_4_.refs_7_.refs_3_.refs_10_), channel_id=1, source_target_pairs={{0,8},{8,16},{16,24},{24,32},{32,40},{40,48},{48,56},{56,0},{64,12... | collective-permute-start | bytes 1966088 | tf_op jit(solution)/shard_map/ppermute | solution.py:282
  132.5 3.5 %collective-permute-start.11 = (bf16[256,1280]{1,0:T(8,128)(2,1)S(1)}, bf16[256,1280]{1,0:T(8,128)(2,1)S(1)}, u32[]{:S(2)}, u32[]{:S(2)}) collective-permute-start(bf16[256,1280]{1,0:T(8,128)(2,1)S(1)} %collective-permute-done.10.refs_8_.refs_11_.refs_2_.refs_9_), channel_id=1, source_target_pairs={{0,64},{64,0},{128,192},{192,128},{1,65},{65,1},{129,193},{193,129... | collective-permute-start | bytes 1966088 | tf_op jit(solution)/shard_map/ppermute | solution.py:285
  136.1 0.0 collective-permute-start.13
  136.1 4.0 %collective-permute-done.14.refs_5_.refs_8_.refs_11_.refs_14_ = bf16[256,1280]{1,0:T(8,128)(2,1)S(1)} collective-permute-done((bf16[256,1280]{1,0:T(8,128)(2,1)S(1)}, bf16[256,1280]{1,0:T(8,128)(2,1)S(1)}, u32[]{:S(2)}, u32[]{:S(2)}) %collective-permute-start.14) | collective-permute-done | bytes 655392 | tf_op jit(solution)/shard_map/ppermute | solution.py:282
  140.0 7.8 %collective-permute-start.15 = (bf16[256,1280]{1,0:T(8,128)(2,1)S(1)}, bf16[256,1280]{1,0:T(8,128)(2,1)S(1)}, u32[]{:S(2)}, u32[]{:S(2)}) collective-permute-start(bf16[256,1280]{1,0:T(8,128)(2,1)S(1)} %collective-permute-done.14.refs_5_.refs_8_.refs_11_.refs_14_), channel_id=1, source_target_pairs={{0,64},{64,0},{128,192},{192,128},{1,65},{65,1},{129,193},{193,129... | collective-permute-start | bytes 1966088 | tf_op jit(solution)/shard_map/ppermute | solution.py:285
  147.8 0.0 collective-permute-start.9
  147.8 0.0 copy-done
  147.9 6.0 %shard_map.100.refs_1_ = f32[5,512,256]{2,1,0:T(8,128)S(1)} custom-call(bf16[4,128,640]{2,1,0:T(8,128)(2,1)S(1)} %copy-done, bf16[4,128,640]{2,1,0:T(8,128)(2,1)S(1)} %copy-done.2, bf16[4,128,640]{2,1,0:T(8,128)(2,1)S(1)} %copy-done.3), custom_call_target="tpu_custom_call" | custom-call | flops 167772160 | bytes 6291456 | tf_op jit(solution)/shard_map/pallas_call | solution.py:237
  153.9 0.0 collective-permute-done.9.refs_7_.refs_12_
  153.9 0.0 collective-permute-done.11.refs_9_.refs_10_.refs_3_.refs_8_
  153.9 12.0 %shard_map.102.refs_1_ = f32[5,512,256]{2,1,0:T(8,128)S(1)} custom-call(bf16[4,128,640]{2,1,0:T(8,128)(2,1)S(1)} %copy-done, f32[5,512,256]{2,1,0:T(8,128)S(1)} %shard_map.100.refs_1_, bf16[256,640]{1,0:T(8,128)(2,1)S(1)} %slice.47.refs_2_.refs_5_, bf16[256,640]{1,0:T(8,128)(2,1)S(1)} %collective-permute-done.7.refs_3_.refs_4_, ...), custom_call_target="tpu_custom_call" | custom-call | flops 1006632960 | bytes 6291456 | tf_op jit(solution)/shard_map/pallas_call | solution.py:237
  165.9 0.0 copy-start.4
  165.9 0.0 collective-permute-done.13.refs_5_.refs_6_.refs_4_.refs_9_
  165.9 9.8 %shard_map.103.refs_2_ = f32[5,512,256]{2,1,0:T(8,128)S(1)} custom-call(bf16[4,128,640]{2,1,0:T(8,128)(2,1)S(1)} %copy-done, f32[5,512,256]{2,1,0:T(8,128)S(1)} %shard_map.102.refs_1_, bf16[256,1280]{1,0:T(8,128)(2,1)S(1)} %collective-permute-done.10.refs_8_.refs_11_.refs_2_.refs_9_, ...), custom_call_target="tpu_custom_call" | custom-call | flops 671088640 | bytes 6291456 | tf_op jit(solution)/shard_map/pallas_call | solution.py:237
  175.8 0.0 collective-permute-done.15.refs_6_.refs_7_.refs_12_.refs_13_
  175.8 13.2 %shard_map.104 = bf16[4,128,640]{2,1,0:T(8,128)(2,1)} custom-call(s32[4]{0:T(128)S(1)} %copy-done.4, bf16[4,128,640]{2,1,0:T(8,128)(2,1)S(1)} %copy-done, f32[5,512,256]{2,1,0:T(8,128)S(1)} %shard_map.103.refs_2_, bf16[256,1280]{1,0:T(8,128)(2,1)S(1)} %collective-permute-done.12.refs_4_.refs_7_.refs_3_.refs_10_, ...), custom_call_target="tpu_custom_call" | custom-call | flops 1006632960 | bytes 6291456 | tf_op jit(solution)/shard_map/pallas_call | solution.py:237
  (11 shorter events, 0.1 us)
Async XLA Ops:
  0.0 7.6 %collective-permute-start = (bf16[1024,1152]{1,0:T(8,128)(2,1)}, bf16[1024,1152]{1,0:T(8,128)(2,1)S(1)}, u32[]{:S(2)}, u32[]{:S(2)}) collective-permute-start(bf16[1024,1152]{1,0:T(8,128)(2,1)} %hidden.1), channel_id=1, source_target_pairs={{0,64},{64,0},{128,192},{192,128},{1,65},{65,1},{129,193},{193,129... | collective-permute-start | bytes 7077896 | tf_op jit(solution)/shard_map/ppermute | solution.py:285
  7.6 1.7 copy-start.5
  9.3 1.4 copy-start.6
  10.7 1.4 copy-start.7
  12.0 0.7 copy-start.8
  20.1 1.0 copy-start.1
  21.2 11.0 %collective-permute-start.1 = (f32[232,640]{1,0:T(8,128)}, f32[232,640]{1,0:T(8,128)}, u32[]{:S(2)}, u32[]{:S(2)}) collective-permute-start(f32[232,640]{1,0:T(8,128)} %get-tuple-element.11), channel_id=1, source_target_pairs={{0,8},{8,16},{16,24},{24,32},{32,40},{40,48},{48,56},{56,0},{64,12... | collective-permute-start | bytes 1781768 | tf_op jit(solution)/shard_map/ppermute | solution.py:282
  34.0 16.4 %collective-permute-start.2 = (f32[232,1280]{1,0:T(8,128)S(1)}, f32[232,1280]{1,0:T(8,128)S(1)}, u32[]{:S(2)}, u32[]{:S(2)}) collective-permute-start(f32[232,1280]{1,0:T(8,128)S(1)} %select_add_fusion.1), channel_id=1, source_target_pairs={{0,8},{8,16},{16,24},{24,32},{32,40},{40,48},{48,56},{56,0},{64,12... | collective-permute-start | bytes 3563528 | tf_op jit(solution)/shard_map/ppermute | solution.py:282
  50.6 16.4 %collective-permute-start.3 = (f32[232,1280]{1,0:T(8,128)S(1)}, f32[232,1280]{1,0:T(8,128)S(1)}, u32[]{:S(2)}, u32[]{:S(2)}) collective-permute-start(f32[232,1280]{1,0:T(8,128)S(1)} %add.65), channel_id=1, source_target_pairs={{0,8},{8,16},{16,24},{24,32},{32,40},{40,48},{48,56},{56,0},{64,12... | collective-permute-start | bytes 3563528 | tf_op jit(solution)/shard_map/ppermute | solution.py:282
  67.1 16.4 %collective-permute-start.4 = (f32[232,1280]{1,0:T(8,128)S(1)}, f32[232,1280]{1,0:T(8,128)S(1)}, u32[]{:S(2)}, u32[]{:S(2)}) collective-permute-start(f32[232,1280]{1,0:T(8,128)S(1)} %add.66), channel_id=1, source_target_pairs={{0,8},{8,16},{16,24},{24,32},{32,40},{40,48},{48,56},{56,0},{64,12... | collective-permute-start | bytes 3563528 | tf_op jit(solution)/shard_map/ppermute | solution.py:282
  83.8 9.6 %copy-start.9 = (s32[4]{0:T(128)S(1)}, s32[4]{0:T(128)}, u32[]{:S(2)}) copy-start(s32[4]{0:T(128)} %counts.1) | copy-start | bytes 52
  83.8 6.8 %collective-permute-start.5 = (f32[232,640]{1,0:T(8,128)S(1)}, f32[232,640]{1,0:T(8,128)S(1)}, u32[]{:S(2)}, u32[]{:S(2)}) collective-permute-start(f32[232,640]{1,0:T(8,128)S(1)} %slice_select_fusion), channel_id=1, source_target_pairs={{0,64},{64,0},{128,192},{192,128},{1,65},{65,1},{129,193},{193,129... | collective-permute-start | bytes 1781768 | tf_op jit(solution)/shard_map/ppermute | solution.py:285
  91.0 9.8 %collective-permute-start.6 = (bf16[224,640]{1,0:T(8,128)(2,1)S(1)}, bf16[224,640]{1,0:T(8,128)(2,1)S(1)}, u32[]{:S(2)}, u32[]{:S(2)}) collective-permute-start(bf16[224,640]{1,0:T(8,128)(2,1)S(1)} %fusion.2), channel_id=1, source_target_pairs={{0,128},{64,192},{128,0},{192,64},{1,129},{65,193},{129,1},{193,65... | collective-permute-start | bytes 860168 | tf_op jit(solution)/shard_map/ppermute | solution.py:319
  95.5 52.4 %copy-start = (bf16[4,128,640]{2,1,0:T(8,128)(2,1)S(1)}, bf16[4,128,640]{2,1,0:T(8,128)(2,1)}, u32[]{:S(2)}) copy-start(bf16[4,128,640]{2,1,0:T(8,128)(2,1)} %refs_1_.3) | copy-start | bytes 1966084
  95.5 52.4 %copy-start.2 = (bf16[4,128,640]{2,1,0:T(8,128)(2,1)S(1)}, bf16[4,128,640]{2,1,0:T(8,128)(2,1)}, u32[]{:S(2)}) copy-start(bf16[4,128,640]{2,1,0:T(8,128)(2,1)} %refs_1_.2) | copy-start | bytes 1966084
  95.5 52.4 %copy-start.3 = (bf16[4,128,640]{2,1,0:T(8,128)(2,1)S(1)}, bf16[4,128,640]{2,1,0:T(8,128)(2,1)}, u32[]{:S(2)}) copy-start(bf16[4,128,640]{2,1,0:T(8,128)(2,1)} %refs_2_.1) | copy-start | bytes 1966084
  102.6 2.5 %collective-permute-start.7 = (bf16[256,640]{1,0:T(8,128)(2,1)S(1)}, bf16[256,640]{1,0:T(8,128)(2,1)S(1)}, u32[]{:S(2)}, u32[]{:S(2)}) collective-permute-start(bf16[256,640]{1,0:T(8,128)(2,1)S(1)} %slice.47.refs_2_.refs_5_), channel_id=1, source_target_pairs={{0,64},{64,0},{128,192},{192,128},{1,65},{65,1},{129,193},{193,129... | collective-permute-start | bytes 983048 | tf_op jit(solution)/shard_map/ppermute | solution.py:285
  103.8 6.2 %collective-permute-start.8 = (bf16[256,640]{1,0:T(8,128)(2,1)S(1)}, bf16[256,640]{1,0:T(8,128)(2,1)S(1)}, u32[]{:S(2)}, u32[]{:S(2)}) collective-permute-start(bf16[256,640]{1,0:T(8,128)(2,1)S(1)} %slice.47.refs_2_.refs_5_), channel_id=1, source_target_pairs={{0,8},{8,16},{16,24},{24,32},{32,40},{40,48},{48,56},{56,0},{64,12... | collective-permute-start | bytes 983048 | tf_op jit(solution)/shard_map/ppermute | solution.py:282
  110.2 9.8 %collective-permute-start.10 = (bf16[256,1280]{1,0:T(8,128)(2,1)S(1)}, bf16[256,1280]{1,0:T(8,128)(2,1)S(1)}, u32[]{:S(2)}, u32[]{:S(2)}) collective-permute-start(bf16[256,1280]{1,0:T(8,128)(2,1)S(1)} %maximum_select_fusion), channel_id=1, source_target_pairs={{0,8},{8,16},{16,24},{24,32},{32,40},{40,48},{48,56},{56,0},{64,12... | collective-permute-start | bytes 1966088 | tf_op jit(solution)/shard_map/ppermute | solution.py:282
  120.0 9.7 %collective-permute-start.12 = (bf16[256,1280]{1,0:T(8,128)(2,1)S(1)}, bf16[256,1280]{1,0:T(8,128)(2,1)S(1)}, u32[]{:S(2)}, u32[]{:S(2)}) collective-permute-start(bf16[256,1280]{1,0:T(8,128)(2,1)S(1)} %collective-permute-done.10.refs_8_.refs_11_.refs_2_.refs_9_), channel_id=1, source_target_pairs={{0,8},{8,16},{16,24},{24,32},{32,40},{40,48},{48,56},{56,0},{64,12... | collective-permute-start | bytes 1966088 | tf_op jit(solution)/shard_map/ppermute | solution.py:282
  129.8 10.3 %collective-permute-start.14 = (bf16[256,1280]{1,0:T(8,128)(2,1)S(1)}, bf16[256,1280]{1,0:T(8,128)(2,1)S(1)}, u32[]{:S(2)}, u32[]{:S(2)}) collective-permute-start(bf16[256,1280]{1,0:T(8,128)(2,1)S(1)} %collective-permute-done.12.refs_4_.refs_7_.refs_3_.refs_10_), channel_id=1, source_target_pairs={{0,8},{8,16},{16,24},{24,32},{32,40},{40,48},{48,56},{56,0},{64,12... | collective-permute-start | bytes 1966088 | tf_op jit(solution)/shard_map/ppermute | solution.py:282
  132.5 21.4 %collective-permute-start.11 = (bf16[256,1280]{1,0:T(8,128)(2,1)S(1)}, bf16[256,1280]{1,0:T(8,128)(2,1)S(1)}, u32[]{:S(2)}, u32[]{:S(2)}) collective-permute-start(bf16[256,1280]{1,0:T(8,128)(2,1)S(1)} %collective-permute-done.10.refs_8_.refs_11_.refs_2_.refs_9_), channel_id=1, source_target_pairs={{0,64},{64,0},{128,192},{192,128},{1,65},{65,1},{129,193},{193,129... | collective-permute-start | bytes 1966088 | tf_op jit(solution)/shard_map/ppermute | solution.py:285
  136.1 29.9 %collective-permute-start.13 = (bf16[256,1280]{1,0:T(8,128)(2,1)S(1)}, bf16[256,1280]{1,0:T(8,128)(2,1)S(1)}, u32[]{:S(2)}, u32[]{:S(2)}) collective-permute-start(bf16[256,1280]{1,0:T(8,128)(2,1)S(1)} %collective-permute-done.12.refs_4_.refs_7_.refs_3_.refs_10_), channel_id=1, source_target_pairs={{0,64},{64,0},{128,192},{192,128},{1,65},{65,1},{129,193},{193,129... | collective-permute-start | bytes 1966088 | tf_op jit(solution)/shard_map/ppermute | solution.py:285
  140.0 35.7 %collective-permute-start.15 = (bf16[256,1280]{1,0:T(8,128)(2,1)S(1)}, bf16[256,1280]{1,0:T(8,128)(2,1)S(1)}, u32[]{:S(2)}, u32[]{:S(2)}) collective-permute-start(bf16[256,1280]{1,0:T(8,128)(2,1)S(1)} %collective-permute-done.14.refs_5_.refs_8_.refs_11_.refs_14_), channel_id=1, source_target_pairs={{0,64},{64,0},{128,192},{192,128},{1,65},{65,1},{129,193},{193,129... | collective-permute-start | bytes 1966088 | tf_op jit(solution)/shard_map/ppermute | solution.py:285
  147.8 6.1 %collective-permute-start.9 = (bf16[256,640]{1,0:T(8,128)(2,1)S(1)}, bf16[256,640]{1,0:T(8,128)(2,1)S(1)}, u32[]{:S(2)}, u32[]{:S(2)}) collective-permute-start(bf16[256,640]{1,0:T(8,128)(2,1)S(1)} %collective-permute-done.8.refs_6_.refs_13_), channel_id=1, source_target_pairs={{0,64},{64,0},{128,192},{192,128},{1,65},{65,1},{129,193},{193,129... | collective-permute-start | bytes 983048 | tf_op jit(solution)/shard_map/ppermute | solution.py:285
  165.9 9.9 %copy-start.4 = (s32[4]{0:T(128)S(1)}, s32[4]{0:T(128)}, u32[]{:S(2)}) copy-start(s32[4]{0:T(128)} %refs_0_.7) | copy-start | bytes 52

commit v2 on v1

v2 whole, which is shorter than its diff:
```python
import functools
import math

import jax
import jax.numpy as jnp
from jax import lax
from jax.experimental import pallas as pl
from jax.experimental.pallas import tpu as pltpu
from jax.sharding import PartitionSpec as P

HD = 128
UNIT = 128
MOST_UNITS = 14
SPAN = 16 * MOST_UNITS
TAIL = 8
BLOCK = 256
epsilon = 1e-05
RATE = math.log2(math.e) / math.sqrt(HD)
MIB = 1 << 20


def split(x, count=3):
    pieces = []
    for _ in range(count):
        piece = x.astype(jnp.bfloat16)
        pieces.append(piece)
        x = x - piece.astype(jnp.float32)
    return pieces


def projection_kernel(
    counts, hidden, hidden_other, gain, bias, key_weight, value_weight, *rest
):
    first, second, (rows_in, weights, row_semaphores, weight_semaphores) = (
        rest[:5],
        rest[5:8],
        rest[8:],
    )
    store = lax.axis_index("store")
    me = lax.axis_index("req")
    core = lax.rem(store, 2)
    first_count = counts[store - core]
    second_count = counts[store - core + 1]
    share = (first_count + second_count) // 8
    width = hidden.shape[1]
    cols = key_weight.shape[1]

    def weight_copies(act):
        for side, source in enumerate((key_weight, value_weight)):
            act(
                pltpu.make_async_copy(
                    source, weights.at[lax.rem(core + side, 2)], weight_semaphores.at[side]
                )
            )

    def row_copies(act):
        for side, source in enumerate((hidden, hidden_other)):
            lower = lax.rem(core + side, 2) == 0
            count = jnp.where(lower, first_count, second_count)
            base = SPAN + jnp.where(lower, 0, first_count)
            for unit in range(source.shape[0] // UNIT):

                @pl.when(unit * UNIT < count)
                def _():
                    at = pl.multiple_of(base + unit * UNIT, 32)
                    act(
                        pltpu.make_async_copy(
                            source.at[pl.ds(unit * UNIT, UNIT)],
                            rows_in.at[pl.ds(at, UNIT)],
                            row_semaphores.at[side, unit],
                        )
                    )

    weight_copies(lambda copy: copy.start())
    row_copies(lambda copy: copy.start())

    row_id = lax.broadcasted_iota(jnp.int32, (16, width), 0)
    affine = jnp.where(row_id == 2, gain[...], jnp.where(row_id == 3, bias[...], 0.0))
    pieces = split(affine)
    weight_copies(lambda copy: copy.wait())
    affine_sums = [
        sum(
            jnp.dot(piece, weights[half], preferred_element_type=jnp.float32)
            for piece in pieces
        )
        for half in range(2)
    ]
    row_copies(lambda copy: copy.wait())

    tail_row = lax.broadcasted_iota(jnp.int32, (TAIL, cols), 0)
    lane = lax.broadcasted_iota(jnp.int32, (128, 128), 1)

    for k in range(5):
        steps = 4 - k
        target = lax.rem(me + jnp.where(core == 0, steps, 8 - steps), 8)
        start = jnp.where(store < 2, SPAN + target * share, (target + 1) * share)
        wide = rows_in[pl.ds(pl.multiple_of(start, 16), SPAN), :].astype(jnp.float32)
        row_sum = jnp.sum(wide, axis=1, keepdims=True)
        row_square = jnp.sum(wide * wide, axis=1, keepdims=True)
        centre = row_sum * (1.0 / width)
        scaled = ((wide - centre) * gain[...]).astype(jnp.bfloat16)
        flipped = []
        for at in range(0, SPAN, 128):
            count = min(128, SPAN - at)
            column = jnp.where(
                lane[:count] == 0,
                row_sum[at : at + count],
                jnp.where(lane[:count] == 1, row_square[at : at + count], 0.0),
            )
            if count < 128:
                column = jnp.concatenate(
                    [column, jnp.zeros((128 - count, 128), jnp.float32)], axis=0
                )
            flipped.append(jnp.transpose(column)[:TAIL])
        flipped = jnp.concatenate(flipped, axis=1)
        parts = [first[k]] + ([second[k - 1]] if 1 <= k <= 3 else [])
        for part, half in zip(parts, range(2)):
            affine_sum = affine_sums[half]
            part[0:SPAN, :] = (
                jnp.dot(scaled, weights[half], preferred_element_type=jnp.float32)
                + centre * affine_sum[2:3]
            )
            tail = jnp.where(
                jnp.logical_or(tail_row == 2, tail_row == 3), affine_sum[0:TAIL], 0.0
            )
            part[SPAN : SPAN + TAIL, :] = tail
            part[SPAN : SPAN + TAIL, 0:256] = jnp.where(
                tail_row[:, :256] < 2, flipped, tail[:, :256]
            )


def project_rows(counts, hidden, hidden_other, gain, bias, key_weight, value_weight):
    capacity, width = hidden.shape
    cols = key_weight.shape[1]
    vmem = pl.BlockSpec(memory_space=pltpu.VMEM)
    hbm = pl.BlockSpec(memory_space=pl.ANY)
    return pl.pallas_call(
        projection_kernel,
        out_shape=[jax.ShapeDtypeStruct((SPAN + TAIL, cols), jnp.float32)] * 8,
        in_specs=[pl.BlockSpec(memory_space=pltpu.SMEM), hbm, hbm, vmem, vmem, hbm, hbm],
        out_specs=[vmem] * 8,
        scratch_shapes=[
            pltpu.VMEM((SPAN + MOST_UNITS * UNIT, width), jnp.bfloat16),
            pltpu.VMEM((2, width, cols), jnp.bfloat16),
            pltpu.SemaphoreType.DMA((2, capacity // UNIT)),
            pltpu.SemaphoreType.DMA((2,)),
        ],
        compiler_params=pltpu.CompilerParams(vmem_limit_bytes=56 * MIB),
        cost_estimate=pl.CostEstimate(
            flops=8 * SPAN * width * 2 * cols, bytes_accessed=12 * MIB, transcendentals=0
        ),
    )(counts, hidden, hidden_other, gain, bias, key_weight, value_weight)


def pack_shift(top):
    rows = top.shape[0]
    lane = lax.broadcasted_iota(jnp.int32, (rows, HD), 1)
    left = -jnp.broadcast_to(top, (rows, HD))
    packed = jnp.zeros((rows, HD), jnp.float32)
    for i, piece in enumerate(split(left)):
        packed = jnp.where(lane == i, piece.astype(jnp.float32), packed)
    return packed.astype(jnp.bfloat16)


def own_kernel(q, own_k, own_v, out, shift):
    requests, positions, _ = q.shape
    row = lax.broadcasted_iota(jnp.int32, (positions, positions), 0)
    column = lax.broadcasted_iota(jnp.int32, (positions, positions), 1)
    for r in range(requests):
        at = r * positions
        scores = lax.dot_general(
            q[r], own_k[r], (((1,), (1,)), ((), ())), preferred_element_type=jnp.float32
        )
        scores = jnp.where(column <= row, scores, -jnp.inf)
        top = jnp.max(scores, axis=1, keepdims=True)
        weights = jnp.exp2((scores - top) * RATE).astype(jnp.bfloat16)
        both = jnp.concatenate([own_v[r], jnp.ones((positions, HD), jnp.bfloat16)], axis=1)
        out[0, at : at + positions, :] = jnp.dot(
            weights, both, preferred_element_type=jnp.float32
        )
        shift[0, at : at + positions, :] = pack_shift(top)


def stage_kernel(end, pair_count, *refs):
    refs = list(refs)
    lengths = refs.pop(0) if end else None
    q, state, shift = refs[:3]
    blocks = refs[3 : 3 + 4 * pair_count]
    outs = refs[3 + 4 * pair_count :]
    requests, positions, _ = q.shape
    rows = requests * positions
    first_core = lax.rem(lax.axis_index("store"), 2) == 0

    def pick(i):
        return jnp.where(first_core, blocks[2 * i][...], blocks[2 * i + 1][...])

    keys = jnp.concatenate([pick(2 * i) for i in range(pair_count)], axis=0)
    values = jnp.concatenate([pick(2 * i + 1) for i in range(pair_count)], axis=0)
    ones = jnp.ones(keys.shape, jnp.bfloat16)
    keys = jnp.concatenate([keys, ones], axis=1)
    values = jnp.concatenate([values, ones], axis=1)

    def shifted_scores():
        queries = jnp.concatenate([q[...].reshape(rows, HD), shift[0]], axis=1)
        return lax.dot_general(
            queries, keys, (((1,), (1,)), ((), ())), preferred_element_type=jnp.float32
        )

    def weigh(scores):
        weights = jnp.exp2(scores * RATE).astype(jnp.bfloat16)
        return jnp.dot(weights, values, preferred_element_type=jnp.float32)

    def emit(total, packed):
        if end:
            result = total[:, :HD] / total[:, HD:]
            place = lax.broadcasted_iota(jnp.int32, (positions, HD), 0)
            for r in range(requests):
                part = result[r * positions : (r + 1) * positions]
                outs[0][r] = jnp.where(place < lengths[r], part, 0.0).astype(jnp.bfloat16)
        else:
            outs[0][0] = total
            outs[1][0] = packed

    total = state[0] + weigh(shifted_scores())
    emit(total, shift[0])
    largest = jnp.max(jnp.max(total[:, HD:].reshape(rows // 8, 8, HD), axis=0))

    @pl.when(jnp.logical_not(largest < 1e30))
    def _():
        scores = shifted_scores()
        old = -jnp.sum(shift[0].astype(jnp.float32), axis=1, keepdims=True)
        new = old + jnp.maximum(jnp.max(scores, axis=1, keepdims=True), 0.0)
        moved = new - old
        emit(state[0] * jnp.exp2(-moved * RATE) + weigh(scores - moved), pack_shift(new))


def attend_own(q, k, v):
    requests, positions, width = q.shape
    rows = requests * positions
    heads = width // HD
    whole = pl.BlockSpec((requests, positions, HD), lambda h: (0, 0, h))
    return pl.pallas_call(
        own_kernel,
        grid=(heads,),
        out_shape=[
            jax.ShapeDtypeStruct((heads, rows, 2 * HD), jnp.float32),
            jax.ShapeDtypeStruct((heads, rows, HD), jnp.bfloat16),
        ],
        in_specs=[whole] * 3,
        out_specs=[
            pl.BlockSpec((1, rows, 2 * HD), lambda h: (h, 0, 0)),
            pl.BlockSpec((1, rows, HD), lambda h: (h, 0, 0)),
        ],
        compiler_params=pltpu.CompilerParams(vmem_limit_bytes=40 * MIB),
        cost_estimate=pl.CostEstimate(
            flops=4 * rows * positions * width,
            bytes_accessed=6 * MIB,
            transcendentals=rows * positions * heads,
        ),
    )(q, k, v)


def attend(q, state, pairs, lengths=None):
    requests, positions, width = q.shape
    rows = requests * positions
    heads = width // HD
    whole = pl.BlockSpec((requests, positions, HD), lambda h: (0, 0, h))
    carried = [
        pl.BlockSpec((1, rows, 2 * HD), lambda h: (h, 0, 0)),
        pl.BlockSpec((1, rows, HD), lambda h: (h, 0, 0)),
    ]
    blocks = [array for pair in pairs for array in pair]
    specs = [whole] + carried
    specs += [pl.BlockSpec((array.shape[0], HD), lambda h: (0, h)) for array in blocks]
    operands = [q, *state, *blocks]
    if lengths is not None:
        specs = [pl.BlockSpec(memory_space=pltpu.SMEM)] + specs
        operands = [lengths] + operands
        out_shape, out_specs = jax.ShapeDtypeStruct(q.shape, jnp.bfloat16), whole
    else:
        out_shape = [jax.ShapeDtypeStruct(array.shape, array.dtype) for array in state]
        out_specs = carried
    key_rows = BLOCK * len(pairs)
    return pl.pallas_call(
        functools.partial(stage_kernel, lengths is not None, len(pairs)),
        grid=(heads,),
        out_shape=out_shape,
        in_specs=specs,
        out_specs=out_specs,
        compiler_params=pltpu.CompilerParams(vmem_limit_bytes=40 * MIB),
        cost_estimate=pl.CostEstimate(
            flops=4 * rows * key_rows * width,
            bytes_accessed=8 * MIB,
            transcendentals=rows * key_rows * heads,
        ),
    )(*operands)


def per_device(
    hidden,
    row_counts,
    ln_gain,
    ln_bias,
    key_weight,
    value_weight,
    suffix_q,
    suffix_k,
    suffix_v,
    suffix_lengths,
):
    store = lax.axis_index("store")
    stores = lax.axis_size("store")
    ring = lax.axis_size("req")
    depth = ring * key_weight.shape[0]
    around = [
        (s * ring + z, s * ring + (z + (1 if s % 2 == 0 else ring - 1)) % ring)
        for s in range(stores)
        for z in range(ring)
    ]
    across = [(s, s + 1 - 2 * (s % 2)) for s in range(stores)]
    far = [(s, (s + 2) % 4) for s in range(stores)]

    def step(array):
        return lax.ppermute(array, ("store", "req"), around)

    def swap(array):
        return lax.ppermute(array, "store", across)

    parts = project_rows(
        row_counts,
        hidden,
        swap(hidden),
        ln_gain[None, :],
        ln_bias[None, :],
        key_weight,
        value_weight,
    )
    first, second = parts[:5], parts[5:]

    total = step(first[0]) + first[1]
    rest = step(second[0]) + second[1]
    total = step(total) + first[2]
    rest = step(rest) + second[2]
    state = attend_own(suffix_q, suffix_k, suffix_v)
    total, state = lax.optimization_barrier((total, state))
    total = step(total) + first[3]
    rest = step(rest)
    total = step(total) + first[4]
    total = total + swap(rest)
    mean = total[SPAN, :SPAN] / depth
    var = total[SPAN + 1, :SPAN] / depth - mean * mean
    rows = (total[:SPAN] - mean[:, None] * total[SPAN + 2][None, :]) * lax.rsqrt(var + epsilon)[
        :, None
    ] + total[SPAN + 3][None, :]
    rows = rows.astype(jnp.bfloat16)

    rows_far = lax.ppermute(rows, "store", far)
    low = jnp.where(store < 2, rows, rows_far)
    high = jnp.where(store < 2, rows_far, rows)
    low_rows = (row_counts[0] + row_counts[1]) // ring
    mine = jnp.where(
        jnp.arange(BLOCK, dtype=jnp.int32)[:, None] < low_rows,
        jnp.pad(low, ((0, BLOCK - SPAN), (0, 0))),
        jnp.pad(high, ((BLOCK - SPAN, 0), (0, 0))),
    )

    other = swap(mine)
    g1 = step(mine)
    h1 = step(other)
    xg1 = swap(g1)
    g2 = step(g1)
    xh1 = swap(h1)
    h2 = step(h1)
    xg2 = swap(g2)
    g3 = step(g2)
    xh2 = swap(h2)
    h3 = step(h2)

    def upper(g, xg, h, xh):
        return (g, xg, h, xh)

    def lower(g, xg, h, xh):
        return (xh, h, xg, g)

    near = (g1, xg1, h1, xh1)
    state = attend(
        suffix_q, state, [(mine, other, other, mine), upper(*near), lower(*near)]
    )
    g3, state = lax.optimization_barrier((g3, state))
    xg3 = swap(g3)
    g4 = step(g3)
    xh3 = swap(h3)
    near = (g2, xg2, h2, xh2)
    state = attend(suffix_q, state, [upper(*near), lower(*near)])
    g4, state = lax.optimization_barrier((g4, state))
    xg4 = swap(g4)
    near = (g3, xg3, h3, xh3)
    state = attend(suffix_q, state, [upper(*near), lower(*near)])
    return attend(suffix_q, state, [(g4, xg4, xg4, g4)], lengths=suffix_lengths)


def solution(mesh):
    in_specs = (
        P("store", "req"),
        P(),
        P("req"),
        P("req"),
        P("req", "tp"),
        P("req", "tp"),
        P(("store", "req"), None, "tp"),
        P(("store", "req"), None, "tp"),
        P(("store", "req"), None, "tp"),
        P(("store", "req")),
    )
    out_specs = P(("store", "req"), None, "tp")
    return jax.shard_map(
        per_device, mesh=mesh, in_specs=in_specs, out_specs=out_specs, check_vma=False
    )
```

time: 189 us -> 128 us (0.68)
  waiting for transfers between devices: 83.7 us -> 34.1 us
  Pallas kernels: 48.5 us -> 36.2 us
  local copies, waits for them, and re-layouts: 9.99 us -> 5.49 us
  starting transfers between devices: 42.6 us -> 45.3 us
  other arithmetic: 2.69 us -> 5.16 us
    ppermute x8 -> x14, waiting for transfers between devices: 72.6 us -> 27.1 us  [step(): return lax.ppermute(array, ('store', 'req'), around)]
    pallas_call x4 -> x5, Pallas kernels: 41.1 us -> 24.6 us  [the longest x4 18.7 us: attend(): pl.pallas_call(functools.partial(stage_kernel, lengths is not None, len(p...]
    ppermute x8 -> x14, starting transfers between devices: 19 us -> 30.3 us  [step(): return lax.ppermute(array, ('store', 'req'), around)]
    ppermute x7 -> x10, starting transfers between devices: 21.1 us -> 13.1 us  [swap(): return lax.ppermute(array, 'store', across)]
    pallas_call x1, Pallas kernels: 7.46 us -> 11.6 us  [project_rows(): pl.pallas_call(projection_kernel, out_shape=[jax.ShapeDtypeStruct((SPAN +...]
    ppermute x7 -> x10, waiting for transfers between devices: 5.87 us -> 1.82 us  [swap(): return lax.ppermute(array, 'store', across)]
    unnamed x20 -> x26, local copies, waits for them, and re-layouts: 6.13 us -> 2.25 us
  transfers between devices with their start and end apart: 16 -> 25, of which waited for: 12 -> 12; matrix products, arithmetic and copies ran while one was open for 1% -> 5% of each run, Pallas kernels for 15% -> 16%
where the time goes in v2:
time: 128 us
  starting transfers between devices  45.3 us (35%)
  Pallas kernels  36.2 us (28%)
  waiting for transfers between devices  34.1 us (27%)
  local copies, waits for them, and re-layouts  5.49 us (4%)
  other arithmetic  5.16 us (4%)
  between operations  1.6 us (1%)
    ppermute x14, starting transfers between devices, step(): return lax.ppermute(array, ('store', 'req'), around)  30.3 us
    ppermute x14, waiting for transfers between devices, step(): return lax.ppermute(array, ('store', 'req'), around)  27.1 us
    pallas_call x4, Pallas kernels, attend(): pl.pallas_call(functools.partial(stage_kernel, lengths is not None, len(p...  18.7 us
    ppermute x10, starting transfers between devices, swap(): return lax.ppermute(array, 'store', across)  13.1 us
    pallas_call x1, Pallas kernels, project_rows(): pl.pallas_call(projection_kernel, out_shape=[jax.ShapeDtypeStruct((SPAN +...  11.6 us
    pallas_call x1, Pallas kernels, attend_own(): pl.pallas_call(own_kernel, grid=(heads,), out_shape=[jax.ShapeDtypeStruct...  5.92 us
    ppermute x1, waiting for transfers between devices, per_device(): rows_far = lax.ppermute(rows, 'store', far)  5.21 us
  transfers between devices with their start and end apart: 25, of which 12 were waited for; matrix products, arithmetic and copies ran while one was open for 5% of the time, Pallas kernels for 16%

profile of v2, /device:TPU:1, one launch (start us, length us, event | category | flops | bytes accessed | tf_op | source)
XLA Modules:
  0.0 127.9 jit_solution(4208361312092810034)
XLA Ops:
  0.0 3.2 %collective-permute-start = (bf16[1024,1152]{1,0:T(8,128)(2,1)}, bf16[1024,1152]{1,0:T(8,128)(2,1)S(1)}, u32[]{:S(2)}, u32[]{:S(2)}) collective-permute-start(bf16[1024,1152]{1,0:T(8,128)(2,1)} %hidden.1), channel_id=1, source_target_pairs={{0,64},{64,0},{128,192},{192,128},{1,65},{65,1},{129,193},{193,129... | collective-permute-start | bytes 7077896 | tf_op jit(solution)/shard_map/ppermute | solution.py:327
  3.2 1.3 %broadcast_in_dim.18.gain = f32[1,1152]{1,0:T(1,128)} reshape(f32[1152]{0:T(1024)} %param.12) | data formatting | bytes 9216 | tf_op jit(solution)/shard_map/broadcast_in_dim | solution.py:333
  4.5 1.3 %broadcast_in_dim.19.bias = f32[1,1152]{1,0:T(1,128)} reshape(f32[1152]{0:T(1024)} %param.13) | data formatting | bytes 9216 | tf_op jit(solution)/shard_map/broadcast_in_dim | solution.py:334
  5.8 1.8 %collective-permute-done.hidden_other = bf16[1024,1152]{1,0:T(8,128)(2,1)S(1)} collective-permute-done((bf16[1024,1152]{1,0:T(8,128)(2,1)}, bf16[1024,1152]{1,0:T(8,128)(2,1)S(1)}, u32[]{:S(2)}, u32[]{:S(2)}) %collective-permute-start) | collective-permute-done | bytes 2359328 | tf_op jit(solution)/shard_map/ppermute | solution.py:327
  7.6 1.4 %copy-done.12 = bf16[1024,1152]{1,0:T(8,128)(2,1)} copy-done((bf16[1024,1152]{1,0:T(8,128)(2,1)}, bf16[1024,1152]{1,0:T(8,128)(2,1)S(1)}, u32[]{:S(2)}) %copy-start.12) | copy-done | bytes 2359320
  9.0 11.6 %shard_map.100 = (f32[232,640]{1,0:T(8,128)}, f32[232,640]{1,0:T(8,128)}, f32[232,640]{1,0:T(8,128)}, f32[232,640]{1,0:T(8,128)}, f32[232,640]{1,0:T(8,128)}, /*...) custom-call(s32[4]{0:T(128)} %counts.1, bf16[1024,1152]{1,0:T(8,128)(2,1)} %hidden.1, ...), custom_call_target="tpu_custom_call" | custom-call | flops 2642411520 | bytes 12582912 | tf_op jit(solution)/shard_map/pallas_call | solution.py:137
  20.6 0.0 copy-start
  20.6 0.0 copy-start.1
  20.6 0.0 copy-start.2
  20.7 3.9 %collective-permute-start.1 = (f32[232,640]{1,0:T(8,128)}, f32[232,640]{1,0:T(8,128)S(1)}, u32[]{:S(2)}, u32[]{:S(2)}) collective-permute-start(f32[232,640]{1,0:T(8,128)} %get-tuple-element.30), channel_id=1, source_target_pairs={{0,8},{8,16},{16,24},{24,32},{32,40},{40,48},{48,56},{56,0},{64,12... | collective-permute-start | bytes 1781768 | tf_op jit(solution)/shard_map/ppermute | solution.py:324
  24.6 0.7 collective-permute-start.5
  25.3 6.5 %collective-permute-done.1 = f32[232,640]{1,0:T(8,128)S(1)} collective-permute-done((f32[232,640]{1,0:T(8,128)}, f32[232,640]{1,0:T(8,128)S(1)}, u32[]{:S(2)}, u32[]{:S(2)}) %collective-permute-start.1) | collective-permute-done | bytes 593952 | tf_op jit(solution)/shard_map/ppermute | solution.py:324
  31.8 1.2 add.54
  33.0 3.1 %collective-permute-start.2 = (f32[232,640]{1,0:T(8,128)S(1)}, f32[232,640]{1,0:T(8,128)S(1)}, u32[]{:S(2)}, u32[]{:S(2)}) collective-permute-start(f32[232,640]{1,0:T(8,128)S(1)} %add.54), channel_id=1, source_target_pairs={{0,8},{8,16},{16,24},{24,32},{32,40},{40,48},{48,56},{56,0},{64,12... | collective-permute-start | bytes 1781768 | tf_op jit(solution)/shard_map/ppermute | solution.py:324
  36.0 2.1 %collective-permute-done.5 = f32[232,640]{1,0:T(8,128)S(1)} collective-permute-done((f32[232,640]{1,0:T(8,128)}, f32[232,640]{1,0:T(8,128)S(1)}, u32[]{:S(2)}, u32[]{:S(2)}) %collective-permute-start.5) | collective-permute-done | bytes 593952 | tf_op jit(solution)/shard_map/ppermute | solution.py:324
  38.1 1.2 add.58
  39.3 3.1 %collective-permute-start.6 = (f32[232,640]{1,0:T(8,128)S(1)}, f32[232,640]{1,0:T(8,128)S(1)}, u32[]{:S(2)}, u32[]{:S(2)}) collective-permute-start(f32[232,640]{1,0:T(8,128)S(1)} %add.58), channel_id=1, source_target_pairs={{0,8},{8,16},{16,24},{24,32},{32,40},{40,48},{48,56},{56,0},{64,12... | collective-permute-start | bytes 1781768 | tf_op jit(solution)/shard_map/ppermute | solution.py:324
  42.4 5.9 %shard_map.101 = (f32[5,512,256]{2,1,0:T(8,128)S(1)}, bf16[5,512,128]{2,1,0:T(8,128)(2,1)S(1)}) custom-call(bf16[4,128,640]{2,1,0:T(8,128)(2,1)S(1)} %copy-done, bf16[4,128,640]{2,1,0:T(8,128)(2,1)S(1)} %copy-done.1, bf16[4,128,640]{2,1,0:T(8,128)(2,1)S(1)} %copy-done.2), custom_call_target="tpu_custom_call" | custom-call | flops 167772160 | bytes 6291456 | tf_op jit(solution)/shard_map/pallas_call | solution.py:242
  48.4 0.0 copy-start.3
  48.4 0.1 add.55
  48.5 0.1 collective-permute-start.3
  48.6 2.2 %collective-permute-done.6 = f32[232,640]{1,0:T(8,128)S(1)} collective-permute-done((f32[232,640]{1,0:T(8,128)S(1)}, f32[232,640]{1,0:T(8,128)S(1)}, u32[]{:S(2)}, u32[]{:S(2)}) %collective-permute-start.6) | collective-permute-done | bytes 593952 | tf_op jit(solution)/shard_map/ppermute | solution.py:324
  50.7 0.1 add.59
  50.8 0.0 copy-start.11
  50.8 3.2 %collective-permute-start.7 = (f32[232,640]{1,0:T(8,128)S(1)}, f32[232,640]{1,0:T(8,128)S(1)}, u32[]{:S(2)}, u32[]{:S(2)}) collective-permute-start(f32[232,640]{1,0:T(8,128)S(1)} %add.59), channel_id=1, source_target_pairs={{0,8},{8,16},{16,24},{24,32},{32,40},{40,48},{48,56},{56,0},{64,12... | collective-permute-start | bytes 1781768 | tf_op jit(solution)/shard_map/ppermute | solution.py:324
  54.0 3.6 %collective-permute-done.3 = f32[232,640]{1,0:T(8,128)S(1)} collective-permute-done((f32[232,640]{1,0:T(8,128)S(1)}, f32[232,640]{1,0:T(8,128)S(1)}, u32[]{:S(2)}, u32[]{:S(2)}) %collective-permute-start.3) | collective-permute-done | bytes 593952 | tf_op jit(solution)/shard_map/ppermute | solution.py:324
  57.6 0.1 add.56
  57.7 2.7 %collective-permute-start.4 = (f32[232,640]{1,0:T(8,128)S(1)}, f32[232,640]{1,0:T(8,128)S(1)}, u32[]{:S(2)}, u32[]{:S(2)}) collective-permute-start(f32[232,640]{1,0:T(8,128)S(1)} %add.56), channel_id=1, source_target_pairs={{0,8},{8,16},{16,24},{24,32},{32,40},{40,48},{48,56},{56,0},{64,12... | collective-permute-start | bytes 1781768 | tf_op jit(solution)/shard_map/ppermute | solution.py:324
  60.4 3.6 %collective-permute-done.7 = f32[232,640]{1,0:T(8,128)S(1)} collective-permute-done((f32[232,640]{1,0:T(8,128)S(1)}, f32[232,640]{1,0:T(8,128)S(1)}, u32[]{:S(2)}, u32[]{:S(2)}) %collective-permute-start.7) | collective-permute-done | bytes 593952 | tf_op jit(solution)/shard_map/ppermute | solution.py:324
  64.0 1.1 collective-permute-start.8
  65.1 5.3 %collective-permute-done.4 = f32[232,640]{1,0:T(8,128)S(1)} collective-permute-done((f32[232,640]{1,0:T(8,128)S(1)}, f32[232,640]{1,0:T(8,128)S(1)}, u32[]{:S(2)}, u32[]{:S(2)}) %collective-permute-start.4) | collective-permute-done | bytes 593952 | tf_op jit(solution)/shard_map/ppermute | solution.py:324
  70.4 0.1 add_add_fusion
  70.5 0.8 copy-done.6
  71.3 0.9 fusion.2
  72.2 1.8 %collective-permute-start.9 = (bf16[224,640]{1,0:T(8,128)(2,1)}, bf16[224,640]{1,0:T(8,128)(2,1)}, u32[]{:S(2)}, u32[]{:S(2)}) collective-permute-start(bf16[224,640]{1,0:T(8,128)(2,1)} %fusion.2), channel_id=1, source_target_pairs={{0,128},{64,192},{128,0},{192,64},{1,129},{65,193},{129,1},{193,65... | collective-permute-start | bytes 860168 | tf_op jit(solution)/shard_map/ppermute | solution.py:357
  74.0 0.6 fusion.3
  76.0 0.0 copy-start.4
  76.0 5.2 %collective-permute-done.9 = bf16[224,640]{1,0:T(8,128)(2,1)} collective-permute-done((bf16[224,640]{1,0:T(8,128)(2,1)}, bf16[224,640]{1,0:T(8,128)(2,1)}, u32[]{:S(2)}, u32[]{:S(2)}) %collective-permute-start.9) | collective-permute-done | bytes 286752 | tf_op jit(solution)/shard_map/ppermute | solution.py:357
  81.2 1.4 %broadcast_select_fusion.1 = (bf16[224,640]{1,0:T(8,128)(2,1)S(1)}, bf16[224,640]{1,0:T(8,128)(2,1)S(1)}) fusion(bf16[224,640]{1,0:T(8,128)(2,1)} %collective-permute-done.9, pred[]{:T(512)S(6)} %lt.17, f32[640]{0:T(1024)S(1)} %get-tuple-element.56, f32[224]{0:T(256)S(1)} %add_rsqrt_fusion, f32[640]{0:T(1024)S(1)} %get-tuple-element.55, f32[224]{0:T(256)S(1)} %bitcast.5, ...), kind=kLoop, calls=%fused_computation.7 | loop fusion | flops 1003520 | bytes 1440513 | tf_op jit(solution)/shard_map/jit(_where)/select_n | solution.py:358
  82.6 0.2 pad_select_fusion.refs_3_.refs_6_
  82.8 2.1 %collective-permute-start.13 = (bf16[256,640]{1,0:T(8,128)(2,1)S(1)}, bf16[256,640]{1,0:T(8,128)(2,1)S(1)}, u32[]{:S(2)}, u32[]{:S(2)}) collective-permute-start(bf16[256,640]{1,0:T(8,128)(2,1)S(1)} %pad_select_fusion.refs_3_.refs_6_), channel_id=1, source_target_pairs={{0,64},{64,0},{128,192},{192,128},{1,65},{65,1},{129,193},{193,129... | collective-permute-start | bytes 983048 | tf_op jit(solution)/shard_map/ppermute | solution.py:327
  84.9 2.6 %collective-permute-start.10 = (bf16[256,640]{1,0:T(8,128)(2,1)S(1)}, bf16[256,640]{1,0:T(8,128)(2,1)S(1)}, u32[]{:S(2)}, u32[]{:S(2)}) collective-permute-start(bf16[256,640]{1,0:T(8,128)(2,1)S(1)} %pad_select_fusion.refs_3_.refs_6_), channel_id=1, source_target_pairs={{0,8},{8,16},{16,24},{24,32},{32,40},{40,48},{48,56},{56,0},{64,12... | collective-permute-start | bytes 983048 | tf_op jit(solution)/shard_map/ppermute | solution.py:324
  87.5 0.0 collective-permute-done.13.refs_4_.refs_5_
  87.5 1.3 collective-permute-start.15
  88.7 2.8 %collective-permute-done.10.refs_7_.refs_14_ = bf16[256,640]{1,0:T(8,128)(2,1)S(1)} collective-permute-done((bf16[256,640]{1,0:T(8,128)(2,1)S(1)}, bf16[256,640]{1,0:T(8,128)(2,1)S(1)}, u32[]{:S(2)}, u32[]{:S(2)}) %collective-permute-start.10) | collective-permute-done | bytes 327712 | tf_op jit(solution)/shard_map/ppermute | solution.py:324
  91.5 3.1 %collective-permute-start.11 = (bf16[256,640]{1,0:T(8,128)(2,1)S(1)}, bf16[256,640]{1,0:T(8,128)(2,1)S(1)}, u32[]{:S(2)}, u32[]{:S(2)}) collective-permute-start(bf16[256,640]{1,0:T(8,128)(2,1)S(1)} %collective-permute-done.10.refs_7_.refs_14_), channel_id=1, source_target_pairs={{0,8},{8,16},{16,24},{24,32},{32,40},{40,48},{48,56},{56,0},{64,12... | collective-permute-start | bytes 983048 | tf_op jit(solution)/shard_map/ppermute | solution.py:324
  94.6 0.4 collective-permute-done.15.refs_9_.refs_12_
  95.0 3.1 %collective-permute-start.19 = (bf16[256,640]{1,0:T(8,128)(2,1)S(1)}, bf16[256,640]{1,0:T(8,128)(2,1)S(1)}, u32[]{:S(2)}, u32[]{:S(2)}) collective-permute-start(bf16[256,640]{1,0:T(8,128)(2,1)S(1)} %collective-permute-done.15.refs_9_.refs_12_), channel_id=1, source_target_pairs={{0,8},{8,16},{16,24},{24,32},{32,40},{40,48},{48,56},{56,0},{64,12... | collective-permute-start | bytes 983048 | tf_op jit(solution)/shard_map/ppermute | solution.py:324
  98.1 0.0 collective-permute-start.14
  98.1 0.5 collective-permute-start.16
  98.7 3.1 %collective-permute-start.12 = (bf16[256,640]{1,0:T(8,128)(2,1)S(1)}, bf16[256,640]{1,0:T(8,128)(2,1)S(1)}, u32[]{:S(2)}, u32[]{:S(2)}) collective-permute-start(bf16[256,640]{1,0:T(8,128)(2,1)S(1)} %collective-permute-done.11.refs_3_.refs_10_), channel_id=1, source_target_pairs={{0,8},{8,16},{16,24},{24,32},{32,40},{40,48},{48,56},{56,0},{64,12... | collective-permute-start | bytes 983048 | tf_op jit(solution)/shard_map/ppermute | solution.py:324
  101.8 0.4 collective-permute-done.19.refs_5_.refs_8_
  102.2 2.9 %collective-permute-start.20 = (bf16[256,640]{1,0:T(8,128)(2,1)S(1)}, bf16[256,640]{1,0:T(8,128)(2,1)S(1)}, u32[]{:S(2)}, u32[]{:S(2)}) collective-permute-start(bf16[256,640]{1,0:T(8,128)(2,1)S(1)} %collective-permute-done.19.refs_5_.refs_8_), channel_id=1, source_target_pairs={{0,64},{64,0},{128,192},{192,128},{1,65},{65,1},{129,193},{193,129... | collective-permute-start | bytes 983048 | tf_op jit(solution)/shard_map/ppermute | solution.py:327
  105.1 0.2 collective-permute-start.22
  105.3 5.4 %shard_map.102 = (f32[5,512,256]{2,1,0:T(8,128)S(1)}, bf16[5,512,128]{2,1,0:T(8,128)(2,1)S(1)}) custom-call(bf16[4,128,640]{2,1,0:T(8,128)(2,1)S(1)} %copy-done, f32[5,512,256]{2,1,0:T(8,128)S(1)} %get-tuple-element.41.refs_1_, bf16[5,512,128]{2,1,0:T(8,128)(2,1)S(1)} %copy-done.4, bf16[256,640]{1,0:T(8,128)(2,1)S(1)} %pad_select_fusion.refs_3_.refs_6_, ...), custom_call_target="tpu_custom_call" | custom-call | flops 1006632960 | bytes 8388608 | tf_op jit(solution)/shard_map/pallas_call | solution.py:284
  110.7 0.1 collective-permute-start.17
  110.8 0.1 collective-permute-start.21
  110.9 0.4 collective-permute-done.22.refs_5_.refs_8_
  111.3 2.1 %collective-permute-start.23 = (bf16[256,640]{1,0:T(8,128)(2,1)S(1)}, bf16[256,640]{1,0:T(8,128)(2,1)S(1)}, u32[]{:S(2)}, u32[]{:S(2)}) collective-permute-start(bf16[256,640]{1,0:T(8,128)(2,1)S(1)} %collective-permute-done.22.refs_5_.refs_8_), channel_id=1, source_target_pairs={{0,64},{64,0},{128,192},{192,128},{1,65},{65,1},{129,193},{193,129... | collective-permute-start | bytes 983048 | tf_op jit(solution)/shard_map/ppermute | solution.py:327
  113.4 4.3 %shard_map.103 = (f32[5,512,256]{2,1,0:T(8,128)S(1)}, bf16[5,512,128]{2,1,0:T(8,128)(2,1)S(1)}) custom-call(bf16[4,128,640]{2,1,0:T(8,128)(2,1)S(1)} %copy-done, f32[5,512,256]{2,1,0:T(8,128)S(1)} %get-tuple-element.46.refs_1_, bf16[5,512,128]{2,1,0:T(8,128)(2,1)S(1)} %get-tuple-element.47.refs_2_, ...), custom_call_target="tpu_custom_call" | custom-call | flops 671088640 | bytes 8388608 | tf_op jit(solution)/shard_map/pallas_call | solution.py:284
  117.7 0.0 copy-start.5
  117.7 1.1 collective-permute-start.24
  118.9 4.3 %shard_map.104 = (f32[5,512,256]{2,1,0:T(8,128)S(1)}, bf16[5,512,128]{2,1,0:T(8,128)(2,1)S(1)}) custom-call(bf16[4,128,640]{2,1,0:T(8,128)(2,1)S(1)} %copy-done, f32[5,512,256]{2,1,0:T(8,128)S(1)} %get-tuple-element.50.refs_1_, bf16[5,512,128]{2,1,0:T(8,128)(2,1)S(1)} %get-tuple-element.51.refs_2_, ...), custom_call_target="tpu_custom_call" | custom-call | flops 671088640 | bytes 8388608 | tf_op jit(solution)/shard_map/pallas_call | solution.py:284
  123.2 4.6 %shard_map.105 = bf16[4,128,640]{2,1,0:T(8,128)(2,1)} custom-call(s32[4]{0:T(128)S(1)} %copy-done.5, bf16[4,128,640]{2,1,0:T(8,128)(2,1)S(1)} %copy-done, f32[5,512,256]{2,1,0:T(8,128)S(1)} %get-tuple-element.52.refs_2_, bf16[5,512,128]{2,1,0:T(8,128)(2,1)S(1)} %get-tuple-element.53.refs_3_, bf16[256,640]{1,0:T(8,128)(2,1)S(1)} %collective-permute-done.17.refs_4_.refs_7_, ...), custom_call_target="tpu_custom_call" | custom-call | flops 335544320 | bytes 8388608 | tf_op jit(solution)/shard_map/pallas_call | solution.py:284
  (34 shorter events, 0.1 us)
Async XLA Ops:
  0.0 7.6 %collective-permute-start = (bf16[1024,1152]{1,0:T(8,128)(2,1)}, bf16[1024,1152]{1,0:T(8,128)(2,1)S(1)}, u32[]{:S(2)}, u32[]{:S(2)}) collective-permute-start(bf16[1024,1152]{1,0:T(8,128)(2,1)} %hidden.1), channel_id=1, source_target_pairs={{0,64},{64,0},{128,192},{192,128},{1,65},{65,1},{129,193},{193,129... | collective-permute-start | bytes 7077896 | tf_op jit(solution)/shard_map/ppermute | solution.py:327
  7.6 1.4 %copy-start.12 = (bf16[1024,1152]{1,0:T(8,128)(2,1)}, bf16[1024,1152]{1,0:T(8,128)(2,1)S(1)}, u32[]{:S(2)}) copy-start(bf16[1024,1152]{1,0:T(8,128)(2,1)S(1)} %collective-permute-done.hidden_other) | copy-start | bytes 7077892
  20.6 21.8 %copy-start = (bf16[4,128,640]{2,1,0:T(8,128)(2,1)S(1)}, bf16[4,128,640]{2,1,0:T(8,128)(2,1)}, u32[]{:S(2)}) copy-start(bf16[4,128,640]{2,1,0:T(8,128)(2,1)} %refs_1_.1) | copy-start | bytes 1966084
  20.6 21.8 %copy-start.1 = (bf16[4,128,640]{2,1,0:T(8,128)(2,1)S(1)}, bf16[4,128,640]{2,1,0:T(8,128)(2,1)}, u32[]{:S(2)}) copy-start(bf16[4,128,640]{2,1,0:T(8,128)(2,1)} %own_k.1) | copy-start | bytes 1966084
  20.6 21.8 %copy-start.2 = (bf16[4,128,640]{2,1,0:T(8,128)(2,1)S(1)}, bf16[4,128,640]{2,1,0:T(8,128)(2,1)}, u32[]{:S(2)}) copy-start(bf16[4,128,640]{2,1,0:T(8,128)(2,1)} %own_v.1) | copy-start | bytes 1966084
  20.7 11.1 %collective-permute-start.1 = (f32[232,640]{1,0:T(8,128)}, f32[232,640]{1,0:T(8,128)S(1)}, u32[]{:S(2)}, u32[]{:S(2)}) collective-permute-start(f32[232,640]{1,0:T(8,128)} %get-tuple-element.30), channel_id=1, source_target_pairs={{0,8},{8,16},{16,24},{24,32},{32,40},{40,48},{48,56},{56,0},{64,12... | collective-permute-start | bytes 1781768 | tf_op jit(solution)/shard_map/ppermute | solution.py:324
  24.6 13.6 %collective-permute-start.5 = (f32[232,640]{1,0:T(8,128)}, f32[232,640]{1,0:T(8,128)S(1)}, u32[]{:S(2)}, u32[]{:S(2)}) collective-permute-start(f32[232,640]{1,0:T(8,128)} %get-tuple-element.38), channel_id=1, source_target_pairs={{0,8},{8,16},{16,24},{24,32},{32,40},{40,48},{48,56},{56,0},{64,12... | collective-permute-start | bytes 1781768 | tf_op jit(solution)/shard_map/ppermute | solution.py:324
  31.8 16.6 %copy-start.9 = (f32[232,640]{1,0:T(8,128)S(1)}, f32[232,640]{1,0:T(8,128)}, u32[]{:S(2)}) copy-start(f32[232,640]{1,0:T(8,128)} %get-tuple-element.32) | copy-start | bytes 1781764
  33.0 15.4 %collective-permute-start.2 = (f32[232,640]{1,0:T(8,128)S(1)}, f32[232,640]{1,0:T(8,128)S(1)}, u32[]{:S(2)}, u32[]{:S(2)}) collective-permute-start(f32[232,640]{1,0:T(8,128)S(1)} %add.54), channel_id=1, source_target_pairs={{0,8},{8,16},{16,24},{24,32},{32,40},{40,48},{48,56},{56,0},{64,12... | collective-permute-start | bytes 1781768 | tf_op jit(solution)/shard_map/ppermute | solution.py:324
  38.1 12.6 %copy-start.8 = (f32[232,640]{1,0:T(8,128)S(1)}, f32[232,640]{1,0:T(8,128)}, u32[]{:S(2)}) copy-start(f32[232,640]{1,0:T(8,128)} %get-tuple-element.40) | copy-start | bytes 1781764
  39.3 18.3 %copy-start.7 = (f32[232,640]{1,0:T(8,128)S(1)}, f32[232,640]{1,0:T(8,128)}, u32[]{:S(2)}) copy-start(f32[232,640]{1,0:T(8,128)} %get-tuple-element.36) | copy-start | bytes 1781764
  39.3 11.4 %collective-permute-start.6 = (f32[232,640]{1,0:T(8,128)S(1)}, f32[232,640]{1,0:T(8,128)S(1)}, u32[]{:S(2)}, u32[]{:S(2)}) collective-permute-start(f32[232,640]{1,0:T(8,128)S(1)} %add.58), channel_id=1, source_target_pairs={{0,8},{8,16},{16,24},{24,32},{32,40},{40,48},{48,56},{56,0},{64,12... | collective-permute-start | bytes 1781768 | tf_op jit(solution)/shard_map/ppermute | solution.py:324
  48.4 9.3 %copy-start.3 = (bf16[5,512,128]{2,1,0:T(8,128)(2,1)}, bf16[5,512,128]{2,1,0:T(8,128)(2,1)S(1)}, u32[]{:S(2)}) copy-start(bf16[5,512,128]{2,1,0:T(8,128)(2,1)S(1)} %get-tuple-element.42.refs_2_) | copy-start | bytes 1966084
  48.4 22.0 %copy-start.10 = (f32[232,640]{1,0:T(8,128)S(1)}, f32[232,640]{1,0:T(8,128)}, u32[]{:S(2)}) copy-start(f32[232,640]{1,0:T(8,128)} %get-tuple-element.37) | copy-start | bytes 1781764
  48.5 9.2 %collective-permute-start.3 = (f32[232,640]{1,0:T(8,128)S(1)}, f32[232,640]{1,0:T(8,128)S(1)}, u32[]{:S(2)}, u32[]{:S(2)}) collective-permute-start(f32[232,640]{1,0:T(8,128)S(1)} %add.55), channel_id=1, source_target_pairs={{0,8},{8,16},{16,24},{24,32},{32,40},{40,48},{48,56},{56,0},{64,12... | collective-permute-start | bytes 1781768 | tf_op jit(solution)/shard_map/ppermute | solution.py:324
  50.8 23.2 %copy-start.11 = (s32[4]{0:T(128)S(1)}, s32[4]{0:T(128)}, u32[]{:S(2)}) copy-start(s32[4]{0:T(128)} %counts.1) | copy-start | bytes 52
  50.8 13.1 %collective-permute-start.7 = (f32[232,640]{1,0:T(8,128)S(1)}, f32[232,640]{1,0:T(8,128)S(1)}, u32[]{:S(2)}, u32[]{:S(2)}) collective-permute-start(f32[232,640]{1,0:T(8,128)S(1)} %add.59), channel_id=1, source_target_pairs={{0,8},{8,16},{16,24},{24,32},{32,40},{40,48},{48,56},{56,0},{64,12... | collective-permute-start | bytes 1781768 | tf_op jit(solution)/shard_map/ppermute | solution.py:324
  57.7 12.6 %collective-permute-start.4 = (f32[232,640]{1,0:T(8,128)S(1)}, f32[232,640]{1,0:T(8,128)S(1)}, u32[]{:S(2)}, u32[]{:S(2)}) collective-permute-start(f32[232,640]{1,0:T(8,128)S(1)} %add.56), channel_id=1, source_target_pairs={{0,8},{8,16},{16,24},{24,32},{32,40},{40,48},{48,56},{56,0},{64,12... | collective-permute-start | bytes 1781768 | tf_op jit(solution)/shard_map/ppermute | solution.py:324
  64.0 6.4 %collective-permute-start.8 = (f32[232,640]{1,0:T(8,128)S(1)}, f32[232,640]{1,0:T(8,128)S(1)}, u32[]{:S(2)}, u32[]{:S(2)}) collective-permute-start(f32[232,640]{1,0:T(8,128)S(1)} %collective-permute-done.7), channel_id=1, source_target_pairs={{0,64},{64,0},{128,192},{192,128},{1,65},{65,1},{129,193},{193,129... | collective-permute-start | bytes 1781768 | tf_op jit(solution)/shard_map/ppermute | solution.py:327
  70.5 0.8 copy-start.6
  72.2 9.0 %collective-permute-start.9 = (bf16[224,640]{1,0:T(8,128)(2,1)}, bf16[224,640]{1,0:T(8,128)(2,1)}, u32[]{:S(2)}, u32[]{:S(2)}) collective-permute-start(bf16[224,640]{1,0:T(8,128)(2,1)} %fusion.2), channel_id=1, source_target_pairs={{0,128},{64,192},{128,0},{192,64},{1,129},{65,193},{129,1},{193,65... | collective-permute-start | bytes 860168 | tf_op jit(solution)/shard_map/ppermute | solution.py:357
  76.0 29.3 %copy-start.4 = (bf16[5,512,128]{2,1,0:T(8,128)(2,1)S(1)}, bf16[5,512,128]{2,1,0:T(8,128)(2,1)}, u32[]{:S(2)}) copy-start(bf16[5,512,128]{2,1,0:T(8,128)(2,1)} %copy-done.3) | copy-start | bytes 1966084
  82.8 4.7 %collective-permute-start.13 = (bf16[256,640]{1,0:T(8,128)(2,1)S(1)}, bf16[256,640]{1,0:T(8,128)(2,1)S(1)}, u32[]{:S(2)}, u32[]{:S(2)}) collective-permute-start(bf16[256,640]{1,0:T(8,128)(2,1)S(1)} %pad_select_fusion.refs_3_.refs_6_), channel_id=1, source_target_pairs={{0,64},{64,0},{128,192},{192,128},{1,65},{65,1},{129,193},{193,129... | collective-permute-start | bytes 983048 | tf_op jit(solution)/shard_map/ppermute | solution.py:327
  84.9 6.6 %collective-permute-start.10 = (bf16[256,640]{1,0:T(8,128)(2,1)S(1)}, bf16[256,640]{1,0:T(8,128)(2,1)S(1)}, u32[]{:S(2)}, u32[]{:S(2)}) collective-permute-start(bf16[256,640]{1,0:T(8,128)(2,1)S(1)} %pad_select_fusion.refs_3_.refs_6_), channel_id=1, source_target_pairs={{0,8},{8,16},{16,24},{24,32},{32,40},{40,48},{48,56},{56,0},{64,12... | collective-permute-start | bytes 983048 | tf_op jit(solution)/shard_map/ppermute | solution.py:324
  87.5 7.5 %collective-permute-start.15 = (bf16[256,640]{1,0:T(8,128)(2,1)S(1)}, bf16[256,640]{1,0:T(8,128)(2,1)S(1)}, u32[]{:S(2)}, u32[]{:S(2)}) collective-permute-start(bf16[256,640]{1,0:T(8,128)(2,1)S(1)} %collective-permute-done.13.refs_4_.refs_5_), channel_id=1, source_target_pairs={{0,8},{8,16},{16,24},{24,32},{32,40},{40,48},{48,56},{56,0},{64,12... | collective-permute-start | bytes 983048 | tf_op jit(solution)/shard_map/ppermute | solution.py:324
  91.5 7.1 %collective-permute-start.11 = (bf16[256,640]{1,0:T(8,128)(2,1)S(1)}, bf16[256,640]{1,0:T(8,128)(2,1)S(1)}, u32[]{:S(2)}, u32[]{:S(2)}) collective-permute-start(bf16[256,640]{1,0:T(8,128)(2,1)S(1)} %collective-permute-done.10.refs_7_.refs_14_), channel_id=1, source_target_pairs={{0,8},{8,16},{16,24},{24,32},{32,40},{40,48},{48,56},{56,0},{64,12... | collective-permute-start | bytes 983048 | tf_op jit(solution)/shard_map/ppermute | solution.py:324
  95.0 7.1 %collective-permute-start.19 = (bf16[256,640]{1,0:T(8,128)(2,1)S(1)}, bf16[256,640]{1,0:T(8,128)(2,1)S(1)}, u32[]{:S(2)}, u32[]{:S(2)}) collective-permute-start(bf16[256,640]{1,0:T(8,128)(2,1)S(1)} %collective-permute-done.15.refs_9_.refs_12_), channel_id=1, source_target_pairs={{0,8},{8,16},{16,24},{24,32},{32,40},{40,48},{48,56},{56,0},{64,12... | collective-permute-start | bytes 983048 | tf_op jit(solution)/shard_map/ppermute | solution.py:324
  98.1 6.9 %collective-permute-start.14 = (bf16[256,640]{1,0:T(8,128)(2,1)S(1)}, bf16[256,640]{1,0:T(8,128)(2,1)S(1)}, u32[]{:S(2)}, u32[]{:S(2)}) collective-permute-start(bf16[256,640]{1,0:T(8,128)(2,1)S(1)} %collective-permute-done.10.refs_7_.refs_14_), channel_id=1, source_target_pairs={{0,64},{64,0},{128,192},{192,128},{1,65},{65,1},{129,193},{193,129... | collective-permute-start | bytes 983048 | tf_op jit(solution)/shard_map/ppermute | solution.py:327
  98.1 7.1 %collective-permute-start.16 = (bf16[256,640]{1,0:T(8,128)(2,1)S(1)}, bf16[256,640]{1,0:T(8,128)(2,1)S(1)}, u32[]{:S(2)}, u32[]{:S(2)}) collective-permute-start(bf16[256,640]{1,0:T(8,128)(2,1)S(1)} %collective-permute-done.15.refs_9_.refs_12_), channel_id=1, source_target_pairs={{0,64},{64,0},{128,192},{192,128},{1,65},{65,1},{129,193},{193,129... | collective-permute-start | bytes 983048 | tf_op jit(solution)/shard_map/ppermute | solution.py:327
  98.7 12.0 %collective-permute-start.12 = (bf16[256,640]{1,0:T(8,128)(2,1)S(1)}, bf16[256,640]{1,0:T(8,128)(2,1)S(1)}, u32[]{:S(2)}, u32[]{:S(2)}) collective-permute-start(bf16[256,640]{1,0:T(8,128)(2,1)S(1)} %collective-permute-done.11.refs_3_.refs_10_), channel_id=1, source_target_pairs={{0,8},{8,16},{16,24},{24,32},{32,40},{40,48},{48,56},{56,0},{64,12... | collective-permute-start | bytes 983048 | tf_op jit(solution)/shard_map/ppermute | solution.py:324
  101.8 11.6 %collective-permute-start.18 = (bf16[256,640]{1,0:T(8,128)(2,1)S(1)}, bf16[256,640]{1,0:T(8,128)(2,1)S(1)}, u32[]{:S(2)}, u32[]{:S(2)}) collective-permute-start(bf16[256,640]{1,0:T(8,128)(2,1)S(1)} %collective-permute-done.11.refs_3_.refs_10_), channel_id=1, source_target_pairs={{0,64},{64,0},{128,192},{192,128},{1,65},{65,1},{129,193},{193,129... | collective-permute-start | bytes 983048 | tf_op jit(solution)/shard_map/ppermute | solution.py:327
  102.2 11.2 %collective-permute-start.20 = (bf16[256,640]{1,0:T(8,128)(2,1)S(1)}, bf16[256,640]{1,0:T(8,128)(2,1)S(1)}, u32[]{:S(2)}, u32[]{:S(2)}) collective-permute-start(bf16[256,640]{1,0:T(8,128)(2,1)S(1)} %collective-permute-done.19.refs_5_.refs_8_), channel_id=1, source_target_pairs={{0,64},{64,0},{128,192},{192,128},{1,65},{65,1},{129,193},{193,129... | collective-permute-start | bytes 983048 | tf_op jit(solution)/shard_map/ppermute | solution.py:327
  105.1 6.2 %collective-permute-start.22 = (bf16[256,640]{1,0:T(8,128)(2,1)S(1)}, bf16[256,640]{1,0:T(8,128)(2,1)S(1)}, u32[]{:S(2)}, u32[]{:S(2)}) collective-permute-start(bf16[256,640]{1,0:T(8,128)(2,1)S(1)} %collective-permute-done.19.refs_5_.refs_8_), channel_id=1, source_target_pairs={{0,8},{8,16},{16,24},{24,32},{32,40},{40,48},{48,56},{56,0},{64,12... | collective-permute-start | bytes 983048 | tf_op jit(solution)/shard_map/ppermute | solution.py:324
  110.7 7.0 %collective-permute-start.17 = (bf16[256,640]{1,0:T(8,128)(2,1)S(1)}, bf16[256,640]{1,0:T(8,128)(2,1)S(1)}, u32[]{:S(2)}, u32[]{:S(2)}) collective-permute-start(bf16[256,640]{1,0:T(8,128)(2,1)S(1)} %collective-permute-done.12.refs_3_.refs_10_), channel_id=1, source_target_pairs={{0,8},{8,16},{16,24},{24,32},{32,40},{40,48},{48,56},{56,0},{64,12... | collective-permute-start | bytes 983048 | tf_op jit(solution)/shard_map/ppermute | solution.py:324
  110.8 8.1 %collective-permute-start.21 = (bf16[256,640]{1,0:T(8,128)(2,1)S(1)}, bf16[256,640]{1,0:T(8,128)(2,1)S(1)}, u32[]{:S(2)}, u32[]{:S(2)}) collective-permute-start(bf16[256,640]{1,0:T(8,128)(2,1)S(1)} %collective-permute-done.12.refs_3_.refs_10_), channel_id=1, source_target_pairs={{0,64},{64,0},{128,192},{192,128},{1,65},{65,1},{129,193},{193,129... | collective-permute-start | bytes 983048 | tf_op jit(solution)/shard_map/ppermute | solution.py:327
  111.3 7.6 %collective-permute-start.23 = (bf16[256,640]{1,0:T(8,128)(2,1)S(1)}, bf16[256,640]{1,0:T(8,128)(2,1)S(1)}, u32[]{:S(2)}, u32[]{:S(2)}) collective-permute-start(bf16[256,640]{1,0:T(8,128)(2,1)S(1)} %collective-permute-done.22.refs_5_.refs_8_), channel_id=1, source_target_pairs={{0,64},{64,0},{128,192},{192,128},{1,65},{65,1},{129,193},{193,129... | collective-permute-start | bytes 983048 | tf_op jit(solution)/shard_map/ppermute | solution.py:327
  117.7 5.5 %copy-start.5 = (s32[4]{0:T(128)S(1)}, s32[4]{0:T(128)}, u32[]{:S(2)}) copy-start(s32[4]{0:T(128)} %refs_0_.7) | copy-start | bytes 52
  117.7 5.5 %collective-permute-start.24 = (bf16[256,640]{1,0:T(8,128)(2,1)S(1)}, bf16[256,640]{1,0:T(8,128)(2,1)S(1)}, u32[]{:S(2)}, u32[]{:S(2)}) collective-permute-start(bf16[256,640]{1,0:T(8,128)(2,1)S(1)} %collective-permute-done.17.refs_4_.refs_7_), channel_id=1, source_target_pairs={{0,64},{64,0},{128,192},{192,128},{1,65},{65,1},{129,193},{193,129... | collective-permute-start | bytes 983048 | tf_op jit(solution)/shard_map/ppermute | solution.py:327

commit v3 on v2

v3 whole, which is shorter than its diff:
```python
import functools
import math

import jax
import jax.numpy as jnp
from jax import lax
from jax.experimental import pallas as pl
from jax.experimental.pallas import tpu as pltpu
from jax.sharding import PartitionSpec as P

HD = 128
UNIT = 128
MOST_UNITS = 14
SPAN = 16 * MOST_UNITS
TAIL = 8
BLOCK = 256
epsilon = 1e-05
RATE = math.log2(math.e) / math.sqrt(HD)
MIB = 1 << 20


def split(x, count=3):
    pieces = []
    for _ in range(count):
        piece = x.astype(jnp.bfloat16)
        pieces.append(piece)
        x = x - piece.astype(jnp.float32)
    return pieces


def put_message(out, block, tail):
    out[0:SPAN, :] = block.astype(jnp.bfloat16)
    row = lax.broadcasted_iota(jnp.int32, (16, tail.shape[1]), 0)
    packed = jnp.zeros(row.shape, jnp.float32)
    for n, piece in enumerate(split(jnp.concatenate([tail, tail], axis=0))):
        packed = jnp.where(row // 4 == n, piece.astype(jnp.float32), packed)
    out[SPAN : SPAN + 16, :] = packed.astype(jnp.bfloat16)


def message_tail(message):
    pieces = message[SPAN : SPAN + 16, :].astype(jnp.float32)
    tail = pieces[:8] + pieces[8:]
    return tail + jnp.concatenate([tail[4:], tail[:4]], axis=0)


def affine_kernel(counts, hidden, gain, bias, key_weight, value_weight, *outs):
    row = lax.broadcasted_iota(jnp.int32, (16, gain.shape[0]), 0) % 4
    affine = jnp.where(
        row == 2, gain[...][None, :], jnp.where(row == 3, bias[...][None, :], 0.0)
    )
    affine = jnp.concatenate(split(affine), axis=0)
    sums = []
    for weight in (key_weight, value_weight):
        total = jnp.dot(affine, weight[...], preferred_element_type=jnp.float32)
        sums.append(sum(total[16 * n : 16 * n + TAIL] for n in range(3)))
    own_is_first = lax.rem(lax.axis_index("store"), 2) == 0
    outs[0][...] = jnp.where(own_is_first, sums[0], sums[1])
    outs[1][...] = jnp.where(own_is_first, sums[1], sums[0])


def project_affine(counts, hidden, gain, bias, key_weight, value_weight):
    width, cols = key_weight.shape
    vmem = pl.BlockSpec(memory_space=pltpu.VMEM)
    return pl.pallas_call(
        affine_kernel,
        out_shape=[jax.ShapeDtypeStruct((TAIL, cols), jnp.float32)] * 2,
        in_specs=[pl.BlockSpec(memory_space=pltpu.SMEM)] + [vmem] * 5,
        out_specs=[vmem] * 2,
        compiler_params=pltpu.CompilerParams(vmem_limit_bytes=32 * MIB),
        cost_estimate=pl.CostEstimate(
            flops=4 * 48 * width * cols, bytes_accessed=6 * MIB, transcendentals=0
        ),
    )(counts, hidden, gain, bias, key_weight, value_weight)


def projection_kernel(plan, counts, hidden, hidden_other, gain, *rest):
    opening = len(plan) == 2
    given, affine_sums = rest[:2], rest[2:4]
    outs, (rows_in, weights) = list(rest[4:-2]), rest[-2:]
    store = lax.axis_index("store")
    me = lax.axis_index("req")
    core = lax.rem(store, 2)
    first_count = counts[store - core]
    units = (first_count + counts[store - core + 1]) // UNIT
    low = store < 2
    capacity, width = hidden.shape
    cols = weights.shape[2]
    own_is_first = core == 0

    @pl.when(own_is_first)
    def _():
        weights[0] = given[0][...]
        weights[1] = given[1][...]

    @pl.when(jnp.logical_not(own_is_first))
    def _():
        weights[0] = given[1][...]
        weights[1] = given[0][...]

    tail_row = lax.broadcasted_iota(jnp.int32, (TAIL, cols), 0)
    lane = lax.broadcasted_iota(jnp.int32, (SPAN, 128), 1)
    fill = jnp.zeros((256 - SPAN, 128), jnp.float32)
    gains = gain[...][None, :]
    for step, sides in plan:
        target = lax.rem(me + jnp.where(own_is_first, step, 8 - step), 8)
        base = target * units - jnp.where(low, 0, MOST_UNITS - units)
        for g in range(MOST_UNITS):
            row = (base + g) * 16
            in_first = row < first_count
            at = jnp.where(in_first, row, row - first_count)
            at = pl.multiple_of(jnp.clip(at, 0, capacity - 16), 16)
            from_own = in_first == own_is_first
            rows_in[pl.ds(g * 16, 16), :] = jnp.where(
                from_own, hidden[pl.ds(at, 16), :], hidden_other[pl.ds(at, 16), :]
            )
        wide = rows_in[...].astype(jnp.float32)
        row_sum = jnp.sum(wide, axis=1, keepdims=True)
        row_square = jnp.sum(wide * wide, axis=1, keepdims=True)
        centre = row_sum * (1.0 / width)
        left = ((wide - centre) * gains).astype(jnp.bfloat16)
        moments = jnp.concatenate(
            [jnp.where(lane == 0, row_sum, jnp.where(lane == 1, row_square, 0.0)), fill], axis=0
        )
        moments = jnp.concatenate(
            [jnp.transpose(moments[:128])[:TAIL], jnp.transpose(moments[128:])[:TAIL]], axis=1
        )
        moments = jnp.concatenate(
            [moments, jnp.zeros((TAIL, cols - 256), jnp.float32)], axis=1
        )
        for side in sides:
            out = outs.pop(0)
            affine_sum = affine_sums[side][...]
            block = (
                jnp.dot(left, weights[side], preferred_element_type=jnp.float32)
                + centre * affine_sum[2:3]
            )
            tail = jnp.where(tail_row % 4 < 2, moments, affine_sum)
            if opening:
                put_message(out, block, tail)
            else:
                out[0:SPAN, :] = block
                out[SPAN : SPAN + TAIL, :] = tail


def project_rows(plan, counts, *operands):
    capacity, width = operands[0].shape
    cols = operands[3].shape[1]
    vmem = pl.BlockSpec(memory_space=pltpu.VMEM)
    pieces = sum(len(sides) for _, sides in plan)
    if len(plan) == 2:
        outs = [jax.ShapeDtypeStruct((SPAN + 16, cols), jnp.bfloat16)] * pieces
    else:
        outs = [jax.ShapeDtypeStruct((SPAN + TAIL, cols), jnp.float32)] * pieces
    return pl.pallas_call(
        functools.partial(projection_kernel, plan),
        out_shape=outs,
        in_specs=[pl.BlockSpec(memory_space=pltpu.SMEM)] + [vmem] * len(operands),
        out_specs=[vmem] * len(outs),
        scratch_shapes=[
            pltpu.VMEM((SPAN, width), jnp.bfloat16),
            pltpu.VMEM((2, width, cols), jnp.bfloat16),
        ],
        compiler_params=pltpu.CompilerParams(vmem_limit_bytes=32 * MIB),
        cost_estimate=pl.CostEstimate(
            flops=pieces * SPAN * width * 2 * cols, bytes_accessed=4 * MIB, transcendentals=0
        ),
    )(counts, *operands)


def finish_kernel(depth, block, ours, theirs, out):
    total = block[0:SPAN, :]
    tail = block[SPAN : SPAN + TAIL, :]
    for message in (ours, theirs):
        total = total + message[0:SPAN, :].astype(jnp.float32)
        tail = tail + message_tail(message)
    fill = jnp.zeros((128 - TAIL, 128), jnp.float32)
    columns = jnp.concatenate(
        [
            jnp.transpose(jnp.concatenate([tail[:, at : at + 128], fill], axis=0))
            for at in (0, 128)
        ],
        axis=0,
    )[:SPAN]
    mean = columns[:, 0:1] / depth
    var = columns[:, 1:2] / depth - mean * mean
    out[...] = ((total - mean * tail[2:3]) * lax.rsqrt(var + epsilon) + tail[3:4]).astype(
        jnp.bfloat16
    )


def finish(block, ours, theirs, depth):
    vmem = pl.BlockSpec(memory_space=pltpu.VMEM)
    return pl.pallas_call(
        functools.partial(finish_kernel, depth),
        out_shape=jax.ShapeDtypeStruct((SPAN, block.shape[1]), jnp.bfloat16),
        in_specs=[vmem] * 3,
        out_specs=vmem,
        compiler_params=pltpu.CompilerParams(vmem_limit_bytes=16 * MIB),
        cost_estimate=pl.CostEstimate(
            flops=4 * SPAN * block.shape[1], bytes_accessed=2 * MIB, transcendentals=SPAN
        ),
    )(block, ours, theirs)


def merge_kernel(counts, rows, rows_far, out):
    low = lax.axis_index("store") < 2
    live = (counts[0] + counts[1]) // 8
    lower = jnp.where(low, rows[...], rows_far[...])
    higher = jnp.where(low, rows_far[...], rows[...])
    edge = BLOCK - SPAN
    place = lax.broadcasted_iota(jnp.int32, (SPAN - edge, rows.shape[1]), 0) + edge
    out[0:edge, :] = lower[:edge]
    out[edge:SPAN, :] = jnp.where(
        place < live, lower[edge:].astype(jnp.float32), higher[: SPAN - edge].astype(jnp.float32)
    ).astype(jnp.bfloat16)
    out[SPAN:BLOCK, :] = higher[SPAN - edge :]


def merge(counts, rows, rows_far):
    vmem = pl.BlockSpec(memory_space=pltpu.VMEM)
    return pl.pallas_call(
        merge_kernel,
        out_shape=jax.ShapeDtypeStruct((BLOCK, rows.shape[1]), jnp.bfloat16),
        in_specs=[pl.BlockSpec(memory_space=pltpu.SMEM)] + [vmem] * 2,
        out_specs=vmem,
        compiler_params=pltpu.CompilerParams(vmem_limit_bytes=16 * MIB),
        cost_estimate=pl.CostEstimate(
            flops=BLOCK * rows.shape[1], bytes_accessed=MIB, transcendentals=0
        ),
    )(counts, rows, rows_far)


def relay_kernel(received, block, out):
    put_message(
        out,
        received[0:SPAN, :].astype(jnp.float32) + block[0:SPAN, :],
        message_tail(received) + block[SPAN : SPAN + TAIL, :],
    )


def relay(received, block):
    vmem = pl.BlockSpec(memory_space=pltpu.VMEM)
    return pl.pallas_call(
        relay_kernel,
        out_shape=jax.ShapeDtypeStruct(received.shape, received.dtype),
        in_specs=[vmem] * 2,
        out_specs=vmem,
        compiler_params=pltpu.CompilerParams(vmem_limit_bytes=16 * MIB),
        cost_estimate=pl.CostEstimate(
            flops=2 * SPAN * block.shape[1], bytes_accessed=2 * MIB, transcendentals=0
        ),
    )(received, block)


def pack_shift(top):
    rows = top.shape[0]
    lane = lax.broadcasted_iota(jnp.int32, (rows, HD), 1)
    left = -jnp.broadcast_to(top, (rows, HD))
    packed = jnp.zeros((rows, HD), jnp.float32)
    for i, piece in enumerate(split(left)):
        packed = jnp.where(lane == i, piece.astype(jnp.float32), packed)
    return packed.astype(jnp.bfloat16)


def own_kernel(q, own_k, own_v, out, shift):
    requests, positions, width = q.shape
    row = lax.broadcasted_iota(jnp.int32, (positions, positions), 0)
    column = lax.broadcasted_iota(jnp.int32, (positions, positions), 1)
    ones = jnp.ones((positions, HD), jnp.bfloat16)
    for head in range(width // HD):
        columns = slice(head * HD, (head + 1) * HD)
        for r in range(requests):
            at = r * positions
            scores = lax.dot_general(
                q[r, :, columns],
                own_k[r, :, columns],
                (((1,), (1,)), ((), ())),
                preferred_element_type=jnp.float32,
            )
            scores = jnp.where(column <= row, scores, -jnp.inf)
            top = jnp.max(scores, axis=1, keepdims=True)
            weights = jnp.exp2((scores - top) * RATE).astype(jnp.bfloat16)
            both = jnp.concatenate([own_v[r, :, columns], ones], axis=1)
            out[head, at : at + positions, :] = jnp.dot(
                weights, both, preferred_element_type=jnp.float32
            )
            shift[head, at : at + positions, :] = pack_shift(top)


def stage_kernel(end, pair_count, *refs):
    refs = list(refs)
    lengths = refs.pop(0) if end else None
    q, state, shift = refs[:3]
    blocks = refs[3 : 3 + 4 * pair_count]
    outs = refs[3 + 4 * pair_count :]
    requests, positions, width = q.shape
    rows = requests * positions
    heads = width // HD
    first_core = lax.rem(lax.axis_index("store"), 2) == 0
    ones = jnp.ones((BLOCK * pair_count, HD), jnp.bfloat16)

    def pick(first, columns):
        return jnp.concatenate(
            [
                jnp.where(first_core, blocks[i][:, columns], blocks[i + 1][:, columns])
                for i in range(first, 4 * pair_count, 4)
            ],
            axis=0,
        )

    def shifted_scores(head, columns):
        queries = jnp.concatenate([q[:, :, columns].reshape(rows, HD), shift[head]], axis=1)
        keys = jnp.concatenate([pick(0, columns), ones], axis=1)
        return lax.dot_general(
            queries, keys, (((1,), (1,)), ((), ())), preferred_element_type=jnp.float32
        )

    def weigh(scores, columns):
        weights = jnp.exp2(scores * RATE).astype(jnp.bfloat16)
        values = jnp.concatenate([pick(2, columns), ones], axis=1)
        return jnp.dot(weights, values, preferred_element_type=jnp.float32)

    def emit(head, columns, total, packed):
        if end:
            result = total[:, :HD] / total[:, HD:]
            place = lax.broadcasted_iota(jnp.int32, (positions, HD), 0)
            for r in range(requests):
                part = result[r * positions : (r + 1) * positions]
                outs[0][r, :, columns] = jnp.where(place < lengths[r], part, 0.0).astype(
                    jnp.bfloat16
                )
        else:
            outs[0][head] = total
            outs[1][head] = packed

    largest = jnp.zeros((8, HD), jnp.float32)
    for head in range(heads):
        columns = slice(head * HD, (head + 1) * HD)
        total = state[head] + weigh(shifted_scores(head, columns), columns)
        emit(head, columns, total, shift[head])
        largest = jnp.maximum(
            largest, jnp.max(total[:, HD:].reshape(rows // 8, 8, HD), axis=0)
        )

    @pl.when(jnp.logical_not(jnp.max(largest) < 1e30))
    def _():
        def one_head(head, carry):
            columns = pl.ds(pl.multiple_of(head * HD, HD), HD)
            scores = shifted_scores(head, columns)
            old = -jnp.sum(shift[head].astype(jnp.float32), axis=1, keepdims=True)
            new = old + jnp.maximum(jnp.max(scores, axis=1, keepdims=True), 0.0)
            moved = new - old
            total = state[head] * jnp.exp2(-moved * RATE) + weigh(scores - moved, columns)
            emit(head, columns, total, pack_shift(new))
            return carry

        lax.fori_loop(0, heads, one_head, 0)


def attend_own(q, k, v):
    requests, positions, width = q.shape
    rows = requests * positions
    heads = width // HD
    vmem = pl.BlockSpec(memory_space=pltpu.VMEM)
    return pl.pallas_call(
        own_kernel,
        out_shape=[
            jax.ShapeDtypeStruct((heads, rows, 2 * HD), jnp.float32),
            jax.ShapeDtypeStruct((heads, rows, HD), jnp.bfloat16),
        ],
        in_specs=[vmem] * 3,
        out_specs=[vmem] * 2,
        compiler_params=pltpu.CompilerParams(vmem_limit_bytes=32 * MIB),
        cost_estimate=pl.CostEstimate(
            flops=4 * rows * positions * width,
            bytes_accessed=6 * MIB,
            transcendentals=rows * positions * heads,
        ),
    )(q, k, v)


def attend(q, state, pairs, lengths=None):
    requests, positions, width = q.shape
    rows = requests * positions
    vmem = pl.BlockSpec(memory_space=pltpu.VMEM)
    operands = [q, *state] + [array for pair in pairs for array in pair]
    specs = [vmem] * len(operands)
    if lengths is not None:
        specs = [pl.BlockSpec(memory_space=pltpu.SMEM)] + specs
        operands = [lengths] + operands
        out_shape, out_specs = jax.ShapeDtypeStruct(q.shape, jnp.bfloat16), vmem
    else:
        out_shape = [jax.ShapeDtypeStruct(array.shape, array.dtype) for array in state]
        out_specs = [vmem] * 2
    key_rows = BLOCK * len(pairs)
    return pl.pallas_call(
        functools.partial(stage_kernel, lengths is not None, len(pairs)),
        out_shape=out_shape,
        in_specs=specs,
        out_specs=out_specs,
        compiler_params=pltpu.CompilerParams(vmem_limit_bytes=32 * MIB),
        cost_estimate=pl.CostEstimate(
            flops=4 * rows * key_rows * width,
            bytes_accessed=8 * MIB,
            transcendentals=rows * key_rows * width // HD,
        ),
    )(*operands)


def per_device(
    hidden,
    row_counts,
    ln_gain,
    ln_bias,
    key_weight,
    value_weight,
    suffix_q,
    suffix_k,
    suffix_v,
    suffix_lengths,
):
    store = lax.axis_index("store")
    stores = lax.axis_size("store")
    ring = lax.axis_size("req")
    depth = ring * key_weight.shape[0]
    around = [
        (s * ring + z, s * ring + (z + (1 if s % 2 == 0 else ring - 1)) % ring)
        for s in range(stores)
        for z in range(ring)
    ]
    across = [(s, s + 1 - 2 * (s % 2)) for s in range(stores)]
    far = [(s, (s + 2) % 4) for s in range(stores)]

    def step(array):
        return lax.ppermute(array, ("store", "req"), around)

    def swap(array):
        return lax.ppermute(array, "store", across)

    other_hidden = swap(hidden)
    weights = (key_weight, value_weight)
    affine = project_affine(row_counts, hidden, ln_gain, ln_bias, *weights)
    inputs = (row_counts, hidden, other_hidden, ln_gain, *weights, *affine)
    total, rest = project_rows(((4, (0,)), (3, (1,))), *inputs)
    f1, f2, s2, f3, s3, f4 = project_rows(
        ((3, (0,)), (2, (0, 1)), (1, (0, 1)), (0, (0,))), *inputs
    )

    total = relay(step(total), f1)
    rest = relay(step(rest), s2)
    total = relay(step(total), f2)
    rest = relay(step(rest), s3)
    state = attend_own(suffix_q, suffix_k, suffix_v)
    total = step(total)
    total, state = lax.optimization_barrier((total, state))
    total = step(relay(total, f3))
    rows = finish(f4, total, swap(step(rest)), depth)

    mine = merge(row_counts, rows, lax.ppermute(rows, "store", far))

    other = swap(mine)
    g1 = step(mine)
    h1 = step(other)
    xg1 = swap(g1)
    g2 = step(g1)
    xh1 = swap(h1)
    h2 = step(h1)
    xg2 = swap(g2)
    xh2 = swap(h2)
    g3 = step(g2)

    def upper(g, xg, h, xh):
        return (g, xg, h, xh)

    def lower(g, xg, h, xh):
        return (xh, h, xg, g)

    h2, state = lax.optimization_barrier((h2, state))
    h3 = step(h2)
    near = (g1, xg1, h1, xh1)
    state = attend(
        suffix_q, state, [(mine, other, other, mine), upper(*near), lower(*near)]
    )
    g3, state = lax.optimization_barrier((g3, state))
    xg3 = swap(g3)
    g4 = step(g3)
    h3, state = lax.optimization_barrier((h3, state))
    xh3 = swap(h3)
    near = (g2, xg2, h2, xh2)
    state = attend(suffix_q, state, [upper(*near), lower(*near)])
    near = (g3, xg3, h3, xh3)
    state = attend(suffix_q, state, [upper(*near), lower(*near)])
    g4, state = lax.optimization_barrier((g4, state))
    xg4 = swap(g4)
    return attend(suffix_q, state, [(g4, xg4, xg4, g4)], lengths=suffix_lengths)


def solution(mesh):
    in_specs = (
        P("store", "req"),
        P(),
        P("req"),
        P("req"),
        P("req", "tp"),
        P("req", "tp"),
        P(("store", "req"), None, "tp"),
        P(("store", "req"), None, "tp"),
        P(("store", "req"), None, "tp"),
        P(("store", "req")),
    )
    out_specs = P(("store", "req"), None, "tp")
    return jax.shard_map(
        per_device, mesh=mesh, in_specs=in_specs, out_specs=out_specs, check_vma=False
    )
```

time: 128 us -> 99.3 us (0.78)
  Pallas kernels: 36.2 us -> 22.7 us
  waiting for transfers between devices: 34.1 us -> 22.8 us
  other arithmetic: 5.16 us -> 0 us
  local copies, waits for them, and re-layouts: 5.49 us -> 7.2 us
  between operations: 1.6 us -> 0.2 us
    ppermute x14, waiting for transfers between devices: 27.1 us -> 15.7 us  [step(): return lax.ppermute(array, ('store', 'req'), around)]
    pallas_call x4, Pallas kernels: 18.7 us -> 8.78 us  [attend(): pl.pallas_call(functools.partial(stage_kernel, lengths is not None, len(p...]
    unnamed x26, local copies, waits for them, and re-layouts: 2.25 us -> 7.2 us
    ppermute x14, starting transfers between devices: 30.3 us -> 25.4 us  [step(): return lax.ppermute(array, ('store', 'req'), around)]
    ppermute x10, starting transfers between devices: 13.1 us -> 17.8 us  [swap(): return lax.ppermute(array, 'store', across)]
    pallas_call x2 -> x11, Pallas kernels: 17.5 us -> 13.9 us  [the longest x2 6.44 us: project_rows(): pl.pallas_call(functools.partial(projection_kernel, plan), out_shape=outs...]
    add x6 -> x0, other arithmetic: 2.73 us -> none  [the longest x1 1.19 us: per_device(): rest = step(second[0]) + second[1]]
    broadcast_in_dim x2 -> x0, local copies, waits for them, and re-layouts: 2.58 us -> none  [the longest x1 1.29 us: per_device(): ln_gain[None, :]]
  transfers between devices with their start and end apart: 25 -> 25, of which waited for: 12 -> 11; matrix products, arithmetic and copies ran while one was open for 5% -> 0% of each run, Pallas kernels for 16% -> 17%
where the time goes in v3:
time: 99.3 us; the launch traced here: 99 us
  starting transfers between devices  46.2 us (47%)
  waiting for transfers between devices  22.8 us (23%)
  Pallas kernels  22.7 us (23%)
  local copies, waits for them, and re-layouts  7.2 us (7%)
    ppermute x14, starting transfers between devices, step(): return lax.ppermute(array, ('store', 'req'), around)  25.4 us
    ppermute x10, starting transfers between devices, swap(): return lax.ppermute(array, 'store', across)  17.8 us
    ppermute x14, waiting for transfers between devices, step(): return lax.ppermute(array, ('store', 'req'), around)  15.7 us
    pallas_call x4, Pallas kernels, attend(): pl.pallas_call(functools.partial(stage_kernel, lengths is not None, len(p...  8.78 us
    unnamed x26, local copies, waits for them, and re-layouts  7.2 us
    pallas_call x2, Pallas kernels, project_rows(): pl.pallas_call(functools.partial(projection_kernel, plan), out_shape=outs...  6.44 us
    ppermute x1, waiting for transfers between devices, per_device(): mine = merge(row_counts, rows, lax.ppermute(rows, 'store', far))  5.46 us
    pallas_call x1, Pallas kernels, attend_own(): pl.pallas_call(own_kernel, out_shape=[jax.ShapeDtypeStruct((heads, rows,...  4.92 us
  transfers between devices with their start and end apart: 25, of which 11 were waited for; matrix products, arithmetic and copies ran while one was open for 0% of the time, Pallas kernels for 17%

profile of v3, /device:TPU:1, one launch (start us, length us, event | category | flops | bytes accessed | tf_op | source)
XLA Modules:
  0.0 99.0 jit_solution(16774617495451264849)
XLA Ops:
  0.0 3.2 %collective-permute-start = (bf16[1024,1152]{1,0:T(8,128)(2,1)}, bf16[1024,1152]{1,0:T(8,128)(2,1)S(1)}, u32[]{:S(2)}, u32[]{:S(2)}) collective-permute-start(bf16[1024,1152]{1,0:T(8,128)(2,1)} %hidden.5), channel_id=1, source_target_pairs={{0,64},{64,0},{128,192},{192,128},{1,65},{65,1},{129,193},{193,129... | collective-permute-start | bytes 7077896 | tf_op jit(solution)/shard_map/ppermute | solution.py:438
  3.2 1.7 %copy-done = bf16[1024,1152]{1,0:T(8,128)(2,1)S(1)} copy-done((bf16[1024,1152]{1,0:T(8,128)(2,1)S(1)}, bf16[1024,1152]{1,0:T(8,128)(2,1)}, u32[]{:S(2)}) %copy-start) | copy-done | bytes 2359320
  4.9 1.4 %copy-done.2 = bf16[1152,640]{1,0:T(8,128)(2,1)S(1)} copy-done((bf16[1152,640]{1,0:T(8,128)(2,1)S(1)}, bf16[1152,640]{1,0:T(8,128)(2,1)}, u32[]{:S(2)}) %copy-start.2) | copy-done | bytes 1474584
  6.3 1.4 %copy-done.4 = bf16[1152,640]{1,0:T(8,128)(2,1)S(1)} copy-done((bf16[1152,640]{1,0:T(8,128)(2,1)S(1)}, bf16[1152,640]{1,0:T(8,128)(2,1)}, u32[]{:S(2)}) %copy-start.4) | copy-done | bytes 1474584
  7.7 0.7 copy-done.8
  8.4 0.7 copy-done.9
  9.1 0.7 copy-done.10
  9.7 1.1 %shard_map.100 = (f32[8,640]{1,0:T(8,128)S(1)}, f32[8,640]{1,0:T(8,128)S(1)}) custom-call(s32[4]{0:T(128)S(1)} %copy-done.10, bf16[1024,1152]{1,0:T(8,128)(2,1)S(1)} %copy-done, f32[1152]{0:T(1024)S(1)} %copy-done.8, f32[1152]{0:T(1024)S(1)} %copy-done.9, bf16[1152,640]{1,0:T(8,128)(2,1)S(1)} %copy-done.2, bf16[1152,640]{1,0:T(8,128)(2,1)S(1)} %copy-done.4), custom_call_target="tpu_custom_call" | custom-call | flops 141557760 | bytes 6291456 | tf_op jit(solution)/shard_map/pallas_call | solution.py:64
  10.8 0.3 copy-done.3
  11.1 0.4 copy-done.5
  11.5 2.2 %shard_map.102 = (bf16[240,640]{1,0:T(8,128)(2,1)S(1)}, bf16[240,640]{1,0:T(8,128)(2,1)S(1)}) custom-call(s32[4]{0:T(128)S(1)} %copy-done.10, bf16[1024,1152]{1,0:T(8,128)(2,1)S(1)} %copy-done, bf16[1024,1152]{1,0:T(8,128)(2,1)S(1)} %collective-permute-done.hidden_other, f32[1152]{0:T(1024)S(1)} %copy-done.8, bf16[1152,640]{1,0:T(8,128)(2,1)S(1)} %copy-done.3, ...), custom_call_target="tpu_custom_call" | custom-call | flops 660602880 | bytes 4194304 | tf_op jit(solution)/shard_map/pallas_call | solution.py:154
  13.7 3.9 %collective-permute-start.1 = (bf16[240,640]{1,0:T(8,128)(2,1)S(1)}, bf16[240,640]{1,0:T(8,128)(2,1)S(1)}, u32[]{:S(2)}, u32[]{:S(2)}) collective-permute-start(bf16[240,640]{1,0:T(8,128)(2,1)S(1)} %get-tuple-element.41), channel_id=1, source_target_pairs={{0,8},{8,16},{16,24},{24,32},{32,40},{40,48},{48,56},{56,0},{64,12... | collective-permute-start | bytes 921608 | tf_op jit(solution)/shard_map/ppermute | solution.py:435
  17.6 0.7 collective-permute-start.5
  18.4 4.3 %shard_map.101 = (f32[232,640]{1,0:T(8,128)S(1)}, f32[232,640]{1,0:T(8,128)S(1)}, f32[232,640]{1,0:T(8,128)S(1)}, f32[232,640]{1,0:T(8,128)S(1)}, f32[232,640]{1,0:T(8,128)S(1)}, /*index=5*/f32[232,640]{1,0:T(8,128)S(1)}) custom-call(s32[4]{0:T(128)S(1)} %copy-done.10, bf16[1024,1152]{1,0:T(8,128)(2,1)S(1)} %copy-done, ...), custom_call_target="tpu_custom_call" | custom-call | flops 1981808640 | bytes 4194304 | tf_op jit(solution)/shard_map/pallas_call | solution.py:154
  22.6 0.0 copy-start.1
  22.6 0.0 copy-start.6
  22.6 0.0 copy-start.7
  22.7 0.1 shard_map.103
  22.7 1.9 %collective-permute-start.2 = (bf16[240,640]{1,0:T(8,128)(2,1)S(1)}, bf16[240,640]{1,0:T(8,128)(2,1)S(1)}, u32[]{:S(2)}, u32[]{:S(2)}) collective-permute-start(bf16[240,640]{1,0:T(8,128)(2,1)S(1)} %shard_map.103), channel_id=1, source_target_pairs={{0,8},{8,16},{16,24},{24,32},{32,40},{40,48},{48,56},{56,0},{64,12... | collective-permute-start | bytes 921608 | tf_op jit(solution)/shard_map/ppermute | solution.py:435
  24.7 0.0 collective-permute-done.5.received
  24.7 0.1 shard_map.107
  24.8 3.2 %collective-permute-start.6 = (bf16[240,640]{1,0:T(8,128)(2,1)S(1)}, bf16[240,640]{1,0:T(8,128)(2,1)S(1)}, u32[]{:S(2)}, u32[]{:S(2)}) collective-permute-start(bf16[240,640]{1,0:T(8,128)(2,1)S(1)} %shard_map.107), channel_id=1, source_target_pairs={{0,8},{8,16},{16,24},{24,32},{32,40},{40,48},{48,56},{56,0},{64,12... | collective-permute-start | bytes 921608 | tf_op jit(solution)/shard_map/ppermute | solution.py:435
  28.0 0.8 collective-permute-done.2.received
  28.8 0.1 shard_map.104
  28.9 2.9 %collective-permute-start.3 = (bf16[240,640]{1,0:T(8,128)(2,1)S(1)}, bf16[240,640]{1,0:T(8,128)(2,1)S(1)}, u32[]{:S(2)}, u32[]{:S(2)}) collective-permute-start(bf16[240,640]{1,0:T(8,128)(2,1)S(1)} %shard_map.104), channel_id=1, source_target_pairs={{0,8},{8,16},{16,24},{24,32},{32,40},{40,48},{48,56},{56,0},{64,12... | collective-permute-start | bytes 921608 | tf_op jit(solution)/shard_map/ppermute | solution.py:435
  31.8 0.3 collective-permute-done.6.received
  32.1 0.1 shard_map.108
  32.2 0.0 copy-start.11
  32.2 3.1 %collective-permute-start.7 = (bf16[240,640]{1,0:T(8,128)(2,1)S(1)}, bf16[240,640]{1,0:T(8,128)(2,1)S(1)}, u32[]{:S(2)}, u32[]{:S(2)}) collective-permute-start(bf16[240,640]{1,0:T(8,128)(2,1)S(1)} %shard_map.108), channel_id=1, source_target_pairs={{0,8},{8,16},{16,24},{24,32},{32,40},{40,48},{48,56},{56,0},{64,12... | collective-permute-start | bytes 921608 | tf_op jit(solution)/shard_map/ppermute | solution.py:435
  35.3 4.9 %shard_map.105 = (f32[5,512,256]{2,1,0:T(8,128)S(1)}, bf16[5,512,128]{2,1,0:T(8,128)(2,1)S(1)}) custom-call(bf16[4,128,640]{2,1,0:T(8,128)(2,1)S(1)} %copy-done.1, bf16[4,128,640]{2,1,0:T(8,128)(2,1)S(1)} %copy-done.6, bf16[4,128,640]{2,1,0:T(8,128)(2,1)S(1)} %copy-done.7), custom_call_target="tpu_custom_call" | custom-call | flops 167772160 | bytes 6291456 | tf_op jit(solution)/shard_map/pallas_call | solution.py:365
  40.2 0.1 shard_map.106
  40.3 0.1 collective-permute-start.4
  40.4 2.3 %collective-permute-start.8 = (bf16[240,640]{1,0:T(8,128)(2,1)S(1)}, bf16[240,640]{1,0:T(8,128)(2,1)S(1)}, u32[]{:S(2)}, u32[]{:S(2)}) collective-permute-start(bf16[240,640]{1,0:T(8,128)(2,1)S(1)} %collective-permute-done.7), channel_id=1, source_target_pairs={{0,64},{64,0},{128,192},{192,128},{1,65},{65,1},{129,193},{193,129... | collective-permute-start | bytes 921608 | tf_op jit(solution)/shard_map/ppermute | solution.py:438
  42.7 3.7 %collective-permute-done.4.ours = bf16[240,640]{1,0:T(8,128)(2,1)S(1)} collective-permute-done((bf16[240,640]{1,0:T(8,128)(2,1)S(1)}, bf16[240,640]{1,0:T(8,128)(2,1)S(1)}, u32[]{:S(2)}, u32[]{:S(2)}) %collective-permute-start.4) | collective-permute-done | bytes 307232 | tf_op jit(solution)/shard_map/ppermute | solution.py:435
  46.4 0.4 shard_map.109.rows
  46.8 3.0 %collective-permute-start.9 = (bf16[224,640]{1,0:T(8,128)(2,1)S(1)}, bf16[224,640]{1,0:T(8,128)(2,1)S(1)}, u32[]{:S(2)}, u32[]{:S(2)}) collective-permute-start(bf16[224,640]{1,0:T(8,128)(2,1)S(1)} %shard_map.109.rows), channel_id=1, source_target_pairs={{0,128},{64,192},{128,0},{192,64},{1,129},{65,193},{129,1},{193,65... | collective-permute-start | bytes 860168 | tf_op jit(solution)/shard_map/ppermute | solution.py:459
  49.8 5.5 %collective-permute-done.9.rows_far = bf16[224,640]{1,0:T(8,128)(2,1)S(1)} collective-permute-done((bf16[224,640]{1,0:T(8,128)(2,1)S(1)}, bf16[224,640]{1,0:T(8,128)(2,1)S(1)}, u32[]{:S(2)}, u32[]{:S(2)}) %collective-permute-start.9) | collective-permute-done | bytes 286752 | tf_op jit(solution)/shard_map/ppermute | solution.py:459
  55.2 0.6 shard_map.110.refs_3_.refs_6_
  55.9 2.5 %collective-permute-start.13 = (bf16[256,640]{1,0:T(8,128)(2,1)S(1)}, bf16[256,640]{1,0:T(8,128)(2,1)S(1)}, u32[]{:S(2)}, u32[]{:S(2)}) collective-permute-start(bf16[256,640]{1,0:T(8,128)(2,1)S(1)} %shard_map.110.refs_3_.refs_6_), channel_id=1, source_target_pairs={{0,64},{64,0},{128,192},{192,128},{1,65},{65,1},{129,193},{193,129... | collective-permute-start | bytes 983048 | tf_op jit(solution)/shard_map/ppermute | solution.py:438
  58.4 0.9 collective-permute-start.10
  59.3 0.3 collective-permute-done.13.refs_4_.refs_5_
  59.6 0.9 collective-permute-start.14
  60.6 4.0 %collective-permute-done.10.refs_7_.refs_14_ = bf16[256,640]{1,0:T(8,128)(2,1)S(1)} collective-permute-done((bf16[256,640]{1,0:T(8,128)(2,1)S(1)}, bf16[256,640]{1,0:T(8,128)(2,1)S(1)}, u32[]{:S(2)}, u32[]{:S(2)}) %collective-permute-start.10) | collective-permute-done | bytes 327712 | tf_op jit(solution)/shard_map/ppermute | solution.py:435
  64.6 1.9 %collective-permute-start.11 = (bf16[256,640]{1,0:T(8,128)(2,1)S(1)}, bf16[256,640]{1,0:T(8,128)(2,1)S(1)}, u32[]{:S(2)}, u32[]{:S(2)}) collective-permute-start(bf16[256,640]{1,0:T(8,128)(2,1)S(1)} %collective-permute-done.10.refs_7_.refs_14_), channel_id=1, source_target_pairs={{0,8},{8,16},{16,24},{24,32},{32,40},{40,48},{48,56},{56,0},{64,12... | collective-permute-start | bytes 983048 | tf_op jit(solution)/shard_map/ppermute | solution.py:435
  66.4 1.6 %collective-permute-done.14.refs_9_.refs_12_ = bf16[256,640]{1,0:T(8,128)(2,1)S(1)} collective-permute-done((bf16[256,640]{1,0:T(8,128)(2,1)S(1)}, bf16[256,640]{1,0:T(8,128)(2,1)S(1)}, u32[]{:S(2)}, u32[]{:S(2)}) %collective-permute-start.14) | collective-permute-done | bytes 327712 | tf_op jit(solution)/shard_map/ppermute | solution.py:435
  68.1 1.9 %collective-permute-start.15 = (bf16[256,640]{1,0:T(8,128)(2,1)S(1)}, bf16[256,640]{1,0:T(8,128)(2,1)S(1)}, u32[]{:S(2)}, u32[]{:S(2)}) collective-permute-start(bf16[256,640]{1,0:T(8,128)(2,1)S(1)} %collective-permute-done.14.refs_9_.refs_12_), channel_id=1, source_target_pairs={{0,8},{8,16},{16,24},{24,32},{32,40},{40,48},{48,56},{56,0},{64,12... | collective-permute-start | bytes 983048 | tf_op jit(solution)/shard_map/ppermute | solution.py:435
  70.0 0.3 collective-permute-start.16
  70.3 0.2 collective-permute-start.17
  70.5 1.1 %collective-permute-done.11.refs_3_.refs_10_ = bf16[256,640]{1,0:T(8,128)(2,1)S(1)} collective-permute-done((bf16[256,640]{1,0:T(8,128)(2,1)S(1)}, bf16[256,640]{1,0:T(8,128)(2,1)S(1)}, u32[]{:S(2)}, u32[]{:S(2)}) %collective-permute-start.11) | collective-permute-done | bytes 327712 | tf_op jit(solution)/shard_map/ppermute | solution.py:435
  71.6 2.0 %collective-permute-start.12 = (bf16[256,640]{1,0:T(8,128)(2,1)S(1)}, bf16[256,640]{1,0:T(8,128)(2,1)S(1)}, u32[]{:S(2)}, u32[]{:S(2)}) collective-permute-start(bf16[256,640]{1,0:T(8,128)(2,1)S(1)} %collective-permute-done.11.refs_3_.refs_10_), channel_id=1, source_target_pairs={{0,8},{8,16},{16,24},{24,32},{32,40},{40,48},{48,56},{56,0},{64,12... | collective-permute-start | bytes 983048 | tf_op jit(solution)/shard_map/ppermute | solution.py:435
  73.6 1.5 %collective-permute-done.15.refs_5_.refs_8_ = bf16[256,640]{1,0:T(8,128)(2,1)S(1)} collective-permute-done((bf16[256,640]{1,0:T(8,128)(2,1)S(1)}, bf16[256,640]{1,0:T(8,128)(2,1)S(1)}, u32[]{:S(2)}, u32[]{:S(2)}) %collective-permute-start.15) | collective-permute-done | bytes 327712 | tf_op jit(solution)/shard_map/ppermute | solution.py:435
  75.1 2.0 %collective-permute-start.19 = (bf16[256,640]{1,0:T(8,128)(2,1)S(1)}, bf16[256,640]{1,0:T(8,128)(2,1)S(1)}, u32[]{:S(2)}, u32[]{:S(2)}) collective-permute-start(bf16[256,640]{1,0:T(8,128)(2,1)S(1)} %collective-permute-done.15.refs_5_.refs_8_), channel_id=1, source_target_pairs={{0,8},{8,16},{16,24},{24,32},{32,40},{40,48},{48,56},{56,0},{64,12... | collective-permute-start | bytes 983048 | tf_op jit(solution)/shard_map/ppermute | solution.py:435
  77.1 1.4 %collective-permute-start.20 = (bf16[256,640]{1,0:T(8,128)(2,1)S(1)}, bf16[256,640]{1,0:T(8,128)(2,1)S(1)}, u32[]{:S(2)}, u32[]{:S(2)}) collective-permute-start(bf16[256,640]{1,0:T(8,128)(2,1)S(1)} %collective-permute-done.11.refs_3_.refs_10_), channel_id=1, source_target_pairs={{0,64},{64,0},{128,192},{192,128},{1,65},{65,1},{129,193},{193,129... | collective-permute-start | bytes 983048 | tf_op jit(solution)/shard_map/ppermute | solution.py:438
  78.5 0.3 collective-permute-start.21
  78.9 2.5 %shard_map.111 = (f32[5,512,256]{2,1,0:T(8,128)S(1)}, bf16[5,512,128]{2,1,0:T(8,128)(2,1)S(1)}) custom-call(bf16[4,128,640]{2,1,0:T(8,128)(2,1)S(1)} %copy-done.1, f32[5,512,256]{2,1,0:T(8,128)S(1)} %get-tuple-element.53.refs_1_, bf16[5,512,128]{2,1,0:T(8,128)(2,1)S(1)} %get-tuple-element.54.refs_2_, bf16[256,640]{1,0:T(8,128)(2,1)S(1)} %shard_map.110.refs_3_.refs_6_, ...), custom_call_target="tpu_custom_call" | custom-call | flops 1006632960 | bytes 8388608 | tf_op jit(solution)/shard_map/pallas_call | solution.py:396
  81.4 1.9 %collective-permute-start.22 = (bf16[256,640]{1,0:T(8,128)(2,1)S(1)}, bf16[256,640]{1,0:T(8,128)(2,1)S(1)}, u32[]{:S(2)}, u32[]{:S(2)}) collective-permute-start(bf16[256,640]{1,0:T(8,128)(2,1)S(1)} %collective-permute-done.12.refs_3_.refs_10_), channel_id=1, source_target_pairs={{0,64},{64,0},{128,192},{192,128},{1,65},{65,1},{129,193},{193,129... | collective-permute-start | bytes 983048 | tf_op jit(solution)/shard_map/ppermute | solution.py:438
  83.3 3.5 %collective-permute-start.23 = (bf16[256,640]{1,0:T(8,128)(2,1)S(1)}, bf16[256,640]{1,0:T(8,128)(2,1)S(1)}, u32[]{:S(2)}, u32[]{:S(2)}) collective-permute-start(bf16[256,640]{1,0:T(8,128)(2,1)S(1)} %collective-permute-done.19.refs_5_.refs_8_), channel_id=1, source_target_pairs={{0,64},{64,0},{128,192},{192,128},{1,65},{65,1},{129,193},{193,129... | collective-permute-start | bytes 983048 | tf_op jit(solution)/shard_map/ppermute | solution.py:438
  86.8 1.8 %shard_map.112 = (f32[5,512,256]{2,1,0:T(8,128)S(1)}, bf16[5,512,128]{2,1,0:T(8,128)(2,1)S(1)}) custom-call(bf16[4,128,640]{2,1,0:T(8,128)(2,1)S(1)} %copy-done.1, f32[5,512,256]{2,1,0:T(8,128)S(1)} %get-tuple-element.61.refs_1_, bf16[5,512,128]{2,1,0:T(8,128)(2,1)S(1)} %get-tuple-element.62.refs_2_, ...), custom_call_target="tpu_custom_call" | custom-call | flops 671088640 | bytes 8388608 | tf_op jit(solution)/shard_map/pallas_call | solution.py:396
  88.7 0.0 copy-start.12
  88.7 1.8 %shard_map.113 = (f32[5,512,256]{2,1,0:T(8,128)S(1)}, bf16[5,512,128]{2,1,0:T(8,128)(2,1)S(1)}) custom-call(bf16[4,128,640]{2,1,0:T(8,128)(2,1)S(1)} %copy-done.1, f32[5,512,256]{2,1,0:T(8,128)S(1)} %get-tuple-element.63.refs_1_, bf16[5,512,128]{2,1,0:T(8,128)(2,1)S(1)} %get-tuple-element.64.refs_2_, ...), custom_call_target="tpu_custom_call" | custom-call | flops 671088640 | bytes 8388608 | tf_op jit(solution)/shard_map/pallas_call | solution.py:396
  90.5 2.5 %collective-permute-done.18.refs_4_.refs_7_ = bf16[256,640]{1,0:T(8,128)(2,1)S(1)} collective-permute-done((bf16[256,640]{1,0:T(8,128)(2,1)S(1)}, bf16[256,640]{1,0:T(8,128)(2,1)S(1)}, u32[]{:S(2)}, u32[]{:S(2)}) %collective-permute-start.18) | collective-permute-done | bytes 327712 | tf_op jit(solution)/shard_map/ppermute | solution.py:435
  93.0 2.1 %collective-permute-start.24 = (bf16[256,640]{1,0:T(8,128)(2,1)S(1)}, bf16[256,640]{1,0:T(8,128)(2,1)S(1)}, u32[]{:S(2)}, u32[]{:S(2)}) collective-permute-start(bf16[256,640]{1,0:T(8,128)(2,1)S(1)} %collective-permute-done.18.refs_4_.refs_7_), channel_id=1, source_target_pairs={{0,64},{64,0},{128,192},{192,128},{1,65},{65,1},{129,193},{193,129... | collective-permute-start | bytes 983048 | tf_op jit(solution)/shard_map/ppermute | solution.py:438
  95.1 1.3 %collective-permute-done.24.refs_5_.refs_6_ = bf16[256,640]{1,0:T(8,128)(2,1)S(1)} collective-permute-done((bf16[256,640]{1,0:T(8,128)(2,1)S(1)}, bf16[256,640]{1,0:T(8,128)(2,1)S(1)}, u32[]{:S(2)}, u32[]{:S(2)}) %collective-permute-start.24) | collective-permute-done | bytes 327712 | tf_op jit(solution)/shard_map/ppermute | solution.py:438
  96.4 2.6 %shard_map.114 = bf16[4,128,640]{2,1,0:T(8,128)(2,1)} custom-call(s32[4]{0:T(128)S(1)} %copy-done.12, bf16[4,128,640]{2,1,0:T(8,128)(2,1)S(1)} %copy-done.1, f32[5,512,256]{2,1,0:T(8,128)S(1)} %get-tuple-element.68.refs_2_, bf16[5,512,128]{2,1,0:T(8,128)(2,1)S(1)} %get-tuple-element.69.refs_3_, bf16[256,640]{1,0:T(8,128)(2,1)S(1)} %collective-permute-done.18.refs_4_.refs_7_, ...), custom_call_target="tpu_custom_call" | custom-call | flops 335544320 | bytes 8388608 | tf_op jit(solution)/shard_map/pallas_call | solution.py:396
  (27 shorter events, 0.1 us)
Async XLA Ops:
  0.0 10.8 %collective-permute-start = (bf16[1024,1152]{1,0:T(8,128)(2,1)}, bf16[1024,1152]{1,0:T(8,128)(2,1)S(1)}, u32[]{:S(2)}, u32[]{:S(2)}) collective-permute-start(bf16[1024,1152]{1,0:T(8,128)(2,1)} %hidden.5), channel_id=1, source_target_pairs={{0,64},{64,0},{128,192},{192,128},{1,65},{65,1},{129,193},{193,129... | collective-permute-start | bytes 7077896 | tf_op jit(solution)/shard_map/ppermute | solution.py:438
  3.2 1.7 %copy-start = (bf16[1024,1152]{1,0:T(8,128)(2,1)S(1)}, bf16[1024,1152]{1,0:T(8,128)(2,1)}, u32[]{:S(2)}) copy-start(bf16[1024,1152]{1,0:T(8,128)(2,1)} %hidden.5) | copy-start | bytes 7077892
  4.9 1.4 %copy-start.2 = (bf16[1152,640]{1,0:T(8,128)(2,1)S(1)}, bf16[1152,640]{1,0:T(8,128)(2,1)}, u32[]{:S(2)}) copy-start(bf16[1152,640]{1,0:T(8,128)(2,1)} %rest_0_.3) | copy-start | bytes 4423684
  6.3 1.4 %copy-start.4 = (bf16[1152,640]{1,0:T(8,128)(2,1)S(1)}, bf16[1152,640]{1,0:T(8,128)(2,1)}, u32[]{:S(2)}) copy-start(bf16[1152,640]{1,0:T(8,128)(2,1)} %rest_1_.3) | copy-start | bytes 4423684
  7.7 0.7 copy-start.8
  8.4 0.7 copy-start.9
  9.0 0.7 copy-start.10
  9.7 1.4 %copy-start.3 = (bf16[1152,640]{1,0:T(8,128)(2,1)S(1)}, bf16[1152,640]{1,0:T(8,128)(2,1)}, u32[]{:S(2)}) copy-start(bf16[1152,640]{1,0:T(8,128)(2,1)} %rest_0_.3) | copy-start | bytes 4423684
  9.7 1.8 %copy-start.5 = (bf16[1152,640]{1,0:T(8,128)(2,1)S(1)}, bf16[1152,640]{1,0:T(8,128)(2,1)}, u32[]{:S(2)}) copy-start(bf16[1152,640]{1,0:T(8,128)(2,1)} %rest_1_.3) | copy-start | bytes 4423684
  13.7 8.9 %collective-permute-start.1 = (bf16[240,640]{1,0:T(8,128)(2,1)S(1)}, bf16[240,640]{1,0:T(8,128)(2,1)S(1)}, u32[]{:S(2)}, u32[]{:S(2)}) collective-permute-start(bf16[240,640]{1,0:T(8,128)(2,1)S(1)} %get-tuple-element.41), channel_id=1, source_target_pairs={{0,8},{8,16},{16,24},{24,32},{32,40},{40,48},{48,56},{56,0},{64,12... | collective-permute-start | bytes 921608 | tf_op jit(solution)/shard_map/ppermute | solution.py:435
  17.6 7.1 %collective-permute-start.5 = (bf16[240,640]{1,0:T(8,128)(2,1)S(1)}, bf16[240,640]{1,0:T(8,128)(2,1)S(1)}, u32[]{:S(2)}, u32[]{:S(2)}) collective-permute-start(bf16[240,640]{1,0:T(8,128)(2,1)S(1)} %get-tuple-element.48), channel_id=1, source_target_pairs={{0,8},{8,16},{16,24},{24,32},{32,40},{40,48},{48,56},{56,0},{64,12... | collective-permute-start | bytes 921608 | tf_op jit(solution)/shard_map/ppermute | solution.py:435
  22.6 12.7 %copy-start.1 = (bf16[4,128,640]{2,1,0:T(8,128)(2,1)S(1)}, bf16[4,128,640]{2,1,0:T(8,128)(2,1)}, u32[]{:S(2)}) copy-start(bf16[4,128,640]{2,1,0:T(8,128)(2,1)} %refs_1_.1) | copy-start | bytes 1966084
  22.6 12.6 %copy-start.6 = (bf16[4,128,640]{2,1,0:T(8,128)(2,1)S(1)}, bf16[4,128,640]{2,1,0:T(8,128)(2,1)}, u32[]{:S(2)}) copy-start(bf16[4,128,640]{2,1,0:T(8,128)(2,1)} %own_k.1) | copy-start | bytes 1966084
  22.6 12.6 %copy-start.7 = (bf16[4,128,640]{2,1,0:T(8,128)(2,1)S(1)}, bf16[4,128,640]{2,1,0:T(8,128)(2,1)}, u32[]{:S(2)}) copy-start(bf16[4,128,640]{2,1,0:T(8,128)(2,1)} %own_v.1) | copy-start | bytes 1966084
  22.7 6.1 %collective-permute-start.2 = (bf16[240,640]{1,0:T(8,128)(2,1)S(1)}, bf16[240,640]{1,0:T(8,128)(2,1)S(1)}, u32[]{:S(2)}, u32[]{:S(2)}) collective-permute-start(bf16[240,640]{1,0:T(8,128)(2,1)S(1)} %shard_map.103), channel_id=1, source_target_pairs={{0,8},{8,16},{16,24},{24,32},{32,40},{40,48},{48,56},{56,0},{64,12... | collective-permute-start | bytes 921608 | tf_op jit(solution)/shard_map/ppermute | solution.py:435
  24.8 7.3 %collective-permute-start.6 = (bf16[240,640]{1,0:T(8,128)(2,1)S(1)}, bf16[240,640]{1,0:T(8,128)(2,1)S(1)}, u32[]{:S(2)}, u32[]{:S(2)}) collective-permute-start(bf16[240,640]{1,0:T(8,128)(2,1)S(1)} %shard_map.107), channel_id=1, source_target_pairs={{0,8},{8,16},{16,24},{24,32},{32,40},{40,48},{48,56},{56,0},{64,12... | collective-permute-start | bytes 921608 | tf_op jit(solution)/shard_map/ppermute | solution.py:435
  28.9 11.3 %collective-permute-start.3 = (bf16[240,640]{1,0:T(8,128)(2,1)S(1)}, bf16[240,640]{1,0:T(8,128)(2,1)S(1)}, u32[]{:S(2)}, u32[]{:S(2)}) collective-permute-start(bf16[240,640]{1,0:T(8,128)(2,1)S(1)} %shard_map.104), channel_id=1, source_target_pairs={{0,8},{8,16},{16,24},{24,32},{32,40},{40,48},{48,56},{56,0},{64,12... | collective-permute-start | bytes 921608 | tf_op jit(solution)/shard_map/ppermute | solution.py:435
  32.2 23.0 %copy-start.11 = (s32[4]{0:T(128)S(1)}, s32[4]{0:T(128)}, u32[]{:S(2)}) copy-start(s32[4]{0:T(128)} %counts.7) | copy-start | bytes 52
  32.2 8.2 %collective-permute-start.7 = (bf16[240,640]{1,0:T(8,128)(2,1)S(1)}, bf16[240,640]{1,0:T(8,128)(2,1)S(1)}, u32[]{:S(2)}, u32[]{:S(2)}) collective-permute-start(bf16[240,640]{1,0:T(8,128)(2,1)S(1)} %shard_map.108), channel_id=1, source_target_pairs={{0,8},{8,16},{16,24},{24,32},{32,40},{40,48},{48,56},{56,0},{64,12... | collective-permute-start | bytes 921608 | tf_op jit(solution)/shard_map/ppermute | solution.py:435
  40.3 6.1 %collective-permute-start.4 = (bf16[240,640]{1,0:T(8,128)(2,1)S(1)}, bf16[240,640]{1,0:T(8,128)(2,1)S(1)}, u32[]{:S(2)}, u32[]{:S(2)}) collective-permute-start(bf16[240,640]{1,0:T(8,128)(2,1)S(1)} %shard_map.106), channel_id=1, source_target_pairs={{0,8},{8,16},{16,24},{24,32},{32,40},{40,48},{48,56},{56,0},{64,12... | collective-permute-start | bytes 921608 | tf_op jit(solution)/shard_map/ppermute | solution.py:435
  40.4 6.0 %collective-permute-start.8 = (bf16[240,640]{1,0:T(8,128)(2,1)S(1)}, bf16[240,640]{1,0:T(8,128)(2,1)S(1)}, u32[]{:S(2)}, u32[]{:S(2)}) collective-permute-start(bf16[240,640]{1,0:T(8,128)(2,1)S(1)} %collective-permute-done.7), channel_id=1, source_target_pairs={{0,64},{64,0},{128,192},{192,128},{1,65},{65,1},{129,193},{193,129... | collective-permute-start | bytes 921608 | tf_op jit(solution)/shard_map/ppermute | solution.py:438
  46.8 8.5 %collective-permute-start.9 = (bf16[224,640]{1,0:T(8,128)(2,1)S(1)}, bf16[224,640]{1,0:T(8,128)(2,1)S(1)}, u32[]{:S(2)}, u32[]{:S(2)}) collective-permute-start(bf16[224,640]{1,0:T(8,128)(2,1)S(1)} %shard_map.109.rows), channel_id=1, source_target_pairs={{0,128},{64,192},{128,0},{192,64},{1,129},{65,193},{129,1},{193,65... | collective-permute-start | bytes 860168 | tf_op jit(solution)/shard_map/ppermute | solution.py:459
  55.9 3.7 %collective-permute-start.13 = (bf16[256,640]{1,0:T(8,128)(2,1)S(1)}, bf16[256,640]{1,0:T(8,128)(2,1)S(1)}, u32[]{:S(2)}, u32[]{:S(2)}) collective-permute-start(bf16[256,640]{1,0:T(8,128)(2,1)S(1)} %shard_map.110.refs_3_.refs_6_), channel_id=1, source_target_pairs={{0,64},{64,0},{128,192},{192,128},{1,65},{65,1},{129,193},{193,129... | collective-permute-start | bytes 983048 | tf_op jit(solution)/shard_map/ppermute | solution.py:438
  58.4 6.2 %collective-permute-start.10 = (bf16[256,640]{1,0:T(8,128)(2,1)S(1)}, bf16[256,640]{1,0:T(8,128)(2,1)S(1)}, u32[]{:S(2)}, u32[]{:S(2)}) collective-permute-start(bf16[256,640]{1,0:T(8,128)(2,1)S(1)} %shard_map.110.refs_3_.refs_6_), channel_id=1, source_target_pairs={{0,8},{8,16},{16,24},{24,32},{32,40},{40,48},{48,56},{56,0},{64,12... | collective-permute-start | bytes 983048 | tf_op jit(solution)/shard_map/ppermute | solution.py:435
  59.6 8.5 %collective-permute-start.14 = (bf16[256,640]{1,0:T(8,128)(2,1)S(1)}, bf16[256,640]{1,0:T(8,128)(2,1)S(1)}, u32[]{:S(2)}, u32[]{:S(2)}) collective-permute-start(bf16[256,640]{1,0:T(8,128)(2,1)S(1)} %collective-permute-done.13.refs_4_.refs_5_), channel_id=1, source_target_pairs={{0,8},{8,16},{16,24},{24,32},{32,40},{40,48},{48,56},{56,0},{64,12... | collective-permute-start | bytes 983048 | tf_op jit(solution)/shard_map/ppermute | solution.py:435
  64.6 7.0 %collective-permute-start.11 = (bf16[256,640]{1,0:T(8,128)(2,1)S(1)}, bf16[256,640]{1,0:T(8,128)(2,1)S(1)}, u32[]{:S(2)}, u32[]{:S(2)}) collective-permute-start(bf16[256,640]{1,0:T(8,128)(2,1)S(1)} %collective-permute-done.10.refs_7_.refs_14_), channel_id=1, source_target_pairs={{0,8},{8,16},{16,24},{24,32},{32,40},{40,48},{48,56},{56,0},{64,12... | collective-permute-start | bytes 983048 | tf_op jit(solution)/shard_map/ppermute | solution.py:435
  68.1 7.0 %collective-permute-start.15 = (bf16[256,640]{1,0:T(8,128)(2,1)S(1)}, bf16[256,640]{1,0:T(8,128)(2,1)S(1)}, u32[]{:S(2)}, u32[]{:S(2)}) collective-permute-start(bf16[256,640]{1,0:T(8,128)(2,1)S(1)} %collective-permute-done.14.refs_9_.refs_12_), channel_id=1, source_target_pairs={{0,8},{8,16},{16,24},{24,32},{32,40},{40,48},{48,56},{56,0},{64,12... | collective-permute-start | bytes 983048 | tf_op jit(solution)/shard_map/ppermute | solution.py:435
  70.0 8.6 %collective-permute-start.16 = (bf16[256,640]{1,0:T(8,128)(2,1)S(1)}, bf16[256,640]{1,0:T(8,128)(2,1)S(1)}, u32[]{:S(2)}, u32[]{:S(2)}) collective-permute-start(bf16[256,640]{1,0:T(8,128)(2,1)S(1)} %collective-permute-done.10.refs_7_.refs_14_), channel_id=1, source_target_pairs={{0,64},{64,0},{128,192},{192,128},{1,65},{65,1},{129,193},{193,129... | collective-permute-start | bytes 983048 | tf_op jit(solution)/shard_map/ppermute | solution.py:438
  70.3 8.6 %collective-permute-start.17 = (bf16[256,640]{1,0:T(8,128)(2,1)S(1)}, bf16[256,640]{1,0:T(8,128)(2,1)S(1)}, u32[]{:S(2)}, u32[]{:S(2)}) collective-permute-start(bf16[256,640]{1,0:T(8,128)(2,1)S(1)} %collective-permute-done.14.refs_9_.refs_12_), channel_id=1, source_target_pairs={{0,64},{64,0},{128,192},{192,128},{1,65},{65,1},{129,193},{193,129... | collective-permute-start | bytes 983048 | tf_op jit(solution)/shard_map/ppermute | solution.py:438
  71.6 9.8 %collective-permute-start.12 = (bf16[256,640]{1,0:T(8,128)(2,1)S(1)}, bf16[256,640]{1,0:T(8,128)(2,1)S(1)}, u32[]{:S(2)}, u32[]{:S(2)}) collective-permute-start(bf16[256,640]{1,0:T(8,128)(2,1)S(1)} %collective-permute-done.11.refs_3_.refs_10_), channel_id=1, source_target_pairs={{0,8},{8,16},{16,24},{24,32},{32,40},{40,48},{48,56},{56,0},{64,12... | collective-permute-start | bytes 983048 | tf_op jit(solution)/shard_map/ppermute | solution.py:435
  75.1 8.2 %collective-permute-start.19 = (bf16[256,640]{1,0:T(8,128)(2,1)S(1)}, bf16[256,640]{1,0:T(8,128)(2,1)S(1)}, u32[]{:S(2)}, u32[]{:S(2)}) collective-permute-start(bf16[256,640]{1,0:T(8,128)(2,1)S(1)} %collective-permute-done.15.refs_5_.refs_8_), channel_id=1, source_target_pairs={{0,8},{8,16},{16,24},{24,32},{32,40},{40,48},{48,56},{56,0},{64,12... | collective-permute-start | bytes 983048 | tf_op jit(solution)/shard_map/ppermute | solution.py:435
  77.1 9.7 %collective-permute-start.20 = (bf16[256,640]{1,0:T(8,128)(2,1)S(1)}, bf16[256,640]{1,0:T(8,128)(2,1)S(1)}, u32[]{:S(2)}, u32[]{:S(2)}) collective-permute-start(bf16[256,640]{1,0:T(8,128)(2,1)S(1)} %collective-permute-done.11.refs_3_.refs_10_), channel_id=1, source_target_pairs={{0,64},{64,0},{128,192},{192,128},{1,65},{65,1},{129,193},{193,129... | collective-permute-start | bytes 983048 | tf_op jit(solution)/shard_map/ppermute | solution.py:438
  78.5 8.3 %collective-permute-start.21 = (bf16[256,640]{1,0:T(8,128)(2,1)S(1)}, bf16[256,640]{1,0:T(8,128)(2,1)S(1)}, u32[]{:S(2)}, u32[]{:S(2)}) collective-permute-start(bf16[256,640]{1,0:T(8,128)(2,1)S(1)} %collective-permute-done.15.refs_5_.refs_8_), channel_id=1, source_target_pairs={{0,64},{64,0},{128,192},{192,128},{1,65},{65,1},{129,193},{193,129... | collective-permute-start | bytes 983048 | tf_op jit(solution)/shard_map/ppermute | solution.py:438
  81.4 7.3 %collective-permute-start.22 = (bf16[256,640]{1,0:T(8,128)(2,1)S(1)}, bf16[256,640]{1,0:T(8,128)(2,1)S(1)}, u32[]{:S(2)}, u32[]{:S(2)}) collective-permute-start(bf16[256,640]{1,0:T(8,128)(2,1)S(1)} %collective-permute-done.12.refs_3_.refs_10_), channel_id=1, source_target_pairs={{0,64},{64,0},{128,192},{192,128},{1,65},{65,1},{129,193},{193,129... | collective-permute-start | bytes 983048 | tf_op jit(solution)/shard_map/ppermute | solution.py:438
  83.3 5.4 %collective-permute-start.23 = (bf16[256,640]{1,0:T(8,128)(2,1)S(1)}, bf16[256,640]{1,0:T(8,128)(2,1)S(1)}, u32[]{:S(2)}, u32[]{:S(2)}) collective-permute-start(bf16[256,640]{1,0:T(8,128)(2,1)S(1)} %collective-permute-done.19.refs_5_.refs_8_), channel_id=1, source_target_pairs={{0,64},{64,0},{128,192},{192,128},{1,65},{65,1},{129,193},{193,129... | collective-permute-start | bytes 983048 | tf_op jit(solution)/shard_map/ppermute | solution.py:438
  86.8 6.2 %collective-permute-start.18 = (bf16[256,640]{1,0:T(8,128)(2,1)S(1)}, bf16[256,640]{1,0:T(8,128)(2,1)S(1)}, u32[]{:S(2)}, u32[]{:S(2)}) collective-permute-start(bf16[256,640]{1,0:T(8,128)(2,1)S(1)} %collective-permute-done.12.refs_3_.refs_10_), channel_id=1, source_target_pairs={{0,8},{8,16},{16,24},{24,32},{32,40},{40,48},{48,56},{56,0},{64,12... | collective-permute-start | bytes 983048 | tf_op jit(solution)/shard_map/ppermute | solution.py:435
  88.7 7.7 %copy-start.12 = (s32[4]{0:T(128)S(1)}, s32[4]{0:T(128)}, u32[]{:S(2)}) copy-start(s32[4]{0:T(128)} %refs_0_.7) | copy-start | bytes 52
  93.0 3.3 %collective-permute-start.24 = (bf16[256,640]{1,0:T(8,128)(2,1)S(1)}, bf16[256,640]{1,0:T(8,128)(2,1)S(1)}, u32[]{:S(2)}, u32[]{:S(2)}) collective-permute-start(bf16[256,640]{1,0:T(8,128)(2,1)S(1)} %collective-permute-done.18.refs_4_.refs_7_), channel_id=1, source_target_pairs={{0,64},{64,0},{128,192},{192,128},{1,65},{65,1},{129,193},{193,129... | collective-permute-start | bytes 983048 | tf_op jit(solution)/shard_map/ppermute | solution.py:438

commit v4 on v3

--- a/solution.py
+++ b/solution.py
@@ -484,14 +484,13 @@
     g3, state = lax.optimization_barrier((g3, state))
     xg3 = swap(g3)
     g4 = step(g3)
-    h3, state = lax.optimization_barrier((h3, state))
-    xh3 = swap(h3)
     near = (g2, xg2, h2, xh2)
     state = attend(suffix_q, state, [upper(*near), lower(*near)])
+    xh3 = swap(h3)
+    g4, state = lax.optimization_barrier((g4, state))
+    xg4 = swap(g4)
     near = (g3, xg3, h3, xh3)
     state = attend(suffix_q, state, [upper(*near), lower(*near)])
-    g4, state = lax.optimization_barrier((g4, state))
-    xg4 = swap(g4)
     return attend(suffix_q, state, [(g4, xg4, xg4, g4)], lengths=suffix_lengths)
 
 

time: 99.3 us -> 96.4 us (0.971)
  waiting for transfers between devices: 22.8 us -> 17.6 us
  starting transfers between devices: 46.2 us -> 48.5 us
    ppermute x14, waiting for transfers between devices: 15.7 us -> 11.8 us  [step(): return lax.ppermute(array, ('store', 'req'), around)]
    ppermute x14, starting transfers between devices: 25.4 us -> 29.3 us  [step(): return lax.ppermute(array, ('store', 'req'), around)]
    ppermute x10, starting transfers between devices: 17.8 us -> 16.1 us  [swap(): return lax.ppermute(array, 'store', across)]
    ppermute x10, waiting for transfers between devices: 1.58 us -> 0.33 us  [swap(): return lax.ppermute(array, 'store', across)]
  transfers between devices with their start and end apart: 25 -> 25, of which waited for: 11 -> 9; matrix products, arithmetic and copies ran while one was open for 0% -> 0% of each run, Pallas kernels for 17% -> 17%
where the time goes in v4:
time: 96.4 us; the launch traced here: 96.1 us
  starting transfers between devices  48.5 us (50%)
  Pallas kernels  22.7 us (24%)
  waiting for transfers between devices  17.6 us (18%)
  local copies, waits for them, and re-layouts  7.2 us (7%)
    ppermute x14, starting transfers between devices, step(): return lax.ppermute(array, ('store', 'req'), around)  29.3 us
    ppermute x10, starting transfers between devices, swap(): return lax.ppermute(array, 'store', across)  16.1 us
    ppermute x14, waiting for transfers between devices, step(): return lax.ppermute(array, ('store', 'req'), around)  11.8 us
    pallas_call x4, Pallas kernels, attend(): pl.pallas_call(functools.partial(stage_kernel, lengths is not None, len(p...  8.76 us
    unnamed x26, local copies, waits for them, and re-layouts  7.2 us
    pallas_call x2, Pallas kernels, project_rows(): pl.pallas_call(functools.partial(projection_kernel, plan), out_shape=outs...  6.44 us
    ppermute x1, waiting for transfers between devices, per_device(): mine = merge(row_counts, rows, lax.ppermute(rows, 'store', far))  5.46 us
    pallas_call x1, Pallas kernels, attend_own(): pl.pallas_call(own_kernel, out_shape=[jax.ShapeDtypeStruct((heads, rows,...  4.92 us
  transfers between devices with their start and end apart: 25, of which 9 were waited for; matrix products, arithmetic and copies ran while one was open for 0% of the time, Pallas kernels for 17%

profile of v4, /device:TPU:1, one launch (start us, length us, event | category | flops | bytes accessed | tf_op | source)
XLA Modules:
  0.0 96.1 jit_solution(1022519148980488189)
XLA Ops:
  0.0 3.2 %collective-permute-start = (bf16[1024,1152]{1,0:T(8,128)(2,1)}, bf16[1024,1152]{1,0:T(8,128)(2,1)S(1)}, u32[]{:S(2)}, u32[]{:S(2)}) collective-permute-start(bf16[1024,1152]{1,0:T(8,128)(2,1)} %hidden.5), channel_id=1, source_target_pairs={{0,64},{64,0},{128,192},{192,128},{1,65},{65,1},{129,193},{193,129... | collective-permute-start | bytes 7077896 | tf_op jit(solution)/shard_map/ppermute | solution.py:438
  3.2 1.7 %copy-done = bf16[1024,1152]{1,0:T(8,128)(2,1)S(1)} copy-done((bf16[1024,1152]{1,0:T(8,128)(2,1)S(1)}, bf16[1024,1152]{1,0:T(8,128)(2,1)}, u32[]{:S(2)}) %copy-start) | copy-done | bytes 2359320
  4.9 1.4 %copy-done.2 = bf16[1152,640]{1,0:T(8,128)(2,1)S(1)} copy-done((bf16[1152,640]{1,0:T(8,128)(2,1)S(1)}, bf16[1152,640]{1,0:T(8,128)(2,1)}, u32[]{:S(2)}) %copy-start.2) | copy-done | bytes 1474584
  6.3 1.4 %copy-done.4 = bf16[1152,640]{1,0:T(8,128)(2,1)S(1)} copy-done((bf16[1152,640]{1,0:T(8,128)(2,1)S(1)}, bf16[1152,640]{1,0:T(8,128)(2,1)}, u32[]{:S(2)}) %copy-start.4) | copy-done | bytes 1474584
  7.7 0.7 copy-done.8
  8.4 0.7 copy-done.9
  9.1 0.7 copy-done.10
  9.7 1.1 %shard_map.100 = (f32[8,640]{1,0:T(8,128)S(1)}, f32[8,640]{1,0:T(8,128)S(1)}) custom-call(s32[4]{0:T(128)S(1)} %copy-done.10, bf16[1024,1152]{1,0:T(8,128)(2,1)S(1)} %copy-done, f32[1152]{0:T(1024)S(1)} %copy-done.8, f32[1152]{0:T(1024)S(1)} %copy-done.9, bf16[1152,640]{1,0:T(8,128)(2,1)S(1)} %copy-done.2, bf16[1152,640]{1,0:T(8,128)(2,1)S(1)} %copy-done.4), custom_call_target="tpu_custom_call" | custom-call | flops 141557760 | bytes 6291456 | tf_op jit(solution)/shard_map/pallas_call | solution.py:64
  10.8 0.0 collective-permute-done.hidden_other
  10.8 0.3 copy-done.3
  11.1 0.4 copy-done.5
  11.5 2.2 %shard_map.102 = (bf16[240,640]{1,0:T(8,128)(2,1)S(1)}, bf16[240,640]{1,0:T(8,128)(2,1)S(1)}) custom-call(s32[4]{0:T(128)S(1)} %copy-done.10, bf16[1024,1152]{1,0:T(8,128)(2,1)S(1)} %copy-done, bf16[1024,1152]{1,0:T(8,128)(2,1)S(1)} %collective-permute-done.hidden_other, f32[1152]{0:T(1024)S(1)} %copy-done.8, bf16[1152,640]{1,0:T(8,128)(2,1)S(1)} %copy-done.3, ...), custom_call_target="tpu_custom_call" | custom-call | flops 660602880 | bytes 4194304 | tf_op jit(solution)/shard_map/pallas_call | solution.py:154
  13.7 3.9 %collective-permute-start.1 = (bf16[240,640]{1,0:T(8,128)(2,1)S(1)}, bf16[240,640]{1,0:T(8,128)(2,1)S(1)}, u32[]{:S(2)}, u32[]{:S(2)}) collective-permute-start(bf16[240,640]{1,0:T(8,128)(2,1)S(1)} %get-tuple-element.38), channel_id=1, source_target_pairs={{0,8},{8,16},{16,24},{24,32},{32,40},{40,48},{48,56},{56,0},{64,12... | collective-permute-start | bytes 921608 | tf_op jit(solution)/shard_map/ppermute | solution.py:435
  17.6 0.7 collective-permute-start.5
  18.4 4.3 %shard_map.101 = (f32[232,640]{1,0:T(8,128)S(1)}, f32[232,640]{1,0:T(8,128)S(1)}, f32[232,640]{1,0:T(8,128)S(1)}, f32[232,640]{1,0:T(8,128)S(1)}, f32[232,640]{1,0:T(8,128)S(1)}, /*index=5*/f32[232,640]{1,0:T(8,128)S(1)}) custom-call(s32[4]{0:T(128)S(1)} %copy-done.10, bf16[1024,1152]{1,0:T(8,128)(2,1)S(1)} %copy-done, ...), custom_call_target="tpu_custom_call" | custom-call | flops 1981808640 | bytes 4194304 | tf_op jit(solution)/shard_map/pallas_call | solution.py:154
  22.6 0.0 copy-start.1
  22.6 0.0 copy-start.6
  22.6 0.0 copy-start.7
  22.7 0.1 shard_map.103
  22.7 2.0 %collective-permute-start.2 = (bf16[240,640]{1,0:T(8,128)(2,1)S(1)}, bf16[240,640]{1,0:T(8,128)(2,1)S(1)}, u32[]{:S(2)}, u32[]{:S(2)}) collective-permute-start(bf16[240,640]{1,0:T(8,128)(2,1)S(1)} %shard_map.103), channel_id=1, source_target_pairs={{0,8},{8,16},{16,24},{24,32},{32,40},{40,48},{48,56},{56,0},{64,12... | collective-permute-start | bytes 921608 | tf_op jit(solution)/shard_map/ppermute | solution.py:435
  24.7 0.0 collective-permute-done.5.received
  24.7 0.1 shard_map.107
  24.8 3.2 %collective-permute-start.6 = (bf16[240,640]{1,0:T(8,128)(2,1)S(1)}, bf16[240,640]{1,0:T(8,128)(2,1)S(1)}, u32[]{:S(2)}, u32[]{:S(2)}) collective-permute-start(bf16[240,640]{1,0:T(8,128)(2,1)S(1)} %shard_map.107), channel_id=1, source_target_pairs={{0,8},{8,16},{16,24},{24,32},{32,40},{40,48},{48,56},{56,0},{64,12... | collective-permute-start | bytes 921608 | tf_op jit(solution)/shard_map/ppermute | solution.py:435
  28.0 0.8 collective-permute-done.2.received
  28.8 0.1 shard_map.104
  28.9 2.9 %collective-permute-start.3 = (bf16[240,640]{1,0:T(8,128)(2,1)S(1)}, bf16[240,640]{1,0:T(8,128)(2,1)S(1)}, u32[]{:S(2)}, u32[]{:S(2)}) collective-permute-start(bf16[240,640]{1,0:T(8,128)(2,1)S(1)} %shard_map.104), channel_id=1, source_target_pairs={{0,8},{8,16},{16,24},{24,32},{32,40},{40,48},{48,56},{56,0},{64,12... | collective-permute-start | bytes 921608 | tf_op jit(solution)/shard_map/ppermute | solution.py:435
  31.8 0.3 collective-permute-done.6.received
  32.1 0.1 shard_map.108
  32.2 0.0 copy-start.11
  32.2 3.1 %collective-permute-start.7 = (bf16[240,640]{1,0:T(8,128)(2,1)S(1)}, bf16[240,640]{1,0:T(8,128)(2,1)S(1)}, u32[]{:S(2)}, u32[]{:S(2)}) collective-permute-start(bf16[240,640]{1,0:T(8,128)(2,1)S(1)} %shard_map.108), channel_id=1, source_target_pairs={{0,8},{8,16},{16,24},{24,32},{32,40},{40,48},{48,56},{56,0},{64,12... | collective-permute-start | bytes 921608 | tf_op jit(solution)/shard_map/ppermute | solution.py:435
  35.3 4.9 %shard_map.105 = (f32[5,512,256]{2,1,0:T(8,128)S(1)}, bf16[5,512,128]{2,1,0:T(8,128)(2,1)S(1)}) custom-call(bf16[4,128,640]{2,1,0:T(8,128)(2,1)S(1)} %copy-done.1, bf16[4,128,640]{2,1,0:T(8,128)(2,1)S(1)} %copy-done.6, bf16[4,128,640]{2,1,0:T(8,128)(2,1)S(1)} %copy-done.7), custom_call_target="tpu_custom_call" | custom-call | flops 167772160 | bytes 6291456 | tf_op jit(solution)/shard_map/pallas_call | solution.py:365
  40.2 0.0 collective-permute-done.3.received
  40.2 0.1 shard_map.106
  40.3 0.1 collective-permute-start.4
  40.4 2.3 %collective-permute-start.8 = (bf16[240,640]{1,0:T(8,128)(2,1)S(1)}, bf16[240,640]{1,0:T(8,128)(2,1)S(1)}, u32[]{:S(2)}, u32[]{:S(2)}) collective-permute-start(bf16[240,640]{1,0:T(8,128)(2,1)S(1)} %collective-permute-done.7), channel_id=1, source_target_pairs={{0,64},{64,0},{128,192},{192,128},{1,65},{65,1},{129,193},{193,129... | collective-permute-start | bytes 921608 | tf_op jit(solution)/shard_map/ppermute | solution.py:438
  42.7 3.7 %collective-permute-done.4.ours = bf16[240,640]{1,0:T(8,128)(2,1)S(1)} collective-permute-done((bf16[240,640]{1,0:T(8,128)(2,1)S(1)}, bf16[240,640]{1,0:T(8,128)(2,1)S(1)}, u32[]{:S(2)}, u32[]{:S(2)}) %collective-permute-start.4) | collective-permute-done | bytes 307232 | tf_op jit(solution)/shard_map/ppermute | solution.py:435
  46.4 0.4 shard_map.109.rows
  46.8 3.0 %collective-permute-start.9 = (bf16[224,640]{1,0:T(8,128)(2,1)S(1)}, bf16[224,640]{1,0:T(8,128)(2,1)S(1)}, u32[]{:S(2)}, u32[]{:S(2)}) collective-permute-start(bf16[224,640]{1,0:T(8,128)(2,1)S(1)} %shard_map.109.rows), channel_id=1, source_target_pairs={{0,128},{64,192},{128,0},{192,64},{1,129},{65,193},{129,1},{193,65... | collective-permute-start | bytes 860168 | tf_op jit(solution)/shard_map/ppermute | solution.py:459
  49.8 5.5 %collective-permute-done.9.rows_far = bf16[224,640]{1,0:T(8,128)(2,1)S(1)} collective-permute-done((bf16[224,640]{1,0:T(8,128)(2,1)S(1)}, bf16[224,640]{1,0:T(8,128)(2,1)S(1)}, u32[]{:S(2)}, u32[]{:S(2)}) %collective-permute-start.9) | collective-permute-done | bytes 286752 | tf_op jit(solution)/shard_map/ppermute | solution.py:459
  55.2 0.6 shard_map.110.refs_3_.refs_6_
  55.9 2.5 %collective-permute-start.13 = (bf16[256,640]{1,0:T(8,128)(2,1)S(1)}, bf16[256,640]{1,0:T(8,128)(2,1)S(1)}, u32[]{:S(2)}, u32[]{:S(2)}) collective-permute-start(bf16[256,640]{1,0:T(8,128)(2,1)S(1)} %shard_map.110.refs_3_.refs_6_), channel_id=1, source_target_pairs={{0,64},{64,0},{128,192},{192,128},{1,65},{65,1},{129,193},{193,129... | collective-permute-start | bytes 983048 | tf_op jit(solution)/shard_map/ppermute | solution.py:438
  58.4 0.9 collective-permute-start.10
  59.3 0.3 collective-permute-done.13.refs_4_.refs_5_
  59.6 0.9 collective-permute-start.14
  60.6 4.0 %collective-permute-done.10.refs_7_.refs_14_ = bf16[256,640]{1,0:T(8,128)(2,1)S(1)} collective-permute-done((bf16[256,640]{1,0:T(8,128)(2,1)S(1)}, bf16[256,640]{1,0:T(8,128)(2,1)S(1)}, u32[]{:S(2)}, u32[]{:S(2)}) %collective-permute-start.10) | collective-permute-done | bytes 327712 | tf_op jit(solution)/shard_map/ppermute | solution.py:435
  64.6 1.9 %collective-permute-start.11 = (bf16[256,640]{1,0:T(8,128)(2,1)S(1)}, bf16[256,640]{1,0:T(8,128)(2,1)S(1)}, u32[]{:S(2)}, u32[]{:S(2)}) collective-permute-start(bf16[256,640]{1,0:T(8,128)(2,1)S(1)} %collective-permute-done.10.refs_7_.refs_14_), channel_id=1, source_target_pairs={{0,8},{8,16},{16,24},{24,32},{32,40},{40,48},{48,56},{56,0},{64,12... | collective-permute-start | bytes 983048 | tf_op jit(solution)/shard_map/ppermute | solution.py:435
  66.4 1.6 %collective-permute-done.14.refs_9_.refs_12_ = bf16[256,640]{1,0:T(8,128)(2,1)S(1)} collective-permute-done((bf16[256,640]{1,0:T(8,128)(2,1)S(1)}, bf16[256,640]{1,0:T(8,128)(2,1)S(1)}, u32[]{:S(2)}, u32[]{:S(2)}) %collective-permute-start.14) | collective-permute-done | bytes 327712 | tf_op jit(solution)/shard_map/ppermute | solution.py:435
  68.1 1.9 %collective-permute-start.15 = (bf16[256,640]{1,0:T(8,128)(2,1)S(1)}, bf16[256,640]{1,0:T(8,128)(2,1)S(1)}, u32[]{:S(2)}, u32[]{:S(2)}) collective-permute-start(bf16[256,640]{1,0:T(8,128)(2,1)S(1)} %collective-permute-done.14.refs_9_.refs_12_), channel_id=1, source_target_pairs={{0,8},{8,16},{16,24},{24,32},{32,40},{40,48},{48,56},{56,0},{64,12... | collective-permute-start | bytes 983048 | tf_op jit(solution)/shard_map/ppermute | solution.py:435
  70.0 0.3 collective-permute-start.16
  70.3 0.2 collective-permute-start.17
  70.5 1.1 %collective-permute-done.11.refs_3_.refs_10_ = bf16[256,640]{1,0:T(8,128)(2,1)S(1)} collective-permute-done((bf16[256,640]{1,0:T(8,128)(2,1)S(1)}, bf16[256,640]{1,0:T(8,128)(2,1)S(1)}, u32[]{:S(2)}, u32[]{:S(2)}) %collective-permute-start.11) | collective-permute-done | bytes 327712 | tf_op jit(solution)/shard_map/ppermute | solution.py:435
  71.6 2.0 %collective-permute-start.12 = (bf16[256,640]{1,0:T(8,128)(2,1)S(1)}, bf16[256,640]{1,0:T(8,128)(2,1)S(1)}, u32[]{:S(2)}, u32[]{:S(2)}) collective-permute-start(bf16[256,640]{1,0:T(8,128)(2,1)S(1)} %collective-permute-done.11.refs_3_.refs_10_), channel_id=1, source_target_pairs={{0,8},{8,16},{16,24},{24,32},{32,40},{40,48},{48,56},{56,0},{64,12... | collective-permute-start | bytes 983048 | tf_op jit(solution)/shard_map/ppermute | solution.py:435
  73.6 1.4 %collective-permute-start.19 = (bf16[256,640]{1,0:T(8,128)(2,1)S(1)}, bf16[256,640]{1,0:T(8,128)(2,1)S(1)}, u32[]{:S(2)}, u32[]{:S(2)}) collective-permute-start(bf16[256,640]{1,0:T(8,128)(2,1)S(1)} %collective-permute-done.11.refs_3_.refs_10_), channel_id=1, source_target_pairs={{0,64},{64,0},{128,192},{192,128},{1,65},{65,1},{129,193},{193,129... | collective-permute-start | bytes 983048 | tf_op jit(solution)/shard_map/ppermute | solution.py:438
  75.0 0.1 collective-permute-done.15.refs_5_.refs_8_
  75.1 2.9 %collective-permute-start.22 = (bf16[256,640]{1,0:T(8,128)(2,1)S(1)}, bf16[256,640]{1,0:T(8,128)(2,1)S(1)}, u32[]{:S(2)}, u32[]{:S(2)}) collective-permute-start(bf16[256,640]{1,0:T(8,128)(2,1)S(1)} %collective-permute-done.15.refs_5_.refs_8_), channel_id=1, source_target_pairs={{0,8},{8,16},{16,24},{24,32},{32,40},{40,48},{48,56},{56,0},{64,12... | collective-permute-start | bytes 983048 | tf_op jit(solution)/shard_map/ppermute | solution.py:435
  78.0 0.6 collective-permute-start.20
  78.5 2.5 %shard_map.111 = (f32[5,512,256]{2,1,0:T(8,128)S(1)}, bf16[5,512,128]{2,1,0:T(8,128)(2,1)S(1)}) custom-call(bf16[4,128,640]{2,1,0:T(8,128)(2,1)S(1)} %copy-done.1, f32[5,512,256]{2,1,0:T(8,128)S(1)} %get-tuple-element.50.refs_1_, bf16[5,512,128]{2,1,0:T(8,128)(2,1)S(1)} %get-tuple-element.51.refs_2_, bf16[256,640]{1,0:T(8,128)(2,1)S(1)} %shard_map.110.refs_3_.refs_6_, ...), custom_call_target="tpu_custom_call" | custom-call | flops 1006632960 | bytes 8388608 | tf_op jit(solution)/shard_map/pallas_call | solution.py:396
  81.1 3.0 %collective-permute-start.18 = (bf16[256,640]{1,0:T(8,128)(2,1)S(1)}, bf16[256,640]{1,0:T(8,128)(2,1)S(1)}, u32[]{:S(2)}, u32[]{:S(2)}) collective-permute-start(bf16[256,640]{1,0:T(8,128)(2,1)S(1)} %collective-permute-done.12.refs_3_.refs_10_), channel_id=1, source_target_pairs={{0,8},{8,16},{16,24},{24,32},{32,40},{40,48},{48,56},{56,0},{64,12... | collective-permute-start | bytes 983048 | tf_op jit(solution)/shard_map/ppermute | solution.py:435
  84.1 2.7 %collective-permute-start.23 = (bf16[256,640]{1,0:T(8,128)(2,1)S(1)}, bf16[256,640]{1,0:T(8,128)(2,1)S(1)}, u32[]{:S(2)}, u32[]{:S(2)}) collective-permute-start(bf16[256,640]{1,0:T(8,128)(2,1)S(1)} %collective-permute-done.22.refs_5_.refs_8_), channel_id=1, source_target_pairs={{0,64},{64,0},{128,192},{192,128},{1,65},{65,1},{129,193},{193,129... | collective-permute-start | bytes 983048 | tf_op jit(solution)/shard_map/ppermute | solution.py:438
  86.8 1.8 %shard_map.112 = (f32[5,512,256]{2,1,0:T(8,128)S(1)}, bf16[5,512,128]{2,1,0:T(8,128)(2,1)S(1)}) custom-call(bf16[4,128,640]{2,1,0:T(8,128)(2,1)S(1)} %copy-done.1, f32[5,512,256]{2,1,0:T(8,128)S(1)} %get-tuple-element.55.refs_1_, bf16[5,512,128]{2,1,0:T(8,128)(2,1)S(1)} %get-tuple-element.56.refs_2_, ...), custom_call_target="tpu_custom_call" | custom-call | flops 671088640 | bytes 8388608 | tf_op jit(solution)/shard_map/pallas_call | solution.py:396
  88.7 0.0 copy-start.12
  88.7 2.9 %collective-permute-start.24 = (bf16[256,640]{1,0:T(8,128)(2,1)S(1)}, bf16[256,640]{1,0:T(8,128)(2,1)S(1)}, u32[]{:S(2)}, u32[]{:S(2)}) collective-permute-start(bf16[256,640]{1,0:T(8,128)(2,1)S(1)} %collective-permute-done.18.refs_4_.refs_7_), channel_id=1, source_target_pairs={{0,64},{64,0},{128,192},{192,128},{1,65},{65,1},{129,193},{193,129... | collective-permute-start | bytes 983048 | tf_op jit(solution)/shard_map/ppermute | solution.py:438
  91.6 1.8 %shard_map.113 = (f32[5,512,256]{2,1,0:T(8,128)S(1)}, bf16[5,512,128]{2,1,0:T(8,128)(2,1)S(1)}) custom-call(bf16[4,128,640]{2,1,0:T(8,128)(2,1)S(1)} %copy-done.1, f32[5,512,256]{2,1,0:T(8,128)S(1)} %get-tuple-element.60.refs_1_, bf16[5,512,128]{2,1,0:T(8,128)(2,1)S(1)} %get-tuple-element.61.refs_2_, ...), custom_call_target="tpu_custom_call" | custom-call | flops 671088640 | bytes 8388608 | tf_op jit(solution)/shard_map/pallas_call | solution.py:396
  93.5 2.6 %shard_map.114 = bf16[4,128,640]{2,1,0:T(8,128)(2,1)} custom-call(s32[4]{0:T(128)S(1)} %copy-done.12, bf16[4,128,640]{2,1,0:T(8,128)(2,1)S(1)} %copy-done.1, f32[5,512,256]{2,1,0:T(8,128)S(1)} %get-tuple-element.62.refs_2_, bf16[5,512,128]{2,1,0:T(8,128)(2,1)S(1)} %get-tuple-element.63.refs_3_, bf16[256,640]{1,0:T(8,128)(2,1)S(1)} %collective-permute-done.18.refs_4_.refs_7_, ...), custom_call_target="tpu_custom_call" | custom-call | flops 335544320 | bytes 8388608 | tf_op jit(solution)/shard_map/pallas_call | solution.py:396
  (27 shorter events, 0.1 us)
Async XLA Ops:
  0.0 10.8 %collective-permute-start = (bf16[1024,1152]{1,0:T(8,128)(2,1)}, bf16[1024,1152]{1,0:T(8,128)(2,1)S(1)}, u32[]{:S(2)}, u32[]{:S(2)}) collective-permute-start(bf16[1024,1152]{1,0:T(8,128)(2,1)} %hidden.5), channel_id=1, source_target_pairs={{0,64},{64,0},{128,192},{192,128},{1,65},{65,1},{129,193},{193,129... | collective-permute-start | bytes 7077896 | tf_op jit(solution)/shard_map/ppermute | solution.py:438
  3.2 1.7 %copy-start = (bf16[1024,1152]{1,0:T(8,128)(2,1)S(1)}, bf16[1024,1152]{1,0:T(8,128)(2,1)}, u32[]{:S(2)}) copy-start(bf16[1024,1152]{1,0:T(8,128)(2,1)} %hidden.5) | copy-start | bytes 7077892
  4.9 1.4 %copy-start.2 = (bf16[1152,640]{1,0:T(8,128)(2,1)S(1)}, bf16[1152,640]{1,0:T(8,128)(2,1)}, u32[]{:S(2)}) copy-start(bf16[1152,640]{1,0:T(8,128)(2,1)} %rest_0_.3) | copy-start | bytes 4423684
  6.3 1.4 %copy-start.4 = (bf16[1152,640]{1,0:T(8,128)(2,1)S(1)}, bf16[1152,640]{1,0:T(8,128)(2,1)}, u32[]{:S(2)}) copy-start(bf16[1152,640]{1,0:T(8,128)(2,1)} %rest_1_.3) | copy-start | bytes 4423684
  7.7 0.7 copy-start.8
  8.4 0.7 copy-start.9
  9.0 0.7 copy-start.10
  9.7 1.4 %copy-start.3 = (bf16[1152,640]{1,0:T(8,128)(2,1)S(1)}, bf16[1152,640]{1,0:T(8,128)(2,1)}, u32[]{:S(2)}) copy-start(bf16[1152,640]{1,0:T(8,128)(2,1)} %rest_0_.3) | copy-start | bytes 4423684
  9.7 1.8 %copy-start.5 = (bf16[1152,640]{1,0:T(8,128)(2,1)S(1)}, bf16[1152,640]{1,0:T(8,128)(2,1)}, u32[]{:S(2)}) copy-start(bf16[1152,640]{1,0:T(8,128)(2,1)} %rest_1_.3) | copy-start | bytes 4423684
  13.7 8.9 %collective-permute-start.1 = (bf16[240,640]{1,0:T(8,128)(2,1)S(1)}, bf16[240,640]{1,0:T(8,128)(2,1)S(1)}, u32[]{:S(2)}, u32[]{:S(2)}) collective-permute-start(bf16[240,640]{1,0:T(8,128)(2,1)S(1)} %get-tuple-element.38), channel_id=1, source_target_pairs={{0,8},{8,16},{16,24},{24,32},{32,40},{40,48},{48,56},{56,0},{64,12... | collective-permute-start | bytes 921608 | tf_op jit(solution)/shard_map/ppermute | solution.py:435
  17.6 7.1 %collective-permute-start.5 = (bf16[240,640]{1,0:T(8,128)(2,1)S(1)}, bf16[240,640]{1,0:T(8,128)(2,1)S(1)}, u32[]{:S(2)}, u32[]{:S(2)}) collective-permute-start(bf16[240,640]{1,0:T(8,128)(2,1)S(1)} %get-tuple-element.45), channel_id=1, source_target_pairs={{0,8},{8,16},{16,24},{24,32},{32,40},{40,48},{48,56},{56,0},{64,12... | collective-permute-start | bytes 921608 | tf_op jit(solution)/shard_map/ppermute | solution.py:435
  22.6 12.7 %copy-start.1 = (bf16[4,128,640]{2,1,0:T(8,128)(2,1)S(1)}, bf16[4,128,640]{2,1,0:T(8,128)(2,1)}, u32[]{:S(2)}) copy-start(bf16[4,128,640]{2,1,0:T(8,128)(2,1)} %refs_1_.1) | copy-start | bytes 1966084
  22.6 12.7 %copy-start.6 = (bf16[4,128,640]{2,1,0:T(8,128)(2,1)S(1)}, bf16[4,128,640]{2,1,0:T(8,128)(2,1)}, u32[]{:S(2)}) copy-start(bf16[4,128,640]{2,1,0:T(8,128)(2,1)} %own_k.1) | copy-start | bytes 1966084
  22.6 12.6 %copy-start.7 = (bf16[4,128,640]{2,1,0:T(8,128)(2,1)S(1)}, bf16[4,128,640]{2,1,0:T(8,128)(2,1)}, u32[]{:S(2)}) copy-start(bf16[4,128,640]{2,1,0:T(8,128)(2,1)} %own_v.1) | copy-start | bytes 1966084
  22.7 6.1 %collective-permute-start.2 = (bf16[240,640]{1,0:T(8,128)(2,1)S(1)}, bf16[240,640]{1,0:T(8,128)(2,1)S(1)}, u32[]{:S(2)}, u32[]{:S(2)}) collective-permute-start(bf16[240,640]{1,0:T(8,128)(2,1)S(1)} %shard_map.103), channel_id=1, source_target_pairs={{0,8},{8,16},{16,24},{24,32},{32,40},{40,48},{48,56},{56,0},{64,12... | collective-permute-start | bytes 921608 | tf_op jit(solution)/shard_map/ppermute | solution.py:435
  24.8 7.3 %collective-permute-start.6 = (bf16[240,640]{1,0:T(8,128)(2,1)S(1)}, bf16[240,640]{1,0:T(8,128)(2,1)S(1)}, u32[]{:S(2)}, u32[]{:S(2)}) collective-permute-start(bf16[240,640]{1,0:T(8,128)(2,1)S(1)} %shard_map.107), channel_id=1, source_target_pairs={{0,8},{8,16},{16,24},{24,32},{32,40},{40,48},{48,56},{56,0},{64,12... | collective-permute-start | bytes 921608 | tf_op jit(solution)/shard_map/ppermute | solution.py:435
  28.9 11.3 %collective-permute-start.3 = (bf16[240,640]{1,0:T(8,128)(2,1)S(1)}, bf16[240,640]{1,0:T(8,128)(2,1)S(1)}, u32[]{:S(2)}, u32[]{:S(2)}) collective-permute-start(bf16[240,640]{1,0:T(8,128)(2,1)S(1)} %shard_map.104), channel_id=1, source_target_pairs={{0,8},{8,16},{16,24},{24,32},{32,40},{40,48},{48,56},{56,0},{64,12... | collective-permute-start | bytes 921608 | tf_op jit(solution)/shard_map/ppermute | solution.py:435
  32.2 23.0 %copy-start.11 = (s32[4]{0:T(128)S(1)}, s32[4]{0:T(128)}, u32[]{:S(2)}) copy-start(s32[4]{0:T(128)} %counts.7) | copy-start | bytes 52
  32.2 8.2 %collective-permute-start.7 = (bf16[240,640]{1,0:T(8,128)(2,1)S(1)}, bf16[240,640]{1,0:T(8,128)(2,1)S(1)}, u32[]{:S(2)}, u32[]{:S(2)}) collective-permute-start(bf16[240,640]{1,0:T(8,128)(2,1)S(1)} %shard_map.108), channel_id=1, source_target_pairs={{0,8},{8,16},{16,24},{24,32},{32,40},{40,48},{48,56},{56,0},{64,12... | collective-permute-start | bytes 921608 | tf_op jit(solution)/shard_map/ppermute | solution.py:435
  40.3 6.1 %collective-permute-start.4 = (bf16[240,640]{1,0:T(8,128)(2,1)S(1)}, bf16[240,640]{1,0:T(8,128)(2,1)S(1)}, u32[]{:S(2)}, u32[]{:S(2)}) collective-permute-start(bf16[240,640]{1,0:T(8,128)(2,1)S(1)} %shard_map.106), channel_id=1, source_target_pairs={{0,8},{8,16},{16,24},{24,32},{32,40},{40,48},{48,56},{56,0},{64,12... | collective-permute-start | bytes 921608 | tf_op jit(solution)/shard_map/ppermute | solution.py:435
  40.4 6.0 %collective-permute-start.8 = (bf16[240,640]{1,0:T(8,128)(2,1)S(1)}, bf16[240,640]{1,0:T(8,128)(2,1)S(1)}, u32[]{:S(2)}, u32[]{:S(2)}) collective-permute-start(bf16[240,640]{1,0:T(8,128)(2,1)S(1)} %collective-permute-done.7), channel_id=1, source_target_pairs={{0,64},{64,0},{128,192},{192,128},{1,65},{65,1},{129,193},{193,129... | collective-permute-start | bytes 921608 | tf_op jit(solution)/shard_map/ppermute | solution.py:438
  46.8 8.5 %collective-permute-start.9 = (bf16[224,640]{1,0:T(8,128)(2,1)S(1)}, bf16[224,640]{1,0:T(8,128)(2,1)S(1)}, u32[]{:S(2)}, u32[]{:S(2)}) collective-permute-start(bf16[224,640]{1,0:T(8,128)(2,1)S(1)} %shard_map.109.rows), channel_id=1, source_target_pairs={{0,128},{64,192},{128,0},{192,64},{1,129},{65,193},{129,1},{193,65... | collective-permute-start | bytes 860168 | tf_op jit(solution)/shard_map/ppermute | solution.py:459
  55.9 3.7 %collective-permute-start.13 = (bf16[256,640]{1,0:T(8,128)(2,1)S(1)}, bf16[256,640]{1,0:T(8,128)(2,1)S(1)}, u32[]{:S(2)}, u32[]{:S(2)}) collective-permute-start(bf16[256,640]{1,0:T(8,128)(2,1)S(1)} %shard_map.110.refs_3_.refs_6_), channel_id=1, source_target_pairs={{0,64},{64,0},{128,192},{192,128},{1,65},{65,1},{129,193},{193,129... | collective-permute-start | bytes 983048 | tf_op jit(solution)/shard_map/ppermute | solution.py:438
  58.4 6.2 %collective-permute-start.10 = (bf16[256,640]{1,0:T(8,128)(2,1)S(1)}, bf16[256,640]{1,0:T(8,128)(2,1)S(1)}, u32[]{:S(2)}, u32[]{:S(2)}) collective-permute-start(bf16[256,640]{1,0:T(8,128)(2,1)S(1)} %shard_map.110.refs_3_.refs_6_), channel_id=1, source_target_pairs={{0,8},{8,16},{16,24},{24,32},{32,40},{40,48},{48,56},{56,0},{64,12... | collective-permute-start | bytes 983048 | tf_op jit(solution)/shard_map/ppermute | solution.py:435
  59.6 8.5 %collective-permute-start.14 = (bf16[256,640]{1,0:T(8,128)(2,1)S(1)}, bf16[256,640]{1,0:T(8,128)(2,1)S(1)}, u32[]{:S(2)}, u32[]{:S(2)}) collective-permute-start(bf16[256,640]{1,0:T(8,128)(2,1)S(1)} %collective-permute-done.13.refs_4_.refs_5_), channel_id=1, source_target_pairs={{0,8},{8,16},{16,24},{24,32},{32,40},{40,48},{48,56},{56,0},{64,12... | collective-permute-start | bytes 983048 | tf_op jit(solution)/shard_map/ppermute | solution.py:435
  64.6 7.0 %collective-permute-start.11 = (bf16[256,640]{1,0:T(8,128)(2,1)S(1)}, bf16[256,640]{1,0:T(8,128)(2,1)S(1)}, u32[]{:S(2)}, u32[]{:S(2)}) collective-permute-start(bf16[256,640]{1,0:T(8,128)(2,1)S(1)} %collective-permute-done.10.refs_7_.refs_14_), channel_id=1, source_target_pairs={{0,8},{8,16},{16,24},{24,32},{32,40},{40,48},{48,56},{56,0},{64,12... | collective-permute-start | bytes 983048 | tf_op jit(solution)/shard_map/ppermute | solution.py:435
  68.1 7.0 %collective-permute-start.15 = (bf16[256,640]{1,0:T(8,128)(2,1)S(1)}, bf16[256,640]{1,0:T(8,128)(2,1)S(1)}, u32[]{:S(2)}, u32[]{:S(2)}) collective-permute-start(bf16[256,640]{1,0:T(8,128)(2,1)S(1)} %collective-permute-done.14.refs_9_.refs_12_), channel_id=1, source_target_pairs={{0,8},{8,16},{16,24},{24,32},{32,40},{40,48},{48,56},{56,0},{64,12... | collective-permute-start | bytes 983048 | tf_op jit(solution)/shard_map/ppermute | solution.py:435
  70.0 8.0 %collective-permute-start.16 = (bf16[256,640]{1,0:T(8,128)(2,1)S(1)}, bf16[256,640]{1,0:T(8,128)(2,1)S(1)}, u32[]{:S(2)}, u32[]{:S(2)}) collective-permute-start(bf16[256,640]{1,0:T(8,128)(2,1)S(1)} %collective-permute-done.10.refs_7_.refs_14_), channel_id=1, source_target_pairs={{0,64},{64,0},{128,192},{192,128},{1,65},{65,1},{129,193},{193,129... | collective-permute-start | bytes 983048 | tf_op jit(solution)/shard_map/ppermute | solution.py:438
  70.3 8.3 %collective-permute-start.17 = (bf16[256,640]{1,0:T(8,128)(2,1)S(1)}, bf16[256,640]{1,0:T(8,128)(2,1)S(1)}, u32[]{:S(2)}, u32[]{:S(2)}) collective-permute-start(bf16[256,640]{1,0:T(8,128)(2,1)S(1)} %collective-permute-done.14.refs_9_.refs_12_), channel_id=1, source_target_pairs={{0,64},{64,0},{128,192},{192,128},{1,65},{65,1},{129,193},{193,129... | collective-permute-start | bytes 983048 | tf_op jit(solution)/shard_map/ppermute | solution.py:438
  71.6 9.5 %collective-permute-start.12 = (bf16[256,640]{1,0:T(8,128)(2,1)S(1)}, bf16[256,640]{1,0:T(8,128)(2,1)S(1)}, u32[]{:S(2)}, u32[]{:S(2)}) collective-permute-start(bf16[256,640]{1,0:T(8,128)(2,1)S(1)} %collective-permute-done.11.refs_3_.refs_10_), channel_id=1, source_target_pairs={{0,8},{8,16},{16,24},{24,32},{32,40},{40,48},{48,56},{56,0},{64,12... | collective-permute-start | bytes 983048 | tf_op jit(solution)/shard_map/ppermute | solution.py:435
  73.6 13.2 %collective-permute-start.19 = (bf16[256,640]{1,0:T(8,128)(2,1)S(1)}, bf16[256,640]{1,0:T(8,128)(2,1)S(1)}, u32[]{:S(2)}, u32[]{:S(2)}) collective-permute-start(bf16[256,640]{1,0:T(8,128)(2,1)S(1)} %collective-permute-done.11.refs_3_.refs_10_), channel_id=1, source_target_pairs={{0,64},{64,0},{128,192},{192,128},{1,65},{65,1},{129,193},{193,129... | collective-permute-start | bytes 983048 | tf_op jit(solution)/shard_map/ppermute | solution.py:438
  75.1 9.0 %collective-permute-start.22 = (bf16[256,640]{1,0:T(8,128)(2,1)S(1)}, bf16[256,640]{1,0:T(8,128)(2,1)S(1)}, u32[]{:S(2)}, u32[]{:S(2)}) collective-permute-start(bf16[256,640]{1,0:T(8,128)(2,1)S(1)} %collective-permute-done.15.refs_5_.refs_8_), channel_id=1, source_target_pairs={{0,8},{8,16},{16,24},{24,32},{32,40},{40,48},{48,56},{56,0},{64,12... | collective-permute-start | bytes 983048 | tf_op jit(solution)/shard_map/ppermute | solution.py:435
  78.0 8.8 %collective-permute-start.20 = (bf16[256,640]{1,0:T(8,128)(2,1)S(1)}, bf16[256,640]{1,0:T(8,128)(2,1)S(1)}, u32[]{:S(2)}, u32[]{:S(2)}) collective-permute-start(bf16[256,640]{1,0:T(8,128)(2,1)S(1)} %collective-permute-done.15.refs_5_.refs_8_), channel_id=1, source_target_pairs={{0,64},{64,0},{128,192},{192,128},{1,65},{65,1},{129,193},{193,129... | collective-permute-start | bytes 983048 | tf_op jit(solution)/shard_map/ppermute | solution.py:438
  81.1 7.6 %collective-permute-start.18 = (bf16[256,640]{1,0:T(8,128)(2,1)S(1)}, bf16[256,640]{1,0:T(8,128)(2,1)S(1)}, u32[]{:S(2)}, u32[]{:S(2)}) collective-permute-start(bf16[256,640]{1,0:T(8,128)(2,1)S(1)} %collective-permute-done.12.refs_3_.refs_10_), channel_id=1, source_target_pairs={{0,8},{8,16},{16,24},{24,32},{32,40},{40,48},{48,56},{56,0},{64,12... | collective-permute-start | bytes 983048 | tf_op jit(solution)/shard_map/ppermute | solution.py:435
  84.1 7.5 %collective-permute-start.21 = (bf16[256,640]{1,0:T(8,128)(2,1)S(1)}, bf16[256,640]{1,0:T(8,128)(2,1)S(1)}, u32[]{:S(2)}, u32[]{:S(2)}) collective-permute-start(bf16[256,640]{1,0:T(8,128)(2,1)S(1)} %collective-permute-done.12.refs_3_.refs_10_), channel_id=1, source_target_pairs={{0,64},{64,0},{128,192},{192,128},{1,65},{65,1},{129,193},{193,129... | collective-permute-start | bytes 983048 | tf_op jit(solution)/shard_map/ppermute | solution.py:438
  84.1 7.5 %collective-permute-start.23 = (bf16[256,640]{1,0:T(8,128)(2,1)S(1)}, bf16[256,640]{1,0:T(8,128)(2,1)S(1)}, u32[]{:S(2)}, u32[]{:S(2)}) collective-permute-start(bf16[256,640]{1,0:T(8,128)(2,1)S(1)} %collective-permute-done.22.refs_5_.refs_8_), channel_id=1, source_target_pairs={{0,64},{64,0},{128,192},{192,128},{1,65},{65,1},{129,193},{193,129... | collective-permute-start | bytes 983048 | tf_op jit(solution)/shard_map/ppermute | solution.py:438
  88.7 4.8 %copy-start.12 = (s32[4]{0:T(128)S(1)}, s32[4]{0:T(128)}, u32[]{:S(2)}) copy-start(s32[4]{0:T(128)} %refs_0_.7) | copy-start | bytes 52
  88.7 4.8 %collective-permute-start.24 = (bf16[256,640]{1,0:T(8,128)(2,1)S(1)}, bf16[256,640]{1,0:T(8,128)(2,1)S(1)}, u32[]{:S(2)}, u32[]{:S(2)}) collective-permute-start(bf16[256,640]{1,0:T(8,128)(2,1)S(1)} %collective-permute-done.18.refs_4_.refs_7_), channel_id=1, source_target_pairs={{0,64},{64,0},{128,192},{192,128},{1,65},{65,1},{129,193},{193,129... | collective-permute-start | bytes 983048 | tf_op jit(solution)/shard_map/ppermute | solution.py:438

commit v5 on v4

--- a/solution.py
+++ b/solution.py
@@ -43,119 +43,157 @@
     return tail + jnp.concatenate([tail[4:], tail[:4]], axis=0)
 
 
-def affine_kernel(counts, hidden, gain, bias, key_weight, value_weight, *outs):
+def affine_kernel(counts, hidden, gain, bias, out):
     row = lax.broadcasted_iota(jnp.int32, (16, gain.shape[0]), 0) % 4
     affine = jnp.where(
         row == 2, gain[...][None, :], jnp.where(row == 3, bias[...][None, :], 0.0)
     )
-    affine = jnp.concatenate(split(affine), axis=0)
-    sums = []
-    for weight in (key_weight, value_weight):
-        total = jnp.dot(affine, weight[...], preferred_element_type=jnp.float32)
-        sums.append(sum(total[16 * n : 16 * n + TAIL] for n in range(3)))
-    own_is_first = lax.rem(lax.axis_index("store"), 2) == 0
-    outs[0][...] = jnp.where(own_is_first, sums[0], sums[1])
-    outs[1][...] = jnp.where(own_is_first, sums[1], sums[0])
-
-
-def project_affine(counts, hidden, gain, bias, key_weight, value_weight):
-    width, cols = key_weight.shape
+    for n, piece in enumerate(split(affine)):
+        out[16 * n : 16 * (n + 1), :] = piece
+
+
+def affine_rows(counts, hidden, gain, bias):
     vmem = pl.BlockSpec(memory_space=pltpu.VMEM)
     return pl.pallas_call(
         affine_kernel,
-        out_shape=[jax.ShapeDtypeStruct((TAIL, cols), jnp.float32)] * 2,
-        in_specs=[pl.BlockSpec(memory_space=pltpu.SMEM)] + [vmem] * 5,
-        out_specs=[vmem] * 2,
+        out_shape=jax.ShapeDtypeStruct((48, gain.shape[0]), jnp.bfloat16),
+        in_specs=[pl.BlockSpec(memory_space=pltpu.SMEM)] + [vmem] * 3,
+        out_specs=vmem,
         compiler_params=pltpu.CompilerParams(vmem_limit_bytes=32 * MIB),
         cost_estimate=pl.CostEstimate(
-            flops=4 * 48 * width * cols, bytes_accessed=6 * MIB, transcendentals=0
-        ),
-    )(counts, hidden, gain, bias, key_weight, value_weight)
-
-
-def projection_kernel(plan, counts, hidden, hidden_other, gain, *rest):
-    opening = len(plan) == 2
-    given, affine_sums = rest[:2], rest[2:4]
-    outs, (rows_in, weights) = list(rest[4:-2]), rest[-2:]
+            flops=48 * gain.shape[0], bytes_accessed=6 * MIB, transcendentals=0
+        ),
+    )(counts, hidden, gain, bias)
+
+
+def window(counts, hidden, hidden_other, step, rows_in):
     store = lax.axis_index("store")
-    me = lax.axis_index("req")
     core = lax.rem(store, 2)
     first_count = counts[store - core]
     units = (first_count + counts[store - core + 1]) // UNIT
-    low = store < 2
-    capacity, width = hidden.shape
+    own_is_first = core == 0
+    target = lax.rem(
+        lax.axis_index("req") + jnp.where(own_is_first, step, 8 - step), 8
+    )
+    base = target * units - jnp.where(store < 2, 0, MOST_UNITS - units)
+    for g in range(MOST_UNITS):
+        row = (base + g) * 16
+        in_first = row < first_count
+        at = jnp.where(in_first, row, row - first_count)
+        at = pl.multiple_of(jnp.clip(at, 0, hidden.shape[0] - 16), 16)
+        from_own = in_first == own_is_first
+        rows_in[pl.ds(g * 16, 16), :] = jnp.where(
+            from_own, hidden[pl.ds(at, 16), :], hidden_other[pl.ds(at, 16), :]
+        )
+
+
+def centred(rows_in, gain, cols):
+    wide = rows_in[...].astype(jnp.float32)
+    row_sum = jnp.sum(wide, axis=1, keepdims=True)
+    row_square = jnp.sum(wide * wide, axis=1, keepdims=True)
+    centre = row_sum * (1.0 / wide.shape[1])
+    left = ((wide - centre) * gain[...][None, :]).astype(jnp.bfloat16)
+    lane = lax.broadcasted_iota(jnp.int32, (SPAN, 128), 1) % 4
+    fill = jnp.zeros((256 - SPAN, 128), jnp.float32)
+    moments = jnp.concatenate(
+        [jnp.where(lane == 0, row_sum, jnp.where(lane == 1, row_square, 0.0)), fill], axis=0
+    )
+    moments = jnp.concatenate(
+        [jnp.transpose(moments[:128])[:TAIL], jnp.transpose(moments[128:])[:TAIL]], axis=1
+    )
+    moments = jnp.concatenate([moments, jnp.zeros((TAIL, cols - 256), jnp.float32)], axis=1)
+    return left, centre, moments
+
+
+def opening_kernel(
+    step,
+    side,
+    counts,
+    hidden,
+    hidden_other,
+    gain,
+    affine,
+    key_weight,
+    value_weight,
+    out,
+    affine_sum,
+    rows_in,
+):
+    cols = key_weight.shape[1]
+    window(counts, hidden, hidden_other, step, rows_in)
+    left, centre, moments = centred(rows_in, gain, cols)
+    left = jnp.concatenate([left, affine[...]], axis=0)
+
+    def project(weight):
+        sums = jnp.dot(left, weight[...], preferred_element_type=jnp.float32)
+        total = sum(sums[SPAN + 16 * n : SPAN + 16 * n + TAIL] for n in range(3))
+        affine_sum[...] = total
+        tail_row = lax.broadcasted_iota(jnp.int32, (TAIL, cols), 0) % 4
+        put_message(
+            out, sums[:SPAN] + centre * total[2:3], jnp.where(tail_row < 2, moments, total)
+        )
+
+    keys_here = lax.rem(lax.axis_index("store") + side, 2) == 0
+    for wanted, weight in ((True, key_weight), (False, value_weight)):
+        pl.when(keys_here == wanted)(functools.partial(project, weight))
+
+
+def open_chain(step, side, counts, *operands):
+    width = operands[0].shape[1]
+    cols = operands[-1].shape[1]
+    vmem = pl.BlockSpec(memory_space=pltpu.VMEM)
+    return pl.pallas_call(
+        functools.partial(opening_kernel, step, side),
+        out_shape=[
+            jax.ShapeDtypeStruct((SPAN + 16, cols), jnp.bfloat16),
+            jax.ShapeDtypeStruct((TAIL, cols), jnp.float32),
+        ],
+        in_specs=[pl.BlockSpec(memory_space=pltpu.SMEM)] + [vmem] * 6,
+        out_specs=[vmem] * 2,
+        scratch_shapes=[pltpu.VMEM((SPAN, width), jnp.bfloat16)],
+        compiler_params=pltpu.CompilerParams(vmem_limit_bytes=32 * MIB),
+        cost_estimate=pl.CostEstimate(
+            flops=2 * SPAN * width * cols, bytes_accessed=4 * MIB, transcendentals=0
+        ),
+    )(counts, *operands)
+
+
+def projection_kernel(plan, counts, hidden, hidden_other, gain, *rest):
+    given, affine_sums = rest[:2], rest[2:4]
+    outs, (rows_in, weights) = list(rest[4:-2]), rest[-2:]
     cols = weights.shape[2]
-    own_is_first = core == 0
-
-    @pl.when(own_is_first)
-    def _():
-        weights[0] = given[0][...]
-        weights[1] = given[1][...]
-
-    @pl.when(jnp.logical_not(own_is_first))
-    def _():
-        weights[0] = given[1][...]
-        weights[1] = given[0][...]
-
-    tail_row = lax.broadcasted_iota(jnp.int32, (TAIL, cols), 0)
-    lane = lax.broadcasted_iota(jnp.int32, (SPAN, 128), 1)
-    fill = jnp.zeros((256 - SPAN, 128), jnp.float32)
-    gains = gain[...][None, :]
+    own_is_first = lax.rem(lax.axis_index("store"), 2) == 0
+    for wanted in (True, False):
+
+        @pl.when(own_is_first == wanted)
+        def _():
+            weights[0] = given[0 if wanted else 1][...]
+            weights[1] = given[1 if wanted else 0][...]
+
+    tail_row = lax.broadcasted_iota(jnp.int32, (TAIL, cols), 0) % 4
     for step, sides in plan:
-        target = lax.rem(me + jnp.where(own_is_first, step, 8 - step), 8)
-        base = target * units - jnp.where(low, 0, MOST_UNITS - units)
-        for g in range(MOST_UNITS):
-            row = (base + g) * 16
-            in_first = row < first_count
-            at = jnp.where(in_first, row, row - first_count)
-            at = pl.multiple_of(jnp.clip(at, 0, capacity - 16), 16)
-            from_own = in_first == own_is_first
-            rows_in[pl.ds(g * 16, 16), :] = jnp.where(
-                from_own, hidden[pl.ds(at, 16), :], hidden_other[pl.ds(at, 16), :]
-            )
-        wide = rows_in[...].astype(jnp.float32)
-        row_sum = jnp.sum(wide, axis=1, keepdims=True)
-        row_square = jnp.sum(wide * wide, axis=1, keepdims=True)
-        centre = row_sum * (1.0 / width)
-        left = ((wide - centre) * gains).astype(jnp.bfloat16)
-        moments = jnp.concatenate(
-            [jnp.where(lane == 0, row_sum, jnp.where(lane == 1, row_square, 0.0)), fill], axis=0
-        )
-        moments = jnp.concatenate(
-            [jnp.transpose(moments[:128])[:TAIL], jnp.transpose(moments[128:])[:TAIL]], axis=1
-        )
-        moments = jnp.concatenate(
-            [moments, jnp.zeros((TAIL, cols - 256), jnp.float32)], axis=1
-        )
+        window(counts, hidden, hidden_other, step, rows_in)
+        left, centre, moments = centred(rows_in, gain, cols)
         for side in sides:
             out = outs.pop(0)
-            affine_sum = affine_sums[side][...]
-            block = (
+            total = affine_sums[side][...]
+            out[0:SPAN, :] = (
                 jnp.dot(left, weights[side], preferred_element_type=jnp.float32)
-                + centre * affine_sum[2:3]
+                + centre * total[2:3]
             )
-            tail = jnp.where(tail_row % 4 < 2, moments, affine_sum)
-            if opening:
-                put_message(out, block, tail)
-            else:
-                out[0:SPAN, :] = block
-                out[SPAN : SPAN + TAIL, :] = tail
+            out[SPAN : SPAN + TAIL, :] = jnp.where(tail_row < 2, moments, total)
 
 
 def project_rows(plan, counts, *operands):
-    capacity, width = operands[0].shape
-    cols = operands[3].shape[1]
+    width = operands[0].shape[1]
+    cols = operands[-1].shape[1]
     vmem = pl.BlockSpec(memory_space=pltpu.VMEM)
     pieces = sum(len(sides) for _, sides in plan)
-    if len(plan) == 2:
-        outs = [jax.ShapeDtypeStruct((SPAN + 16, cols), jnp.bfloat16)] * pieces
-    else:
-        outs = [jax.ShapeDtypeStruct((SPAN + TAIL, cols), jnp.float32)] * pieces
     return pl.pallas_call(
         functools.partial(projection_kernel, plan),
-        out_shape=outs,
+        out_shape=[jax.ShapeDtypeStruct((SPAN + TAIL, cols), jnp.float32)] * pieces,
         in_specs=[pl.BlockSpec(memory_space=pltpu.SMEM)] + [vmem] * len(operands),
-        out_specs=[vmem] * len(outs),
+        out_specs=[vmem] * pieces,
         scratch_shapes=[
             pltpu.VMEM((SPAN, width), jnp.bfloat16),
             pltpu.VMEM((2, width, cols), jnp.bfloat16),
@@ -439,21 +477,25 @@
 
     other_hidden = swap(hidden)
     weights = (key_weight, value_weight)
-    affine = project_affine(row_counts, hidden, ln_gain, ln_bias, *weights)
-    inputs = (row_counts, hidden, other_hidden, ln_gain, *weights, *affine)
-    total, rest = project_rows(((4, (0,)), (3, (1,))), *inputs)
+    affine = affine_rows(row_counts, hidden, ln_gain, ln_bias)
+    inputs = (row_counts, hidden, other_hidden, ln_gain)
+    total, affine_0 = open_chain(4, 0, *inputs, affine, *weights)
+    rest, affine_1 = open_chain(3, 1, *inputs, affine, *weights)
+    total = step(total)
+    rest = step(rest)
     f1, f2, s2, f3, s3, f4 = project_rows(
-        ((3, (0,)), (2, (0, 1)), (1, (0, 1)), (0, (0,))), *inputs
-    )
-
-    total = relay(step(total), f1)
-    rest = relay(step(rest), s2)
+        ((3, (0,)), (2, (0, 1)), (1, (0, 1)), (0, (0,))),
+        *inputs,
+        *weights,
+        affine_0,
+        affine_1,
+    )
+
+    total = relay(total, f1)
+    rest = relay(rest, s2)
     total = relay(step(total), f2)
     rest = relay(step(rest), s3)
-    state = attend_own(suffix_q, suffix_k, suffix_v)
-    total = step(total)
-    total, state = lax.optimization_barrier((total, state))
-    total = step(relay(total, f3))
+    total = step(relay(step(total), f3))
     rows = finish(f4, total, swap(step(rest)), depth)
 
     mine = merge(row_counts, rows, lax.ppermute(rows, "store", far))
@@ -461,6 +503,8 @@
     other = swap(mine)
     g1 = step(mine)
     h1 = step(other)
+    state = attend_own(suffix_q, suffix_k, suffix_v)
+    g1, state = lax.optimization_barrier((g1, state))
     xg1 = swap(g1)
     g2 = step(g1)
     xh1 = swap(h1)

time: 96.4 us -> 92.6 us (0.961)
  waiting for transfers between devices: 17.6 us -> 15.1 us
  local copies, waits for them, and re-layouts: 7.2 us -> 5.84 us
    ppermute x14, starting transfers between devices: 29.3 us -> 27 us  [step(): return lax.ppermute(array, ('store', 'req'), around)]
    ppermute x10, starting transfers between devices: 16.1 us -> 17.7 us  [swap(): return lax.ppermute(array, 'store', across)]
    ppermute x1, waiting for transfers between devices: 5.46 us -> 4.08 us  [per_device(): mine = merge(row_counts, rows, lax.ppermute(rows, 'store', far))]
    unnamed x26 -> x24, local copies, waits for them, and re-layouts: 7.2 us -> 5.84 us
    pallas_call x3 -> x4, Pallas kernels: 7.53 us -> 8.37 us  [the longest x1 4.26 us: project_rows(): pl.pallas_call(functools.partial(projection_kernel, plan), out_shape=[jax...]
  transfers between devices with their start and end apart: 25 -> 25, of which waited for: 9 -> 12; matrix products, arithmetic and copies ran while one was open for 0% -> 0% of each run, Pallas kernels for 17% -> 20%
where the time goes in v5:
time: 92.6 us; the launch traced here: 92.3 us
  starting transfers between devices  47.7 us (52%)
  Pallas kernels  23.5 us (25%)
  waiting for transfers between devices  15.1 us (16%)
  local copies, waits for them, and re-layouts  5.84 us (6%)
    ppermute x14, starting transfers between devices, step(): return lax.ppermute(array, ('store', 'req'), around)  27 us
    ppermute x10, starting transfers between devices, swap(): return lax.ppermute(array, 'store', across)  17.7 us
    ppermute x14, waiting for transfers between devices, step(): return lax.ppermute(array, ('store', 'req'), around)  10.9 us
    pallas_call x4, Pallas kernels, attend(): pl.pallas_call(functools.partial(stage_kernel, lengths is not None, len(p...  8.76 us
    unnamed x24, local copies, waits for them, and re-layouts  5.84 us
    pallas_call x1, Pallas kernels, attend_own(): pl.pallas_call(own_kernel, out_shape=[jax.ShapeDtypeStruct((heads, rows,...  4.92 us
    pallas_call x1, Pallas kernels, project_rows(): pl.pallas_call(functools.partial(projection_kernel, plan), out_shape=[jax...  4.26 us
    ppermute x1, waiting for transfers between devices, per_device(): mine = merge(row_counts, rows, lax.ppermute(rows, 'store', far))  4.08 us
  transfers between devices with their start and end apart: 25, of which 12 were waited for; matrix products, arithmetic and copies ran while one was open for 0% of the time, Pallas kernels for 20%

profile of v5, /device:TPU:1, one launch (start us, length us, event | category | flops | bytes accessed | tf_op | source)
XLA Modules:
  0.0 92.3 jit_solution(2401659620126231989)
XLA Ops:
  0.0 3.2 %collective-permute-start = (bf16[1024,1152]{1,0:T(8,128)(2,1)}, bf16[1024,1152]{1,0:T(8,128)(2,1)S(1)}, u32[]{:S(2)}, u32[]{:S(2)}) collective-permute-start(bf16[1024,1152]{1,0:T(8,128)(2,1)} %hidden.7), channel_id=1, source_target_pairs={{0,64},{64,0},{128,192},{192,128},{1,65},{65,1},{129,193},{193,129... | collective-permute-start | bytes 7077896 | tf_op jit(solution)/shard_map/ppermute | solution.py:476
  3.2 1.7 %copy-done = bf16[1024,1152]{1,0:T(8,128)(2,1)S(1)} copy-done((bf16[1024,1152]{1,0:T(8,128)(2,1)S(1)}, bf16[1024,1152]{1,0:T(8,128)(2,1)}, u32[]{:S(2)}) %copy-start) | copy-done | bytes 2359320
  4.9 0.7 copy-done.7
  5.6 0.7 copy-done.8
  6.3 0.7 copy-done.10
  7.0 0.6 shard_map.100.affine
  7.5 0.1 collective-permute-done.hidden_other
  7.6 0.7 copy-done.2
  8.3 1.4 %copy-done.3 = bf16[1152,640]{1,0:T(8,128)(2,1)S(1)} copy-done((bf16[1152,640]{1,0:T(8,128)(2,1)S(1)}, bf16[1152,640]{1,0:T(8,128)(2,1)}, u32[]{:S(2)}) %copy-start.3) | copy-done | bytes 1474584
  9.7 1.8 %shard_map.101 = (bf16[240,640]{1,0:T(8,128)(2,1)S(1)}, f32[8,640]{1,0:T(8,128)S(1)}) custom-call(s32[4]{0:T(128)S(1)} %copy-done.8, bf16[1024,1152]{1,0:T(8,128)(2,1)S(1)} %copy-done, bf16[1024,1152]{1,0:T(8,128)(2,1)S(1)} %collective-permute-done.hidden_other, f32[1152]{0:T(1024)S(1)} %copy-done.7, bf16[48,1152]{1,0:T(8,128)(2,1)S(1)} %shard_map.100.affine, ...), custom_call_target="tpu_custom_call" | custom-call | flops 330301440 | bytes 4194304 | tf_op jit(solution)/shard_map/pallas_call | solution.py:145
  11.5 0.0 copy-start.4
  11.5 3.9 %collective-permute-start.1 = (bf16[240,640]{1,0:T(8,128)(2,1)S(1)}, bf16[240,640]{1,0:T(8,128)(2,1)S(1)}, u32[]{:S(2)}, u32[]{:S(2)}) collective-permute-start(bf16[240,640]{1,0:T(8,128)(2,1)S(1)} %get-tuple-element.38), channel_id=1, source_target_pairs={{0,8},{8,16},{16,24},{24,32},{32,40},{40,48},{48,56},{56,0},{64,12... | collective-permute-start | bytes 921608 | tf_op jit(solution)/shard_map/ppermute | solution.py:473
  15.4 1.8 %shard_map.102 = (bf16[240,640]{1,0:T(8,128)(2,1)S(1)}, f32[8,640]{1,0:T(8,128)S(1)}) custom-call(s32[4]{0:T(128)S(1)} %copy-done.8, bf16[1024,1152]{1,0:T(8,128)(2,1)S(1)} %copy-done, bf16[1024,1152]{1,0:T(8,128)(2,1)S(1)} %collective-permute-done.hidden_other, f32[1152]{0:T(1024)S(1)} %copy-done.7, bf16[48,1152]{1,0:T(8,128)(2,1)S(1)} %shard_map.100.affine, ...), custom_call_target="tpu_custom_call" | custom-call | flops 330301440 | bytes 4194304 | tf_op jit(solution)/shard_map/pallas_call | solution.py:145
  17.2 0.8 collective-permute-start.5
  18.0 4.3 %shard_map.103 = (f32[232,640]{1,0:T(8,128)S(1)}, f32[232,640]{1,0:T(8,128)S(1)}, f32[232,640]{1,0:T(8,128)S(1)}, f32[232,640]{1,0:T(8,128)S(1)}, f32[232,640]{1,0:T(8,128)S(1)}, /*index=5*/f32[232,640]{1,0:T(8,128)S(1)}) custom-call(s32[4]{0:T(128)S(1)} %copy-done.8, bf16[1024,1152]{1,0:T(8,128)(2,1)S(1)} %copy-done, ...), custom_call_target="tpu_custom_call" | custom-call | flops 1981808640 | bytes 4194304 | tf_op jit(solution)/shard_map/pallas_call | solution.py:192
  22.3 0.1 shard_map.104
  22.4 0.8 collective-permute-start.2
  23.1 0.1 collective-permute-done.5.received
  23.3 0.1 shard_map.107
  23.4 0.0 copy-start.9
  23.4 2.4 %collective-permute-start.6 = (bf16[240,640]{1,0:T(8,128)(2,1)S(1)}, bf16[240,640]{1,0:T(8,128)(2,1)S(1)}, u32[]{:S(2)}, u32[]{:S(2)}) collective-permute-start(bf16[240,640]{1,0:T(8,128)(2,1)S(1)} %shard_map.107), channel_id=1, source_target_pairs={{0,8},{8,16},{16,24},{24,32},{32,40},{40,48},{48,56},{56,0},{64,12... | collective-permute-start | bytes 921608 | tf_op jit(solution)/shard_map/ppermute | solution.py:473
  25.8 2.6 %collective-permute-done.2.received = bf16[240,640]{1,0:T(8,128)(2,1)S(1)} collective-permute-done((bf16[240,640]{1,0:T(8,128)(2,1)S(1)}, bf16[240,640]{1,0:T(8,128)(2,1)S(1)}, u32[]{:S(2)}, u32[]{:S(2)}) %collective-permute-start.2) | collective-permute-done | bytes 307232 | tf_op jit(solution)/shard_map/ppermute | solution.py:473
  28.4 0.1 shard_map.105
  28.5 0.0 copy-start.1
  28.5 0.0 copy-start.5
  28.5 0.0 copy-start.6
  28.6 1.7 %collective-permute-start.3 = (bf16[240,640]{1,0:T(8,128)(2,1)S(1)}, bf16[240,640]{1,0:T(8,128)(2,1)S(1)}, u32[]{:S(2)}, u32[]{:S(2)}) collective-permute-start(bf16[240,640]{1,0:T(8,128)(2,1)S(1)} %shard_map.105), channel_id=1, source_target_pairs={{0,8},{8,16},{16,24},{24,32},{32,40},{40,48},{48,56},{56,0},{64,12... | collective-permute-start | bytes 921608 | tf_op jit(solution)/shard_map/ppermute | solution.py:473
  30.3 1.4 %collective-permute-done.6.received = bf16[240,640]{1,0:T(8,128)(2,1)S(1)} collective-permute-done((bf16[240,640]{1,0:T(8,128)(2,1)S(1)}, bf16[240,640]{1,0:T(8,128)(2,1)S(1)}, u32[]{:S(2)}, u32[]{:S(2)}) %collective-permute-start.6) | collective-permute-done | bytes 307232 | tf_op jit(solution)/shard_map/ppermute | solution.py:473
  31.7 0.1 shard_map.108
  31.7 1.9 %collective-permute-start.7 = (bf16[240,640]{1,0:T(8,128)(2,1)S(1)}, bf16[240,640]{1,0:T(8,128)(2,1)S(1)}, u32[]{:S(2)}, u32[]{:S(2)}) collective-permute-start(bf16[240,640]{1,0:T(8,128)(2,1)S(1)} %shard_map.108), channel_id=1, source_target_pairs={{0,8},{8,16},{16,24},{24,32},{32,40},{40,48},{48,56},{56,0},{64,12... | collective-permute-start | bytes 921608 | tf_op jit(solution)/shard_map/ppermute | solution.py:473
  33.7 1.3 %collective-permute-done.3.received = bf16[240,640]{1,0:T(8,128)(2,1)S(1)} collective-permute-done((bf16[240,640]{1,0:T(8,128)(2,1)S(1)}, bf16[240,640]{1,0:T(8,128)(2,1)S(1)}, u32[]{:S(2)}, u32[]{:S(2)}) %collective-permute-start.3) | collective-permute-done | bytes 307232 | tf_op jit(solution)/shard_map/ppermute | solution.py:473
  35.0 0.1 shard_map.106
  35.1 2.2 %collective-permute-start.4 = (bf16[240,640]{1,0:T(8,128)(2,1)S(1)}, bf16[240,640]{1,0:T(8,128)(2,1)S(1)}, u32[]{:S(2)}, u32[]{:S(2)}) collective-permute-start(bf16[240,640]{1,0:T(8,128)(2,1)S(1)} %shard_map.106), channel_id=1, source_target_pairs={{0,8},{8,16},{16,24},{24,32},{32,40},{40,48},{48,56},{56,0},{64,12... | collective-permute-start | bytes 921608 | tf_op jit(solution)/shard_map/ppermute | solution.py:473
  37.3 1.0 %collective-permute-done.7 = bf16[240,640]{1,0:T(8,128)(2,1)S(1)} collective-permute-done((bf16[240,640]{1,0:T(8,128)(2,1)S(1)}, bf16[240,640]{1,0:T(8,128)(2,1)S(1)}, u32[]{:S(2)}, u32[]{:S(2)}) %collective-permute-start.7) | collective-permute-done | bytes 307232 | tf_op jit(solution)/shard_map/ppermute | solution.py:473
  38.3 2.2 %collective-permute-start.8 = (bf16[240,640]{1,0:T(8,128)(2,1)S(1)}, bf16[240,640]{1,0:T(8,128)(2,1)S(1)}, u32[]{:S(2)}, u32[]{:S(2)}) collective-permute-start(bf16[240,640]{1,0:T(8,128)(2,1)S(1)} %collective-permute-done.7), channel_id=1, source_target_pairs={{0,64},{64,0},{128,192},{192,128},{1,65},{65,1},{129,193},{193,129... | collective-permute-start | bytes 921608 | tf_op jit(solution)/shard_map/ppermute | solution.py:476
  40.5 1.1 %collective-permute-done.4.ours = bf16[240,640]{1,0:T(8,128)(2,1)S(1)} collective-permute-done((bf16[240,640]{1,0:T(8,128)(2,1)S(1)}, bf16[240,640]{1,0:T(8,128)(2,1)S(1)}, u32[]{:S(2)}, u32[]{:S(2)}) %collective-permute-start.4) | collective-permute-done | bytes 307232 | tf_op jit(solution)/shard_map/ppermute | solution.py:473
  41.6 0.1 collective-permute-done.8.theirs
  41.7 0.4 shard_map.109.rows
  42.1 3.0 %collective-permute-start.9 = (bf16[224,640]{1,0:T(8,128)(2,1)S(1)}, bf16[224,640]{1,0:T(8,128)(2,1)S(1)}, u32[]{:S(2)}, u32[]{:S(2)}) collective-permute-start(bf16[224,640]{1,0:T(8,128)(2,1)S(1)} %shard_map.109.rows), channel_id=1, source_target_pairs={{0,128},{64,192},{128,0},{192,64},{1,129},{65,193},{129,1},{193,65... | collective-permute-start | bytes 860168 | tf_op jit(solution)/shard_map/ppermute | solution.py:501
  45.1 4.1 %collective-permute-done.9.rows_far = bf16[224,640]{1,0:T(8,128)(2,1)S(1)} collective-permute-done((bf16[224,640]{1,0:T(8,128)(2,1)S(1)}, bf16[224,640]{1,0:T(8,128)(2,1)S(1)}, u32[]{:S(2)}, u32[]{:S(2)}) %collective-permute-start.9) | collective-permute-done | bytes 286752 | tf_op jit(solution)/shard_map/ppermute | solution.py:501
  49.2 0.6 shard_map.110.refs_3_.refs_6_
  49.8 4.8 %collective-permute-start.13 = (bf16[256,640]{1,0:T(8,128)(2,1)S(1)}, bf16[256,640]{1,0:T(8,128)(2,1)S(1)}, u32[]{:S(2)}, u32[]{:S(2)}) collective-permute-start(bf16[256,640]{1,0:T(8,128)(2,1)S(1)} %shard_map.110.refs_3_.refs_6_), channel_id=1, source_target_pairs={{0,64},{64,0},{128,192},{192,128},{1,65},{65,1},{129,193},{193,129... | collective-permute-start | bytes 983048 | tf_op jit(solution)/shard_map/ppermute | solution.py:476
  54.6 1.6 %collective-permute-start.10 = (bf16[256,640]{1,0:T(8,128)(2,1)S(1)}, bf16[256,640]{1,0:T(8,128)(2,1)S(1)}, u32[]{:S(2)}, u32[]{:S(2)}) collective-permute-start(bf16[256,640]{1,0:T(8,128)(2,1)S(1)} %shard_map.110.refs_3_.refs_6_), channel_id=1, source_target_pairs={{0,8},{8,16},{16,24},{24,32},{32,40},{40,48},{48,56},{56,0},{64,12... | collective-permute-start | bytes 983048 | tf_op jit(solution)/shard_map/ppermute | solution.py:473
  56.2 0.0 collective-permute-done.13.refs_4_.refs_5_
  56.2 1.3 %collective-permute-start.14 = (bf16[256,640]{1,0:T(8,128)(2,1)S(1)}, bf16[256,640]{1,0:T(8,128)(2,1)S(1)}, u32[]{:S(2)}, u32[]{:S(2)}) collective-permute-start(bf16[256,640]{1,0:T(8,128)(2,1)S(1)} %collective-permute-done.13.refs_4_.refs_5_), channel_id=1, source_target_pairs={{0,8},{8,16},{16,24},{24,32},{32,40},{40,48},{48,56},{56,0},{64,12... | collective-permute-start | bytes 983048 | tf_op jit(solution)/shard_map/ppermute | solution.py:473
  57.5 4.9 %shard_map.111 = (f32[5,512,256]{2,1,0:T(8,128)S(1)}, bf16[5,512,128]{2,1,0:T(8,128)(2,1)S(1)}) custom-call(bf16[4,128,640]{2,1,0:T(8,128)(2,1)S(1)} %copy-done.1, bf16[4,128,640]{2,1,0:T(8,128)(2,1)S(1)} %copy-done.5, bf16[4,128,640]{2,1,0:T(8,128)(2,1)S(1)} %copy-done.6), custom_call_target="tpu_custom_call" | custom-call | flops 167772160 | bytes 6291456 | tf_op jit(solution)/shard_map/pallas_call | solution.py:403
  62.4 0.9 %collective-permute-start.11 = (bf16[256,640]{1,0:T(8,128)(2,1)S(1)}, bf16[256,640]{1,0:T(8,128)(2,1)S(1)}, u32[]{:S(2)}, u32[]{:S(2)}) collective-permute-start(bf16[256,640]{1,0:T(8,128)(2,1)S(1)} %collective-permute-done.10.refs_7_.refs_14_), channel_id=1, source_target_pairs={{0,8},{8,16},{16,24},{24,32},{32,40},{40,48},{48,56},{56,0},{64,12... | collective-permute-start | bytes 983048 | tf_op jit(solution)/shard_map/ppermute | solution.py:473
  63.4 1.0 %collective-permute-done.14.refs_9_.refs_12_ = bf16[256,640]{1,0:T(8,128)(2,1)S(1)} collective-permute-done((bf16[256,640]{1,0:T(8,128)(2,1)S(1)}, bf16[256,640]{1,0:T(8,128)(2,1)S(1)}, u32[]{:S(2)}, u32[]{:S(2)}) %collective-permute-start.14) | collective-permute-done | bytes 327712 | tf_op jit(solution)/shard_map/ppermute | solution.py:473
  64.3 2.5 %collective-permute-start.15 = (bf16[256,640]{1,0:T(8,128)(2,1)S(1)}, bf16[256,640]{1,0:T(8,128)(2,1)S(1)}, u32[]{:S(2)}, u32[]{:S(2)}) collective-permute-start(bf16[256,640]{1,0:T(8,128)(2,1)S(1)} %collective-permute-done.14.refs_9_.refs_12_), channel_id=1, source_target_pairs={{0,8},{8,16},{16,24},{24,32},{32,40},{40,48},{48,56},{56,0},{64,12... | collective-permute-start | bytes 983048 | tf_op jit(solution)/shard_map/ppermute | solution.py:473
  66.9 0.5 collective-permute-start.17
  67.4 1.3 %collective-permute-done.11.refs_3_.refs_10_ = bf16[256,640]{1,0:T(8,128)(2,1)S(1)} collective-permute-done((bf16[256,640]{1,0:T(8,128)(2,1)S(1)}, bf16[256,640]{1,0:T(8,128)(2,1)S(1)}, u32[]{:S(2)}, u32[]{:S(2)}) %collective-permute-start.11) | collective-permute-done | bytes 327712 | tf_op jit(solution)/shard_map/ppermute | solution.py:473
  68.7 1.8 %collective-permute-start.12 = (bf16[256,640]{1,0:T(8,128)(2,1)S(1)}, bf16[256,640]{1,0:T(8,128)(2,1)S(1)}, u32[]{:S(2)}, u32[]{:S(2)}) collective-permute-start(bf16[256,640]{1,0:T(8,128)(2,1)S(1)} %collective-permute-done.11.refs_3_.refs_10_), channel_id=1, source_target_pairs={{0,8},{8,16},{16,24},{24,32},{32,40},{40,48},{48,56},{56,0},{64,12... | collective-permute-start | bytes 983048 | tf_op jit(solution)/shard_map/ppermute | solution.py:473
  70.5 0.8 collective-permute-start.19
  71.3 1.0 %collective-permute-done.15.refs_5_.refs_8_ = bf16[256,640]{1,0:T(8,128)(2,1)S(1)} collective-permute-done((bf16[256,640]{1,0:T(8,128)(2,1)S(1)}, bf16[256,640]{1,0:T(8,128)(2,1)S(1)}, u32[]{:S(2)}, u32[]{:S(2)}) %collective-permute-start.15) | collective-permute-done | bytes 327712 | tf_op jit(solution)/shard_map/ppermute | solution.py:473
  72.2 2.0 %collective-permute-start.22 = (bf16[256,640]{1,0:T(8,128)(2,1)S(1)}, bf16[256,640]{1,0:T(8,128)(2,1)S(1)}, u32[]{:S(2)}, u32[]{:S(2)}) collective-permute-start(bf16[256,640]{1,0:T(8,128)(2,1)S(1)} %collective-permute-done.15.refs_5_.refs_8_), channel_id=1, source_target_pairs={{0,8},{8,16},{16,24},{24,32},{32,40},{40,48},{48,56},{56,0},{64,12... | collective-permute-start | bytes 983048 | tf_op jit(solution)/shard_map/ppermute | solution.py:473
  74.2 0.6 collective-permute-start.20
  74.8 2.5 %shard_map.112 = (f32[5,512,256]{2,1,0:T(8,128)S(1)}, bf16[5,512,128]{2,1,0:T(8,128)(2,1)S(1)}) custom-call(bf16[4,128,640]{2,1,0:T(8,128)(2,1)S(1)} %copy-done.1, f32[5,512,256]{2,1,0:T(8,128)S(1)} %get-tuple-element.50.refs_1_, bf16[5,512,128]{2,1,0:T(8,128)(2,1)S(1)} %get-tuple-element.51.refs_2_, bf16[256,640]{1,0:T(8,128)(2,1)S(1)} %shard_map.110.refs_3_.refs_6_, ...), custom_call_target="tpu_custom_call" | custom-call | flops 1006632960 | bytes 8388608 | tf_op jit(solution)/shard_map/pallas_call | solution.py:434
  77.3 3.0 %collective-permute-start.18 = (bf16[256,640]{1,0:T(8,128)(2,1)S(1)}, bf16[256,640]{1,0:T(8,128)(2,1)S(1)}, u32[]{:S(2)}, u32[]{:S(2)}) collective-permute-start(bf16[256,640]{1,0:T(8,128)(2,1)S(1)} %collective-permute-done.12.refs_3_.refs_10_), channel_id=1, source_target_pairs={{0,8},{8,16},{16,24},{24,32},{32,40},{40,48},{48,56},{56,0},{64,12... | collective-permute-start | bytes 983048 | tf_op jit(solution)/shard_map/ppermute | solution.py:473
  80.3 2.7 %collective-permute-start.23 = (bf16[256,640]{1,0:T(8,128)(2,1)S(1)}, bf16[256,640]{1,0:T(8,128)(2,1)S(1)}, u32[]{:S(2)}, u32[]{:S(2)}) collective-permute-start(bf16[256,640]{1,0:T(8,128)(2,1)S(1)} %collective-permute-done.22.refs_5_.refs_8_), channel_id=1, source_target_pairs={{0,64},{64,0},{128,192},{192,128},{1,65},{65,1},{129,193},{193,129... | collective-permute-start | bytes 983048 | tf_op jit(solution)/shard_map/ppermute | solution.py:476
  83.1 1.8 %shard_map.113 = (f32[5,512,256]{2,1,0:T(8,128)S(1)}, bf16[5,512,128]{2,1,0:T(8,128)(2,1)S(1)}) custom-call(bf16[4,128,640]{2,1,0:T(8,128)(2,1)S(1)} %copy-done.1, f32[5,512,256]{2,1,0:T(8,128)S(1)} %get-tuple-element.55.refs_1_, bf16[5,512,128]{2,1,0:T(8,128)(2,1)S(1)} %get-tuple-element.56.refs_2_, ...), custom_call_target="tpu_custom_call" | custom-call | flops 671088640 | bytes 8388608 | tf_op jit(solution)/shard_map/pallas_call | solution.py:434
  84.9 0.0 copy-start.11
  84.9 2.9 %collective-permute-start.24 = (bf16[256,640]{1,0:T(8,128)(2,1)S(1)}, bf16[256,640]{1,0:T(8,128)(2,1)S(1)}, u32[]{:S(2)}, u32[]{:S(2)}) collective-permute-start(bf16[256,640]{1,0:T(8,128)(2,1)S(1)} %collective-permute-done.18.refs_4_.refs_7_), channel_id=1, source_target_pairs={{0,64},{64,0},{128,192},{192,128},{1,65},{65,1},{129,193},{193,129... | collective-permute-start | bytes 983048 | tf_op jit(solution)/shard_map/ppermute | solution.py:476
  87.9 1.8 %shard_map.114 = (f32[5,512,256]{2,1,0:T(8,128)S(1)}, bf16[5,512,128]{2,1,0:T(8,128)(2,1)S(1)}) custom-call(bf16[4,128,640]{2,1,0:T(8,128)(2,1)S(1)} %copy-done.1, f32[5,512,256]{2,1,0:T(8,128)S(1)} %get-tuple-element.60.refs_1_, bf16[5,512,128]{2,1,0:T(8,128)(2,1)S(1)} %get-tuple-element.61.refs_2_, ...), custom_call_target="tpu_custom_call" | custom-call | flops 671088640 | bytes 8388608 | tf_op jit(solution)/shard_map/pallas_call | solution.py:434
  89.7 2.6 %shard_map.115 = bf16[4,128,640]{2,1,0:T(8,128)(2,1)} custom-call(s32[4]{0:T(128)S(1)} %copy-done.11, bf16[4,128,640]{2,1,0:T(8,128)(2,1)S(1)} %copy-done.1, f32[5,512,256]{2,1,0:T(8,128)S(1)} %get-tuple-element.62.refs_2_, bf16[5,512,128]{2,1,0:T(8,128)(2,1)S(1)} %get-tuple-element.63.refs_3_, bf16[256,640]{1,0:T(8,128)(2,1)S(1)} %collective-permute-done.18.refs_4_.refs_7_, ...), custom_call_target="tpu_custom_call" | custom-call | flops 335544320 | bytes 8388608 | tf_op jit(solution)/shard_map/pallas_call | solution.py:434
  (26 shorter events, 0.1 us)
Async XLA Ops:
  0.0 7.6 %collective-permute-start = (bf16[1024,1152]{1,0:T(8,128)(2,1)}, bf16[1024,1152]{1,0:T(8,128)(2,1)S(1)}, u32[]{:S(2)}, u32[]{:S(2)}) collective-permute-start(bf16[1024,1152]{1,0:T(8,128)(2,1)} %hidden.7), channel_id=1, source_target_pairs={{0,64},{64,0},{128,192},{192,128},{1,65},{65,1},{129,193},{193,129... | collective-permute-start | bytes 7077896 | tf_op jit(solution)/shard_map/ppermute | solution.py:476
  3.2 1.7 %copy-start = (bf16[1024,1152]{1,0:T(8,128)(2,1)S(1)}, bf16[1024,1152]{1,0:T(8,128)(2,1)}, u32[]{:S(2)}) copy-start(bf16[1024,1152]{1,0:T(8,128)(2,1)} %hidden.7) | copy-start | bytes 7077892
  4.9 0.7 copy-start.7
  5.6 0.7 copy-start.8
  6.3 0.7 copy-start.10
  7.0 1.4 %copy-start.2 = (bf16[1152,640]{1,0:T(8,128)(2,1)S(1)}, bf16[1152,640]{1,0:T(8,128)(2,1)}, u32[]{:S(2)}) copy-start(bf16[1152,640]{1,0:T(8,128)(2,1)} %rest_0_.1) | copy-start | bytes 4423684
  8.3 1.4 %copy-start.3 = (bf16[1152,640]{1,0:T(8,128)(2,1)S(1)}, bf16[1152,640]{1,0:T(8,128)(2,1)}, u32[]{:S(2)}) copy-start(bf16[1152,640]{1,0:T(8,128)(2,1)} %rest_1_.1) | copy-start | bytes 4423684
  11.5 6.5 %copy-start.4 = (bf16[1152,640]{1,0:T(8,128)(2,1)S(1)}, bf16[1152,640]{1,0:T(8,128)(2,1)}, u32[]{:S(2)}) copy-start(bf16[1152,640]{1,0:T(8,128)(2,1)} %rest_1_.1) | copy-start | bytes 4423684
  11.5 10.8 %collective-permute-start.1 = (bf16[240,640]{1,0:T(8,128)(2,1)S(1)}, bf16[240,640]{1,0:T(8,128)(2,1)S(1)}, u32[]{:S(2)}, u32[]{:S(2)}) collective-permute-start(bf16[240,640]{1,0:T(8,128)(2,1)S(1)} %get-tuple-element.38), channel_id=1, source_target_pairs={{0,8},{8,16},{16,24},{24,32},{32,40},{40,48},{48,56},{56,0},{64,12... | collective-permute-start | bytes 921608 | tf_op jit(solution)/shard_map/ppermute | solution.py:473
  17.2 6.1 %collective-permute-start.5 = (bf16[240,640]{1,0:T(8,128)(2,1)S(1)}, bf16[240,640]{1,0:T(8,128)(2,1)S(1)}, u32[]{:S(2)}, u32[]{:S(2)}) collective-permute-start(bf16[240,640]{1,0:T(8,128)(2,1)S(1)} %get-tuple-element.42), channel_id=1, source_target_pairs={{0,8},{8,16},{16,24},{24,32},{32,40},{40,48},{48,56},{56,0},{64,12... | collective-permute-start | bytes 921608 | tf_op jit(solution)/shard_map/ppermute | solution.py:473
  22.4 6.1 %collective-permute-start.2 = (bf16[240,640]{1,0:T(8,128)(2,1)S(1)}, bf16[240,640]{1,0:T(8,128)(2,1)S(1)}, u32[]{:S(2)}, u32[]{:S(2)}) collective-permute-start(bf16[240,640]{1,0:T(8,128)(2,1)S(1)} %shard_map.104), channel_id=1, source_target_pairs={{0,8},{8,16},{16,24},{24,32},{32,40},{40,48},{48,56},{56,0},{64,12... | collective-permute-start | bytes 921608 | tf_op jit(solution)/shard_map/ppermute | solution.py:473
  23.4 25.8 %copy-start.9 = (s32[4]{0:T(128)S(1)}, s32[4]{0:T(128)}, u32[]{:S(2)}) copy-start(s32[4]{0:T(128)} %counts.9) | copy-start | bytes 52
  23.4 8.3 %collective-permute-start.6 = (bf16[240,640]{1,0:T(8,128)(2,1)S(1)}, bf16[240,640]{1,0:T(8,128)(2,1)S(1)}, u32[]{:S(2)}, u32[]{:S(2)}) collective-permute-start(bf16[240,640]{1,0:T(8,128)(2,1)S(1)} %shard_map.107), channel_id=1, source_target_pairs={{0,8},{8,16},{16,24},{24,32},{32,40},{40,48},{48,56},{56,0},{64,12... | collective-permute-start | bytes 921608 | tf_op jit(solution)/shard_map/ppermute | solution.py:473
  28.5 29.0 %copy-start.1 = (bf16[4,128,640]{2,1,0:T(8,128)(2,1)S(1)}, bf16[4,128,640]{2,1,0:T(8,128)(2,1)}, u32[]{:S(2)}) copy-start(bf16[4,128,640]{2,1,0:T(8,128)(2,1)} %refs_1_.1) | copy-start | bytes 1966084
  28.5 29.0 %copy-start.5 = (bf16[4,128,640]{2,1,0:T(8,128)(2,1)S(1)}, bf16[4,128,640]{2,1,0:T(8,128)(2,1)}, u32[]{:S(2)}) copy-start(bf16[4,128,640]{2,1,0:T(8,128)(2,1)} %own_k.1) | copy-start | bytes 1966084
  28.5 29.0 %copy-start.6 = (bf16[4,128,640]{2,1,0:T(8,128)(2,1)S(1)}, bf16[4,128,640]{2,1,0:T(8,128)(2,1)}, u32[]{:S(2)}) copy-start(bf16[4,128,640]{2,1,0:T(8,128)(2,1)} %own_v.1) | copy-start | bytes 1966084
  28.6 6.5 %collective-permute-start.3 = (bf16[240,640]{1,0:T(8,128)(2,1)S(1)}, bf16[240,640]{1,0:T(8,128)(2,1)S(1)}, u32[]{:S(2)}, u32[]{:S(2)}) collective-permute-start(bf16[240,640]{1,0:T(8,128)(2,1)S(1)} %shard_map.105), channel_id=1, source_target_pairs={{0,8},{8,16},{16,24},{24,32},{32,40},{40,48},{48,56},{56,0},{64,12... | collective-permute-start | bytes 921608 | tf_op jit(solution)/shard_map/ppermute | solution.py:473
  31.7 6.6 %collective-permute-start.7 = (bf16[240,640]{1,0:T(8,128)(2,1)S(1)}, bf16[240,640]{1,0:T(8,128)(2,1)S(1)}, u32[]{:S(2)}, u32[]{:S(2)}) collective-permute-start(bf16[240,640]{1,0:T(8,128)(2,1)S(1)} %shard_map.108), channel_id=1, source_target_pairs={{0,8},{8,16},{16,24},{24,32},{32,40},{40,48},{48,56},{56,0},{64,12... | collective-permute-start | bytes 921608 | tf_op jit(solution)/shard_map/ppermute | solution.py:473
  35.1 6.5 %collective-permute-start.4 = (bf16[240,640]{1,0:T(8,128)(2,1)S(1)}, bf16[240,640]{1,0:T(8,128)(2,1)S(1)}, u32[]{:S(2)}, u32[]{:S(2)}) collective-permute-start(bf16[240,640]{1,0:T(8,128)(2,1)S(1)} %shard_map.106), channel_id=1, source_target_pairs={{0,8},{8,16},{16,24},{24,32},{32,40},{40,48},{48,56},{56,0},{64,12... | collective-permute-start | bytes 921608 | tf_op jit(solution)/shard_map/ppermute | solution.py:473
  38.3 3.4 %collective-permute-start.8 = (bf16[240,640]{1,0:T(8,128)(2,1)S(1)}, bf16[240,640]{1,0:T(8,128)(2,1)S(1)}, u32[]{:S(2)}, u32[]{:S(2)}) collective-permute-start(bf16[240,640]{1,0:T(8,128)(2,1)S(1)} %collective-permute-done.7), channel_id=1, source_target_pairs={{0,64},{64,0},{128,192},{192,128},{1,65},{65,1},{129,193},{193,129... | collective-permute-start | bytes 921608 | tf_op jit(solution)/shard_map/ppermute | solution.py:476
  42.1 7.1 %collective-permute-start.9 = (bf16[224,640]{1,0:T(8,128)(2,1)S(1)}, bf16[224,640]{1,0:T(8,128)(2,1)S(1)}, u32[]{:S(2)}, u32[]{:S(2)}) collective-permute-start(bf16[224,640]{1,0:T(8,128)(2,1)S(1)} %shard_map.109.rows), channel_id=1, source_target_pairs={{0,128},{64,192},{128,0},{192,64},{1,129},{65,193},{129,1},{193,65... | collective-permute-start | bytes 860168 | tf_op jit(solution)/shard_map/ppermute | solution.py:501
  49.8 6.4 %collective-permute-start.13 = (bf16[256,640]{1,0:T(8,128)(2,1)S(1)}, bf16[256,640]{1,0:T(8,128)(2,1)S(1)}, u32[]{:S(2)}, u32[]{:S(2)}) collective-permute-start(bf16[256,640]{1,0:T(8,128)(2,1)S(1)} %shard_map.110.refs_3_.refs_6_), channel_id=1, source_target_pairs={{0,64},{64,0},{128,192},{192,128},{1,65},{65,1},{129,193},{193,129... | collective-permute-start | bytes 983048 | tf_op jit(solution)/shard_map/ppermute | solution.py:476
  54.6 7.8 %collective-permute-start.10 = (bf16[256,640]{1,0:T(8,128)(2,1)S(1)}, bf16[256,640]{1,0:T(8,128)(2,1)S(1)}, u32[]{:S(2)}, u32[]{:S(2)}) collective-permute-start(bf16[256,640]{1,0:T(8,128)(2,1)S(1)} %shard_map.110.refs_3_.refs_6_), channel_id=1, source_target_pairs={{0,8},{8,16},{16,24},{24,32},{32,40},{40,48},{48,56},{56,0},{64,12... | collective-permute-start | bytes 983048 | tf_op jit(solution)/shard_map/ppermute | solution.py:473
  56.2 8.1 %collective-permute-start.14 = (bf16[256,640]{1,0:T(8,128)(2,1)S(1)}, bf16[256,640]{1,0:T(8,128)(2,1)S(1)}, u32[]{:S(2)}, u32[]{:S(2)}) collective-permute-start(bf16[256,640]{1,0:T(8,128)(2,1)S(1)} %collective-permute-done.13.refs_4_.refs_5_), channel_id=1, source_target_pairs={{0,8},{8,16},{16,24},{24,32},{32,40},{40,48},{48,56},{56,0},{64,12... | collective-permute-start | bytes 983048 | tf_op jit(solution)/shard_map/ppermute | solution.py:473
  62.4 6.3 %collective-permute-start.11 = (bf16[256,640]{1,0:T(8,128)(2,1)S(1)}, bf16[256,640]{1,0:T(8,128)(2,1)S(1)}, u32[]{:S(2)}, u32[]{:S(2)}) collective-permute-start(bf16[256,640]{1,0:T(8,128)(2,1)S(1)} %collective-permute-done.10.refs_7_.refs_14_), channel_id=1, source_target_pairs={{0,8},{8,16},{16,24},{24,32},{32,40},{40,48},{48,56},{56,0},{64,12... | collective-permute-start | bytes 983048 | tf_op jit(solution)/shard_map/ppermute | solution.py:473
  64.3 7.9 %collective-permute-start.15 = (bf16[256,640]{1,0:T(8,128)(2,1)S(1)}, bf16[256,640]{1,0:T(8,128)(2,1)S(1)}, u32[]{:S(2)}, u32[]{:S(2)}) collective-permute-start(bf16[256,640]{1,0:T(8,128)(2,1)S(1)} %collective-permute-done.14.refs_9_.refs_12_), channel_id=1, source_target_pairs={{0,8},{8,16},{16,24},{24,32},{32,40},{40,48},{48,56},{56,0},{64,12... | collective-permute-start | bytes 983048 | tf_op jit(solution)/shard_map/ppermute | solution.py:473
  66.9 7.4 %collective-permute-start.16 = (bf16[256,640]{1,0:T(8,128)(2,1)S(1)}, bf16[256,640]{1,0:T(8,128)(2,1)S(1)}, u32[]{:S(2)}, u32[]{:S(2)}) collective-permute-start(bf16[256,640]{1,0:T(8,128)(2,1)S(1)} %collective-permute-done.10.refs_7_.refs_14_), channel_id=1, source_target_pairs={{0,64},{64,0},{128,192},{192,128},{1,65},{65,1},{129,193},{193,129... | collective-permute-start | bytes 983048 | tf_op jit(solution)/shard_map/ppermute | solution.py:476
  66.9 7.9 %collective-permute-start.17 = (bf16[256,640]{1,0:T(8,128)(2,1)S(1)}, bf16[256,640]{1,0:T(8,128)(2,1)S(1)}, u32[]{:S(2)}, u32[]{:S(2)}) collective-permute-start(bf16[256,640]{1,0:T(8,128)(2,1)S(1)} %collective-permute-done.14.refs_9_.refs_12_), channel_id=1, source_target_pairs={{0,64},{64,0},{128,192},{192,128},{1,65},{65,1},{129,193},{193,129... | collective-permute-start | bytes 983048 | tf_op jit(solution)/shard_map/ppermute | solution.py:476
  68.7 8.6 %collective-permute-start.12 = (bf16[256,640]{1,0:T(8,128)(2,1)S(1)}, bf16[256,640]{1,0:T(8,128)(2,1)S(1)}, u32[]{:S(2)}, u32[]{:S(2)}) collective-permute-start(bf16[256,640]{1,0:T(8,128)(2,1)S(1)} %collective-permute-done.11.refs_3_.refs_10_), channel_id=1, source_target_pairs={{0,8},{8,16},{16,24},{24,32},{32,40},{40,48},{48,56},{56,0},{64,12... | collective-permute-start | bytes 983048 | tf_op jit(solution)/shard_map/ppermute | solution.py:473
  70.5 12.6 %collective-permute-start.19 = (bf16[256,640]{1,0:T(8,128)(2,1)S(1)}, bf16[256,640]{1,0:T(8,128)(2,1)S(1)}, u32[]{:S(2)}, u32[]{:S(2)}) collective-permute-start(bf16[256,640]{1,0:T(8,128)(2,1)S(1)} %collective-permute-done.11.refs_3_.refs_10_), channel_id=1, source_target_pairs={{0,64},{64,0},{128,192},{192,128},{1,65},{65,1},{129,193},{193,129... | collective-permute-start | bytes 983048 | tf_op jit(solution)/shard_map/ppermute | solution.py:476
  72.2 8.1 %collective-permute-start.22 = (bf16[256,640]{1,0:T(8,128)(2,1)S(1)}, bf16[256,640]{1,0:T(8,128)(2,1)S(1)}, u32[]{:S(2)}, u32[]{:S(2)}) collective-permute-start(bf16[256,640]{1,0:T(8,128)(2,1)S(1)} %collective-permute-done.15.refs_5_.refs_8_), channel_id=1, source_target_pairs={{0,8},{8,16},{16,24},{24,32},{32,40},{40,48},{48,56},{56,0},{64,12... | collective-permute-start | bytes 983048 | tf_op jit(solution)/shard_map/ppermute | solution.py:473
  74.2 8.8 %collective-permute-start.20 = (bf16[256,640]{1,0:T(8,128)(2,1)S(1)}, bf16[256,640]{1,0:T(8,128)(2,1)S(1)}, u32[]{:S(2)}, u32[]{:S(2)}) collective-permute-start(bf16[256,640]{1,0:T(8,128)(2,1)S(1)} %collective-permute-done.15.refs_5_.refs_8_), channel_id=1, source_target_pairs={{0,64},{64,0},{128,192},{192,128},{1,65},{65,1},{129,193},{193,129... | collective-permute-start | bytes 983048 | tf_op jit(solution)/shard_map/ppermute | solution.py:476
  77.3 7.6 %collective-permute-start.18 = (bf16[256,640]{1,0:T(8,128)(2,1)S(1)}, bf16[256,640]{1,0:T(8,128)(2,1)S(1)}, u32[]{:S(2)}, u32[]{:S(2)}) collective-permute-start(bf16[256,640]{1,0:T(8,128)(2,1)S(1)} %collective-permute-done.12.refs_3_.refs_10_), channel_id=1, source_target_pairs={{0,8},{8,16},{16,24},{24,32},{32,40},{40,48},{48,56},{56,0},{64,12... | collective-permute-start | bytes 983048 | tf_op jit(solution)/shard_map/ppermute | solution.py:473
  80.3 7.5 %collective-permute-start.21 = (bf16[256,640]{1,0:T(8,128)(2,1)S(1)}, bf16[256,640]{1,0:T(8,128)(2,1)S(1)}, u32[]{:S(2)}, u32[]{:S(2)}) collective-permute-start(bf16[256,640]{1,0:T(8,128)(2,1)S(1)} %collective-permute-done.12.refs_3_.refs_10_), channel_id=1, source_target_pairs={{0,64},{64,0},{128,192},{192,128},{1,65},{65,1},{129,193},{193,129... | collective-permute-start | bytes 983048 | tf_op jit(solution)/shard_map/ppermute | solution.py:476
  80.3 7.5 %collective-permute-start.23 = (bf16[256,640]{1,0:T(8,128)(2,1)S(1)}, bf16[256,640]{1,0:T(8,128)(2,1)S(1)}, u32[]{:S(2)}, u32[]{:S(2)}) collective-permute-start(bf16[256,640]{1,0:T(8,128)(2,1)S(1)} %collective-permute-done.22.refs_5_.refs_8_), channel_id=1, source_target_pairs={{0,64},{64,0},{128,192},{192,128},{1,65},{65,1},{129,193},{193,129... | collective-permute-start | bytes 983048 | tf_op jit(solution)/shard_map/ppermute | solution.py:476
  84.9 4.8 %copy-start.11 = (s32[4]{0:T(128)S(1)}, s32[4]{0:T(128)}, u32[]{:S(2)}) copy-start(s32[4]{0:T(128)} %refs_0_.7) | copy-start | bytes 52
  84.9 4.8 %collective-permute-start.24 = (bf16[256,640]{1,0:T(8,128)(2,1)S(1)}, bf16[256,640]{1,0:T(8,128)(2,1)S(1)}, u32[]{:S(2)}, u32[]{:S(2)}) collective-permute-start(bf16[256,640]{1,0:T(8,128)(2,1)S(1)} %collective-permute-done.18.refs_4_.refs_7_), channel_id=1, source_target_pairs={{0,64},{64,0},{128,192},{192,128},{1,65},{65,1},{129,193},{193,129... | collective-permute-start | bytes 983048 | tf_op jit(solution)/shard_map/ppermute | solution.py:476

commit v6 on v5

--- a/solution.py
+++ b/solution.py
@@ -43,27 +43,31 @@
     return tail + jnp.concatenate([tail[4:], tail[:4]], axis=0)
 
 
-def affine_kernel(counts, hidden, gain, bias, out):
-    row = lax.broadcasted_iota(jnp.int32, (16, gain.shape[0]), 0) % 4
-    affine = jnp.where(
-        row == 2, gain[...][None, :], jnp.where(row == 3, bias[...][None, :], 0.0)
-    )
-    for n, piece in enumerate(split(affine)):
-        out[16 * n : 16 * (n + 1), :] = piece
+def affine_kernel(place, *refs):
+    vector, previous, out = refs[-3:]
+    row = lax.broadcasted_iota(jnp.int32, (16, vector.shape[0]), 0) % 4
+    here = jnp.where(row == place, vector[...][None, :], 0.0)
+    for n, piece in enumerate(split(here)):
+        at = slice(16 * n, 16 * (n + 1))
+        out[at, :] = piece if place == 2 else previous[at, :] + piece
 
 
 def affine_rows(counts, hidden, gain, bias):
     vmem = pl.BlockSpec(memory_space=pltpu.VMEM)
-    return pl.pallas_call(
-        affine_kernel,
-        out_shape=jax.ShapeDtypeStruct((48, gain.shape[0]), jnp.bfloat16),
-        in_specs=[pl.BlockSpec(memory_space=pltpu.SMEM)] + [vmem] * 3,
-        out_specs=vmem,
-        compiler_params=pltpu.CompilerParams(vmem_limit_bytes=32 * MIB),
-        cost_estimate=pl.CostEstimate(
-            flops=48 * gain.shape[0], bytes_accessed=6 * MIB, transcendentals=0
-        ),
-    )(counts, hidden, gain, bias)
+
+    def call(place, *operands):
+        return pl.pallas_call(
+            functools.partial(affine_kernel, place),
+            out_shape=jax.ShapeDtypeStruct((48, gain.shape[0]), jnp.bfloat16),
+            in_specs=[pl.BlockSpec(memory_space=pltpu.SMEM)] + [vmem] * (len(operands) - 1),
+            out_specs=vmem,
+            compiler_params=pltpu.CompilerParams(vmem_limit_bytes=32 * MIB),
+            cost_estimate=pl.CostEstimate(
+                flops=48 * gain.shape[0], bytes_accessed=6 * MIB, transcendentals=0
+            ),
+        )(*operands)
+
+    return call(3, counts, hidden, gain, bias, call(2, counts, hidden, gain, hidden))
 
 
 def window(counts, hidden, hidden_other, step, rows_in):

time: 92.6 us -> 90.9 us (0.982)
  local copies, waits for them, and re-layouts: 5.84 us -> 3.65 us
    unnamed x24 -> x22, local copies, waits for them, and re-layouts: 5.84 us -> 3.65 us
  transfers between devices with their start and end apart: 25 -> 25, of which waited for: 12 -> 12; matrix products, arithmetic and copies ran while one was open for 0% -> 0% of each run, Pallas kernels for 20% -> 21%
where the time goes in v6:
time: 90.9 us; the launch traced here: 90.7 us
  starting transfers between devices  47.7 us (52%)
  Pallas kernels  24.1 us (27%)
  waiting for transfers between devices  15.1 us (17%)
  local copies, waits for them, and re-layouts  3.65 us (4%)
    ppermute x14, starting transfers between devices, step(): return lax.ppermute(array, ('store', 'req'), around)  27 us
    ppermute x10, starting transfers between devices, swap(): return lax.ppermute(array, 'store', across)  17.7 us
    ppermute x14, waiting for transfers between devices, step(): return lax.ppermute(array, ('store', 'req'), around)  10.9 us
    pallas_call x4, Pallas kernels, attend(): pl.pallas_call(functools.partial(stage_kernel, lengths is not None, len(p...  8.76 us
    pallas_call x1, Pallas kernels, attend_own(): pl.pallas_call(own_kernel, out_shape=[jax.ShapeDtypeStruct((heads, rows,...  4.92 us
    pallas_call x1, Pallas kernels, project_rows(): pl.pallas_call(functools.partial(projection_kernel, plan), out_shape=[jax...  4.26 us
    ppermute x1, waiting for transfers between devices, per_device(): mine = merge(row_counts, rows, lax.ppermute(rows, 'store', far))  4.08 us
    unnamed x22, local copies, waits for them, and re-layouts  3.65 us
  transfers between devices with their start and end apart: 25, of which 12 were waited for; matrix products, arithmetic and copies ran while one was open for 0% of the time, Pallas kernels for 21%

profile of v6, /device:TPU:1, one launch (start us, length us, event | category | flops | bytes accessed | tf_op | source)
XLA Modules:
  0.0 90.7 jit_solution(11636668632058913483)
XLA Ops:
  0.0 3.2 %collective-permute-start = (bf16[1024,1152]{1,0:T(8,128)(2,1)}, bf16[1024,1152]{1,0:T(8,128)(2,1)S(1)}, u32[]{:S(2)}, u32[]{:S(2)}) collective-permute-start(bf16[1024,1152]{1,0:T(8,128)(2,1)} %hidden.5), channel_id=1, source_target_pairs={{0,64},{64,0},{128,192},{192,128},{1,65},{65,1},{129,193},{193,129... | collective-permute-start | bytes 7077896 | tf_op jit(solution)/shard_map/ppermute | solution.py:480
  3.2 1.7 %copy-done = bf16[1024,1152]{1,0:T(8,128)(2,1)S(1)} copy-done((bf16[1024,1152]{1,0:T(8,128)(2,1)S(1)}, bf16[1024,1152]{1,0:T(8,128)(2,1)}, u32[]{:S(2)}) %copy-start) | copy-done | bytes 2359320
  4.9 0.7 copy-done.6
  5.6 0.7 copy-done.7
  6.3 0.6 shard_map.100.refs_4_
  6.8 0.1 copy-done.9
  7.0 0.6 shard_map.101.affine
  7.5 0.1 collective-permute-done.hidden_other
  7.6 0.0 copy-done.2
  7.7 0.4 copy-done.3
  8.1 1.8 %shard_map.102 = (bf16[240,640]{1,0:T(8,128)(2,1)S(1)}, f32[8,640]{1,0:T(8,128)S(1)}) custom-call(s32[4]{0:T(128)S(1)} %copy-done.7, bf16[1024,1152]{1,0:T(8,128)(2,1)S(1)} %copy-done, bf16[1024,1152]{1,0:T(8,128)(2,1)S(1)} %collective-permute-done.hidden_other, f32[1152]{0:T(1024)S(1)} %copy-done.6, bf16[48,1152]{1,0:T(8,128)(2,1)S(1)} %shard_map.101.affine, ...), custom_call_target="tpu_custom_call" | custom-call | flops 330301440 | bytes 4194304 | tf_op jit(solution)/shard_map/pallas_call | solution.py:149
  9.9 3.9 %collective-permute-start.1 = (bf16[240,640]{1,0:T(8,128)(2,1)S(1)}, bf16[240,640]{1,0:T(8,128)(2,1)S(1)}, u32[]{:S(2)}, u32[]{:S(2)}) collective-permute-start(bf16[240,640]{1,0:T(8,128)(2,1)S(1)} %get-tuple-element.38), channel_id=1, source_target_pairs={{0,8},{8,16},{16,24},{24,32},{32,40},{40,48},{48,56},{56,0},{64,12... | collective-permute-start | bytes 921608 | tf_op jit(solution)/shard_map/ppermute | solution.py:477
  13.8 1.8 %shard_map.103 = (bf16[240,640]{1,0:T(8,128)(2,1)S(1)}, f32[8,640]{1,0:T(8,128)S(1)}) custom-call(s32[4]{0:T(128)S(1)} %copy-done.7, bf16[1024,1152]{1,0:T(8,128)(2,1)S(1)} %copy-done, bf16[1024,1152]{1,0:T(8,128)(2,1)S(1)} %collective-permute-done.hidden_other, f32[1152]{0:T(1024)S(1)} %copy-done.6, bf16[48,1152]{1,0:T(8,128)(2,1)S(1)} %shard_map.101.affine, ...), custom_call_target="tpu_custom_call" | custom-call | flops 330301440 | bytes 4194304 | tf_op jit(solution)/shard_map/pallas_call | solution.py:149
  15.6 0.8 collective-permute-start.5
  16.4 4.3 %shard_map.104 = (f32[232,640]{1,0:T(8,128)S(1)}, f32[232,640]{1,0:T(8,128)S(1)}, f32[232,640]{1,0:T(8,128)S(1)}, f32[232,640]{1,0:T(8,128)S(1)}, f32[232,640]{1,0:T(8,128)S(1)}, /*index=5*/f32[232,640]{1,0:T(8,128)S(1)}) custom-call(s32[4]{0:T(128)S(1)} %copy-done.7, bf16[1024,1152]{1,0:T(8,128)(2,1)S(1)} %copy-done, ...), custom_call_target="tpu_custom_call" | custom-call | flops 1981808640 | bytes 4194304 | tf_op jit(solution)/shard_map/pallas_call | solution.py:196
  20.7 0.1 shard_map.105
  20.7 0.8 collective-permute-start.2
  21.5 0.1 collective-permute-done.5.received
  21.7 0.1 shard_map.108
  21.7 0.0 copy-start.8
  21.8 2.4 %collective-permute-start.6 = (bf16[240,640]{1,0:T(8,128)(2,1)S(1)}, bf16[240,640]{1,0:T(8,128)(2,1)S(1)}, u32[]{:S(2)}, u32[]{:S(2)}) collective-permute-start(bf16[240,640]{1,0:T(8,128)(2,1)S(1)} %shard_map.108), channel_id=1, source_target_pairs={{0,8},{8,16},{16,24},{24,32},{32,40},{40,48},{48,56},{56,0},{64,12... | collective-permute-start | bytes 921608 | tf_op jit(solution)/shard_map/ppermute | solution.py:477
  24.2 2.6 %collective-permute-done.2.received = bf16[240,640]{1,0:T(8,128)(2,1)S(1)} collective-permute-done((bf16[240,640]{1,0:T(8,128)(2,1)S(1)}, bf16[240,640]{1,0:T(8,128)(2,1)S(1)}, u32[]{:S(2)}, u32[]{:S(2)}) %collective-permute-start.2) | collective-permute-done | bytes 307232 | tf_op jit(solution)/shard_map/ppermute | solution.py:477
  26.8 0.1 shard_map.106
  26.9 0.0 copy-start.1
  26.9 0.0 copy-start.4
  26.9 0.0 copy-start.5
  26.9 1.7 %collective-permute-start.3 = (bf16[240,640]{1,0:T(8,128)(2,1)S(1)}, bf16[240,640]{1,0:T(8,128)(2,1)S(1)}, u32[]{:S(2)}, u32[]{:S(2)}) collective-permute-start(bf16[240,640]{1,0:T(8,128)(2,1)S(1)} %shard_map.106), channel_id=1, source_target_pairs={{0,8},{8,16},{16,24},{24,32},{32,40},{40,48},{48,56},{56,0},{64,12... | collective-permute-start | bytes 921608 | tf_op jit(solution)/shard_map/ppermute | solution.py:477
  28.7 1.4 %collective-permute-done.6.received = bf16[240,640]{1,0:T(8,128)(2,1)S(1)} collective-permute-done((bf16[240,640]{1,0:T(8,128)(2,1)S(1)}, bf16[240,640]{1,0:T(8,128)(2,1)S(1)}, u32[]{:S(2)}, u32[]{:S(2)}) %collective-permute-start.6) | collective-permute-done | bytes 307232 | tf_op jit(solution)/shard_map/ppermute | solution.py:477
  30.1 0.1 shard_map.109
  30.1 2.0 %collective-permute-start.7 = (bf16[240,640]{1,0:T(8,128)(2,1)S(1)}, bf16[240,640]{1,0:T(8,128)(2,1)S(1)}, u32[]{:S(2)}, u32[]{:S(2)}) collective-permute-start(bf16[240,640]{1,0:T(8,128)(2,1)S(1)} %shard_map.109), channel_id=1, source_target_pairs={{0,8},{8,16},{16,24},{24,32},{32,40},{40,48},{48,56},{56,0},{64,12... | collective-permute-start | bytes 921608 | tf_op jit(solution)/shard_map/ppermute | solution.py:477
  32.1 1.3 %collective-permute-done.3.received = bf16[240,640]{1,0:T(8,128)(2,1)S(1)} collective-permute-done((bf16[240,640]{1,0:T(8,128)(2,1)S(1)}, bf16[240,640]{1,0:T(8,128)(2,1)S(1)}, u32[]{:S(2)}, u32[]{:S(2)}) %collective-permute-start.3) | collective-permute-done | bytes 307232 | tf_op jit(solution)/shard_map/ppermute | solution.py:477
  33.4 0.1 shard_map.107
  33.5 2.2 %collective-permute-start.4 = (bf16[240,640]{1,0:T(8,128)(2,1)S(1)}, bf16[240,640]{1,0:T(8,128)(2,1)S(1)}, u32[]{:S(2)}, u32[]{:S(2)}) collective-permute-start(bf16[240,640]{1,0:T(8,128)(2,1)S(1)} %shard_map.107), channel_id=1, source_target_pairs={{0,8},{8,16},{16,24},{24,32},{32,40},{40,48},{48,56},{56,0},{64,12... | collective-permute-start | bytes 921608 | tf_op jit(solution)/shard_map/ppermute | solution.py:477
  35.7 1.0 %collective-permute-done.7 = bf16[240,640]{1,0:T(8,128)(2,1)S(1)} collective-permute-done((bf16[240,640]{1,0:T(8,128)(2,1)S(1)}, bf16[240,640]{1,0:T(8,128)(2,1)S(1)}, u32[]{:S(2)}, u32[]{:S(2)}) %collective-permute-start.7) | collective-permute-done | bytes 307232 | tf_op jit(solution)/shard_map/ppermute | solution.py:477
  36.7 2.2 %collective-permute-start.8 = (bf16[240,640]{1,0:T(8,128)(2,1)S(1)}, bf16[240,640]{1,0:T(8,128)(2,1)S(1)}, u32[]{:S(2)}, u32[]{:S(2)}) collective-permute-start(bf16[240,640]{1,0:T(8,128)(2,1)S(1)} %collective-permute-done.7), channel_id=1, source_target_pairs={{0,64},{64,0},{128,192},{192,128},{1,65},{65,1},{129,193},{193,129... | collective-permute-start | bytes 921608 | tf_op jit(solution)/shard_map/ppermute | solution.py:480
  38.9 1.1 %collective-permute-done.4.ours = bf16[240,640]{1,0:T(8,128)(2,1)S(1)} collective-permute-done((bf16[240,640]{1,0:T(8,128)(2,1)S(1)}, bf16[240,640]{1,0:T(8,128)(2,1)S(1)}, u32[]{:S(2)}, u32[]{:S(2)}) %collective-permute-start.4) | collective-permute-done | bytes 307232 | tf_op jit(solution)/shard_map/ppermute | solution.py:477
  40.0 0.1 collective-permute-done.8.theirs
  40.1 0.4 shard_map.110.rows
  40.5 3.0 %collective-permute-start.9 = (bf16[224,640]{1,0:T(8,128)(2,1)S(1)}, bf16[224,640]{1,0:T(8,128)(2,1)S(1)}, u32[]{:S(2)}, u32[]{:S(2)}) collective-permute-start(bf16[224,640]{1,0:T(8,128)(2,1)S(1)} %shard_map.110.rows), channel_id=1, source_target_pairs={{0,128},{64,192},{128,0},{192,64},{1,129},{65,193},{129,1},{193,65... | collective-permute-start | bytes 860168 | tf_op jit(solution)/shard_map/ppermute | solution.py:505
  43.5 4.1 %collective-permute-done.9.rows_far = bf16[224,640]{1,0:T(8,128)(2,1)S(1)} collective-permute-done((bf16[224,640]{1,0:T(8,128)(2,1)S(1)}, bf16[224,640]{1,0:T(8,128)(2,1)S(1)}, u32[]{:S(2)}, u32[]{:S(2)}) %collective-permute-start.9) | collective-permute-done | bytes 286752 | tf_op jit(solution)/shard_map/ppermute | solution.py:505
  47.6 0.6 shard_map.111.refs_3_.refs_6_
  48.2 4.8 %collective-permute-start.13 = (bf16[256,640]{1,0:T(8,128)(2,1)S(1)}, bf16[256,640]{1,0:T(8,128)(2,1)S(1)}, u32[]{:S(2)}, u32[]{:S(2)}) collective-permute-start(bf16[256,640]{1,0:T(8,128)(2,1)S(1)} %shard_map.111.refs_3_.refs_6_), channel_id=1, source_target_pairs={{0,64},{64,0},{128,192},{192,128},{1,65},{65,1},{129,193},{193,129... | collective-permute-start | bytes 983048 | tf_op jit(solution)/shard_map/ppermute | solution.py:480
  53.0 1.6 %collective-permute-start.10 = (bf16[256,640]{1,0:T(8,128)(2,1)S(1)}, bf16[256,640]{1,0:T(8,128)(2,1)S(1)}, u32[]{:S(2)}, u32[]{:S(2)}) collective-permute-start(bf16[256,640]{1,0:T(8,128)(2,1)S(1)} %shard_map.111.refs_3_.refs_6_), channel_id=1, source_target_pairs={{0,8},{8,16},{16,24},{24,32},{32,40},{40,48},{48,56},{56,0},{64,12... | collective-permute-start | bytes 983048 | tf_op jit(solution)/shard_map/ppermute | solution.py:477
  54.6 1.3 %collective-permute-start.14 = (bf16[256,640]{1,0:T(8,128)(2,1)S(1)}, bf16[256,640]{1,0:T(8,128)(2,1)S(1)}, u32[]{:S(2)}, u32[]{:S(2)}) collective-permute-start(bf16[256,640]{1,0:T(8,128)(2,1)S(1)} %collective-permute-done.13.refs_4_.refs_5_), channel_id=1, source_target_pairs={{0,8},{8,16},{16,24},{24,32},{32,40},{40,48},{48,56},{56,0},{64,12... | collective-permute-start | bytes 983048 | tf_op jit(solution)/shard_map/ppermute | solution.py:477
  55.9 4.9 %shard_map.112 = (f32[5,512,256]{2,1,0:T(8,128)S(1)}, bf16[5,512,128]{2,1,0:T(8,128)(2,1)S(1)}) custom-call(bf16[4,128,640]{2,1,0:T(8,128)(2,1)S(1)} %copy-done.1, bf16[4,128,640]{2,1,0:T(8,128)(2,1)S(1)} %copy-done.4, bf16[4,128,640]{2,1,0:T(8,128)(2,1)S(1)} %copy-done.5), custom_call_target="tpu_custom_call" | custom-call | flops 167772160 | bytes 6291456 | tf_op jit(solution)/shard_map/pallas_call | solution.py:407
  60.8 0.9 %collective-permute-start.11 = (bf16[256,640]{1,0:T(8,128)(2,1)S(1)}, bf16[256,640]{1,0:T(8,128)(2,1)S(1)}, u32[]{:S(2)}, u32[]{:S(2)}) collective-permute-start(bf16[256,640]{1,0:T(8,128)(2,1)S(1)} %collective-permute-done.10.refs_7_.refs_14_), channel_id=1, source_target_pairs={{0,8},{8,16},{16,24},{24,32},{32,40},{40,48},{48,56},{56,0},{64,12... | collective-permute-start | bytes 983048 | tf_op jit(solution)/shard_map/ppermute | solution.py:477
  61.8 1.0 %collective-permute-done.14.refs_9_.refs_12_ = bf16[256,640]{1,0:T(8,128)(2,1)S(1)} collective-permute-done((bf16[256,640]{1,0:T(8,128)(2,1)S(1)}, bf16[256,640]{1,0:T(8,128)(2,1)S(1)}, u32[]{:S(2)}, u32[]{:S(2)}) %collective-permute-start.14) | collective-permute-done | bytes 327712 | tf_op jit(solution)/shard_map/ppermute | solution.py:477
  62.7 2.5 %collective-permute-start.15 = (bf16[256,640]{1,0:T(8,128)(2,1)S(1)}, bf16[256,640]{1,0:T(8,128)(2,1)S(1)}, u32[]{:S(2)}, u32[]{:S(2)}) collective-permute-start(bf16[256,640]{1,0:T(8,128)(2,1)S(1)} %collective-permute-done.14.refs_9_.refs_12_), channel_id=1, source_target_pairs={{0,8},{8,16},{16,24},{24,32},{32,40},{40,48},{48,56},{56,0},{64,12... | collective-permute-start | bytes 983048 | tf_op jit(solution)/shard_map/ppermute | solution.py:477
  65.3 0.0 collective-permute-start.16
  65.3 0.5 collective-permute-start.17
  65.8 1.3 %collective-permute-done.11.refs_3_.refs_10_ = bf16[256,640]{1,0:T(8,128)(2,1)S(1)} collective-permute-done((bf16[256,640]{1,0:T(8,128)(2,1)S(1)}, bf16[256,640]{1,0:T(8,128)(2,1)S(1)}, u32[]{:S(2)}, u32[]{:S(2)}) %collective-permute-start.11) | collective-permute-done | bytes 327712 | tf_op jit(solution)/shard_map/ppermute | solution.py:477
  67.1 1.8 %collective-permute-start.12 = (bf16[256,640]{1,0:T(8,128)(2,1)S(1)}, bf16[256,640]{1,0:T(8,128)(2,1)S(1)}, u32[]{:S(2)}, u32[]{:S(2)}) collective-permute-start(bf16[256,640]{1,0:T(8,128)(2,1)S(1)} %collective-permute-done.11.refs_3_.refs_10_), channel_id=1, source_target_pairs={{0,8},{8,16},{16,24},{24,32},{32,40},{40,48},{48,56},{56,0},{64,12... | collective-permute-start | bytes 983048 | tf_op jit(solution)/shard_map/ppermute | solution.py:477
  68.9 0.8 collective-permute-start.19
  69.7 1.0 %collective-permute-done.15.refs_5_.refs_8_ = bf16[256,640]{1,0:T(8,128)(2,1)S(1)} collective-permute-done((bf16[256,640]{1,0:T(8,128)(2,1)S(1)}, bf16[256,640]{1,0:T(8,128)(2,1)S(1)}, u32[]{:S(2)}, u32[]{:S(2)}) %collective-permute-start.15) | collective-permute-done | bytes 327712 | tf_op jit(solution)/shard_map/ppermute | solution.py:477
  70.6 2.0 %collective-permute-start.22 = (bf16[256,640]{1,0:T(8,128)(2,1)S(1)}, bf16[256,640]{1,0:T(8,128)(2,1)S(1)}, u32[]{:S(2)}, u32[]{:S(2)}) collective-permute-start(bf16[256,640]{1,0:T(8,128)(2,1)S(1)} %collective-permute-done.15.refs_5_.refs_8_), channel_id=1, source_target_pairs={{0,8},{8,16},{16,24},{24,32},{32,40},{40,48},{48,56},{56,0},{64,12... | collective-permute-start | bytes 983048 | tf_op jit(solution)/shard_map/ppermute | solution.py:477
  72.6 0.6 collective-permute-start.20
  73.2 2.5 %shard_map.113 = (f32[5,512,256]{2,1,0:T(8,128)S(1)}, bf16[5,512,128]{2,1,0:T(8,128)(2,1)S(1)}) custom-call(bf16[4,128,640]{2,1,0:T(8,128)(2,1)S(1)} %copy-done.1, f32[5,512,256]{2,1,0:T(8,128)S(1)} %get-tuple-element.50.refs_1_, bf16[5,512,128]{2,1,0:T(8,128)(2,1)S(1)} %get-tuple-element.51.refs_2_, bf16[256,640]{1,0:T(8,128)(2,1)S(1)} %shard_map.111.refs_3_.refs_6_, ...), custom_call_target="tpu_custom_call" | custom-call | flops 1006632960 | bytes 8388608 | tf_op jit(solution)/shard_map/pallas_call | solution.py:438
  75.7 3.0 %collective-permute-start.18 = (bf16[256,640]{1,0:T(8,128)(2,1)S(1)}, bf16[256,640]{1,0:T(8,128)(2,1)S(1)}, u32[]{:S(2)}, u32[]{:S(2)}) collective-permute-start(bf16[256,640]{1,0:T(8,128)(2,1)S(1)} %collective-permute-done.12.refs_3_.refs_10_), channel_id=1, source_target_pairs={{0,8},{8,16},{16,24},{24,32},{32,40},{40,48},{48,56},{56,0},{64,12... | collective-permute-start | bytes 983048 | tf_op jit(solution)/shard_map/ppermute | solution.py:477
  78.7 2.7 %collective-permute-start.23 = (bf16[256,640]{1,0:T(8,128)(2,1)S(1)}, bf16[256,640]{1,0:T(8,128)(2,1)S(1)}, u32[]{:S(2)}, u32[]{:S(2)}) collective-permute-start(bf16[256,640]{1,0:T(8,128)(2,1)S(1)} %collective-permute-done.22.refs_5_.refs_8_), channel_id=1, source_target_pairs={{0,64},{64,0},{128,192},{192,128},{1,65},{65,1},{129,193},{193,129... | collective-permute-start | bytes 983048 | tf_op jit(solution)/shard_map/ppermute | solution.py:480
  81.5 1.8 %shard_map.114 = (f32[5,512,256]{2,1,0:T(8,128)S(1)}, bf16[5,512,128]{2,1,0:T(8,128)(2,1)S(1)}) custom-call(bf16[4,128,640]{2,1,0:T(8,128)(2,1)S(1)} %copy-done.1, f32[5,512,256]{2,1,0:T(8,128)S(1)} %get-tuple-element.55.refs_1_, bf16[5,512,128]{2,1,0:T(8,128)(2,1)S(1)} %get-tuple-element.56.refs_2_, ...), custom_call_target="tpu_custom_call" | custom-call | flops 671088640 | bytes 8388608 | tf_op jit(solution)/shard_map/pallas_call | solution.py:438
  83.3 0.0 copy-start.10
  83.3 2.9 %collective-permute-start.24 = (bf16[256,640]{1,0:T(8,128)(2,1)S(1)}, bf16[256,640]{1,0:T(8,128)(2,1)S(1)}, u32[]{:S(2)}, u32[]{:S(2)}) collective-permute-start(bf16[256,640]{1,0:T(8,128)(2,1)S(1)} %collective-permute-done.18.refs_4_.refs_7_), channel_id=1, source_target_pairs={{0,64},{64,0},{128,192},{192,128},{1,65},{65,1},{129,193},{193,129... | collective-permute-start | bytes 983048 | tf_op jit(solution)/shard_map/ppermute | solution.py:480
  86.3 1.8 %shard_map.115 = (f32[5,512,256]{2,1,0:T(8,128)S(1)}, bf16[5,512,128]{2,1,0:T(8,128)(2,1)S(1)}) custom-call(bf16[4,128,640]{2,1,0:T(8,128)(2,1)S(1)} %copy-done.1, f32[5,512,256]{2,1,0:T(8,128)S(1)} %get-tuple-element.60.refs_1_, bf16[5,512,128]{2,1,0:T(8,128)(2,1)S(1)} %get-tuple-element.61.refs_2_, ...), custom_call_target="tpu_custom_call" | custom-call | flops 671088640 | bytes 8388608 | tf_op jit(solution)/shard_map/pallas_call | solution.py:438
  88.1 2.6 %shard_map.116 = bf16[4,128,640]{2,1,0:T(8,128)(2,1)} custom-call(s32[4]{0:T(128)S(1)} %copy-done.10, bf16[4,128,640]{2,1,0:T(8,128)(2,1)S(1)} %copy-done.1, f32[5,512,256]{2,1,0:T(8,128)S(1)} %get-tuple-element.62.refs_2_, bf16[5,512,128]{2,1,0:T(8,128)(2,1)S(1)} %get-tuple-element.63.refs_3_, bf16[256,640]{1,0:T(8,128)(2,1)S(1)} %collective-permute-done.18.refs_4_.refs_7_, ...), custom_call_target="tpu_custom_call" | custom-call | flops 335544320 | bytes 8388608 | tf_op jit(solution)/shard_map/pallas_call | solution.py:438
  (25 shorter events, 0.1 us)
Async XLA Ops:
  0.0 7.6 %collective-permute-start = (bf16[1024,1152]{1,0:T(8,128)(2,1)}, bf16[1024,1152]{1,0:T(8,128)(2,1)S(1)}, u32[]{:S(2)}, u32[]{:S(2)}) collective-permute-start(bf16[1024,1152]{1,0:T(8,128)(2,1)} %hidden.5), channel_id=1, source_target_pairs={{0,64},{64,0},{128,192},{192,128},{1,65},{65,1},{129,193},{193,129... | collective-permute-start | bytes 7077896 | tf_op jit(solution)/shard_map/ppermute | solution.py:480
  3.2 1.7 %copy-start = (bf16[1024,1152]{1,0:T(8,128)(2,1)S(1)}, bf16[1024,1152]{1,0:T(8,128)(2,1)}, u32[]{:S(2)}) copy-start(bf16[1024,1152]{1,0:T(8,128)(2,1)} %hidden.5) | copy-start | bytes 7077892
  4.9 0.7 copy-start.6
  5.6 0.7 copy-start.7
  6.3 0.7 copy-start.9
  6.3 1.4 %copy-start.2 = (bf16[1152,640]{1,0:T(8,128)(2,1)S(1)}, bf16[1152,640]{1,0:T(8,128)(2,1)}, u32[]{:S(2)}) copy-start(bf16[1152,640]{1,0:T(8,128)(2,1)} %rest_0_.1) | copy-start | bytes 4423684
  6.3 1.8 %copy-start.3 = (bf16[1152,640]{1,0:T(8,128)(2,1)S(1)}, bf16[1152,640]{1,0:T(8,128)(2,1)}, u32[]{:S(2)}) copy-start(bf16[1152,640]{1,0:T(8,128)(2,1)} %rest_1_.1) | copy-start | bytes 4423684
  9.9 10.8 %collective-permute-start.1 = (bf16[240,640]{1,0:T(8,128)(2,1)S(1)}, bf16[240,640]{1,0:T(8,128)(2,1)S(1)}, u32[]{:S(2)}, u32[]{:S(2)}) collective-permute-start(bf16[240,640]{1,0:T(8,128)(2,1)S(1)} %get-tuple-element.38), channel_id=1, source_target_pairs={{0,8},{8,16},{16,24},{24,32},{32,40},{40,48},{48,56},{56,0},{64,12... | collective-permute-start | bytes 921608 | tf_op jit(solution)/shard_map/ppermute | solution.py:477
  15.6 6.1 %collective-permute-start.5 = (bf16[240,640]{1,0:T(8,128)(2,1)S(1)}, bf16[240,640]{1,0:T(8,128)(2,1)S(1)}, u32[]{:S(2)}, u32[]{:S(2)}) collective-permute-start(bf16[240,640]{1,0:T(8,128)(2,1)S(1)} %get-tuple-element.42), channel_id=1, source_target_pairs={{0,8},{8,16},{16,24},{24,32},{32,40},{40,48},{48,56},{56,0},{64,12... | collective-permute-start | bytes 921608 | tf_op jit(solution)/shard_map/ppermute | solution.py:477
  20.7 6.1 %collective-permute-start.2 = (bf16[240,640]{1,0:T(8,128)(2,1)S(1)}, bf16[240,640]{1,0:T(8,128)(2,1)S(1)}, u32[]{:S(2)}, u32[]{:S(2)}) collective-permute-start(bf16[240,640]{1,0:T(8,128)(2,1)S(1)} %shard_map.105), channel_id=1, source_target_pairs={{0,8},{8,16},{16,24},{24,32},{32,40},{40,48},{48,56},{56,0},{64,12... | collective-permute-start | bytes 921608 | tf_op jit(solution)/shard_map/ppermute | solution.py:477
  21.7 25.8 %copy-start.8 = (s32[4]{0:T(128)S(1)}, s32[4]{0:T(128)}, u32[]{:S(2)}) copy-start(s32[4]{0:T(128)} %counts.7) | copy-start | bytes 52
  21.8 8.3 %collective-permute-start.6 = (bf16[240,640]{1,0:T(8,128)(2,1)S(1)}, bf16[240,640]{1,0:T(8,128)(2,1)S(1)}, u32[]{:S(2)}, u32[]{:S(2)}) collective-permute-start(bf16[240,640]{1,0:T(8,128)(2,1)S(1)} %shard_map.108), channel_id=1, source_target_pairs={{0,8},{8,16},{16,24},{24,32},{32,40},{40,48},{48,56},{56,0},{64,12... | collective-permute-start | bytes 921608 | tf_op jit(solution)/shard_map/ppermute | solution.py:477
  26.9 29.0 %copy-start.1 = (bf16[4,128,640]{2,1,0:T(8,128)(2,1)S(1)}, bf16[4,128,640]{2,1,0:T(8,128)(2,1)}, u32[]{:S(2)}) copy-start(bf16[4,128,640]{2,1,0:T(8,128)(2,1)} %refs_1_.5) | copy-start | bytes 1966084
  26.9 29.0 %copy-start.4 = (bf16[4,128,640]{2,1,0:T(8,128)(2,1)S(1)}, bf16[4,128,640]{2,1,0:T(8,128)(2,1)}, u32[]{:S(2)}) copy-start(bf16[4,128,640]{2,1,0:T(8,128)(2,1)} %own_k.1) | copy-start | bytes 1966084
  26.9 29.0 %copy-start.5 = (bf16[4,128,640]{2,1,0:T(8,128)(2,1)S(1)}, bf16[4,128,640]{2,1,0:T(8,128)(2,1)}, u32[]{:S(2)}) copy-start(bf16[4,128,640]{2,1,0:T(8,128)(2,1)} %own_v.1) | copy-start | bytes 1966084
  26.9 6.5 %collective-permute-start.3 = (bf16[240,640]{1,0:T(8,128)(2,1)S(1)}, bf16[240,640]{1,0:T(8,128)(2,1)S(1)}, u32[]{:S(2)}, u32[]{:S(2)}) collective-permute-start(bf16[240,640]{1,0:T(8,128)(2,1)S(1)} %shard_map.106), channel_id=1, source_target_pairs={{0,8},{8,16},{16,24},{24,32},{32,40},{40,48},{48,56},{56,0},{64,12... | collective-permute-start | bytes 921608 | tf_op jit(solution)/shard_map/ppermute | solution.py:477
  30.1 6.6 %collective-permute-start.7 = (bf16[240,640]{1,0:T(8,128)(2,1)S(1)}, bf16[240,640]{1,0:T(8,128)(2,1)S(1)}, u32[]{:S(2)}, u32[]{:S(2)}) collective-permute-start(bf16[240,640]{1,0:T(8,128)(2,1)S(1)} %shard_map.109), channel_id=1, source_target_pairs={{0,8},{8,16},{16,24},{24,32},{32,40},{40,48},{48,56},{56,0},{64,12... | collective-permute-start | bytes 921608 | tf_op jit(solution)/shard_map/ppermute | solution.py:477
  33.5 6.5 %collective-permute-start.4 = (bf16[240,640]{1,0:T(8,128)(2,1)S(1)}, bf16[240,640]{1,0:T(8,128)(2,1)S(1)}, u32[]{:S(2)}, u32[]{:S(2)}) collective-permute-start(bf16[240,640]{1,0:T(8,128)(2,1)S(1)} %shard_map.107), channel_id=1, source_target_pairs={{0,8},{8,16},{16,24},{24,32},{32,40},{40,48},{48,56},{56,0},{64,12... | collective-permute-start | bytes 921608 | tf_op jit(solution)/shard_map/ppermute | solution.py:477
  36.7 3.4 %collective-permute-start.8 = (bf16[240,640]{1,0:T(8,128)(2,1)S(1)}, bf16[240,640]{1,0:T(8,128)(2,1)S(1)}, u32[]{:S(2)}, u32[]{:S(2)}) collective-permute-start(bf16[240,640]{1,0:T(8,128)(2,1)S(1)} %collective-permute-done.7), channel_id=1, source_target_pairs={{0,64},{64,0},{128,192},{192,128},{1,65},{65,1},{129,193},{193,129... | collective-permute-start | bytes 921608 | tf_op jit(solution)/shard_map/ppermute | solution.py:480
  40.5 7.1 %collective-permute-start.9 = (bf16[224,640]{1,0:T(8,128)(2,1)S(1)}, bf16[224,640]{1,0:T(8,128)(2,1)S(1)}, u32[]{:S(2)}, u32[]{:S(2)}) collective-permute-start(bf16[224,640]{1,0:T(8,128)(2,1)S(1)} %shard_map.110.rows), channel_id=1, source_target_pairs={{0,128},{64,192},{128,0},{192,64},{1,129},{65,193},{129,1},{193,65... | collective-permute-start | bytes 860168 | tf_op jit(solution)/shard_map/ppermute | solution.py:505
  48.2 6.4 %collective-permute-start.13 = (bf16[256,640]{1,0:T(8,128)(2,1)S(1)}, bf16[256,640]{1,0:T(8,128)(2,1)S(1)}, u32[]{:S(2)}, u32[]{:S(2)}) collective-permute-start(bf16[256,640]{1,0:T(8,128)(2,1)S(1)} %shard_map.111.refs_3_.refs_6_), channel_id=1, source_target_pairs={{0,64},{64,0},{128,192},{192,128},{1,65},{65,1},{129,193},{193,129... | collective-permute-start | bytes 983048 | tf_op jit(solution)/shard_map/ppermute | solution.py:480
  53.0 7.8 %collective-permute-start.10 = (bf16[256,640]{1,0:T(8,128)(2,1)S(1)}, bf16[256,640]{1,0:T(8,128)(2,1)S(1)}, u32[]{:S(2)}, u32[]{:S(2)}) collective-permute-start(bf16[256,640]{1,0:T(8,128)(2,1)S(1)} %shard_map.111.refs_3_.refs_6_), channel_id=1, source_target_pairs={{0,8},{8,16},{16,24},{24,32},{32,40},{40,48},{48,56},{56,0},{64,12... | collective-permute-start | bytes 983048 | tf_op jit(solution)/shard_map/ppermute | solution.py:477
  54.6 8.1 %collective-permute-start.14 = (bf16[256,640]{1,0:T(8,128)(2,1)S(1)}, bf16[256,640]{1,0:T(8,128)(2,1)S(1)}, u32[]{:S(2)}, u32[]{:S(2)}) collective-permute-start(bf16[256,640]{1,0:T(8,128)(2,1)S(1)} %collective-permute-done.13.refs_4_.refs_5_), channel_id=1, source_target_pairs={{0,8},{8,16},{16,24},{24,32},{32,40},{40,48},{48,56},{56,0},{64,12... | collective-permute-start | bytes 983048 | tf_op jit(solution)/shard_map/ppermute | solution.py:477
  60.8 6.3 %collective-permute-start.11 = (bf16[256,640]{1,0:T(8,128)(2,1)S(1)}, bf16[256,640]{1,0:T(8,128)(2,1)S(1)}, u32[]{:S(2)}, u32[]{:S(2)}) collective-permute-start(bf16[256,640]{1,0:T(8,128)(2,1)S(1)} %collective-permute-done.10.refs_7_.refs_14_), channel_id=1, source_target_pairs={{0,8},{8,16},{16,24},{24,32},{32,40},{40,48},{48,56},{56,0},{64,12... | collective-permute-start | bytes 983048 | tf_op jit(solution)/shard_map/ppermute | solution.py:477
  62.7 7.9 %collective-permute-start.15 = (bf16[256,640]{1,0:T(8,128)(2,1)S(1)}, bf16[256,640]{1,0:T(8,128)(2,1)S(1)}, u32[]{:S(2)}, u32[]{:S(2)}) collective-permute-start(bf16[256,640]{1,0:T(8,128)(2,1)S(1)} %collective-permute-done.14.refs_9_.refs_12_), channel_id=1, source_target_pairs={{0,8},{8,16},{16,24},{24,32},{32,40},{40,48},{48,56},{56,0},{64,12... | collective-permute-start | bytes 983048 | tf_op jit(solution)/shard_map/ppermute | solution.py:477
  65.3 7.4 %collective-permute-start.16 = (bf16[256,640]{1,0:T(8,128)(2,1)S(1)}, bf16[256,640]{1,0:T(8,128)(2,1)S(1)}, u32[]{:S(2)}, u32[]{:S(2)}) collective-permute-start(bf16[256,640]{1,0:T(8,128)(2,1)S(1)} %collective-permute-done.10.refs_7_.refs_14_), channel_id=1, source_target_pairs={{0,64},{64,0},{128,192},{192,128},{1,65},{65,1},{129,193},{193,129... | collective-permute-start | bytes 983048 | tf_op jit(solution)/shard_map/ppermute | solution.py:480
  65.3 7.9 %collective-permute-start.17 = (bf16[256,640]{1,0:T(8,128)(2,1)S(1)}, bf16[256,640]{1,0:T(8,128)(2,1)S(1)}, u32[]{:S(2)}, u32[]{:S(2)}) collective-permute-start(bf16[256,640]{1,0:T(8,128)(2,1)S(1)} %collective-permute-done.14.refs_9_.refs_12_), channel_id=1, source_target_pairs={{0,64},{64,0},{128,192},{192,128},{1,65},{65,1},{129,193},{193,129... | collective-permute-start | bytes 983048 | tf_op jit(solution)/shard_map/ppermute | solution.py:480
  67.1 8.6 %collective-permute-start.12 = (bf16[256,640]{1,0:T(8,128)(2,1)S(1)}, bf16[256,640]{1,0:T(8,128)(2,1)S(1)}, u32[]{:S(2)}, u32[]{:S(2)}) collective-permute-start(bf16[256,640]{1,0:T(8,128)(2,1)S(1)} %collective-permute-done.11.refs_3_.refs_10_), channel_id=1, source_target_pairs={{0,8},{8,16},{16,24},{24,32},{32,40},{40,48},{48,56},{56,0},{64,12... | collective-permute-start | bytes 983048 | tf_op jit(solution)/shard_map/ppermute | solution.py:477
  68.9 12.6 %collective-permute-start.19 = (bf16[256,640]{1,0:T(8,128)(2,1)S(1)}, bf16[256,640]{1,0:T(8,128)(2,1)S(1)}, u32[]{:S(2)}, u32[]{:S(2)}) collective-permute-start(bf16[256,640]{1,0:T(8,128)(2,1)S(1)} %collective-permute-done.11.refs_3_.refs_10_), channel_id=1, source_target_pairs={{0,64},{64,0},{128,192},{192,128},{1,65},{65,1},{129,193},{193,129... | collective-permute-start | bytes 983048 | tf_op jit(solution)/shard_map/ppermute | solution.py:480
  70.6 8.1 %collective-permute-start.22 = (bf16[256,640]{1,0:T(8,128)(2,1)S(1)}, bf16[256,640]{1,0:T(8,128)(2,1)S(1)}, u32[]{:S(2)}, u32[]{:S(2)}) collective-permute-start(bf16[256,640]{1,0:T(8,128)(2,1)S(1)} %collective-permute-done.15.refs_5_.refs_8_), channel_id=1, source_target_pairs={{0,8},{8,16},{16,24},{24,32},{32,40},{40,48},{48,56},{56,0},{64,12... | collective-permute-start | bytes 983048 | tf_op jit(solution)/shard_map/ppermute | solution.py:477
  72.6 8.8 %collective-permute-start.20 = (bf16[256,640]{1,0:T(8,128)(2,1)S(1)}, bf16[256,640]{1,0:T(8,128)(2,1)S(1)}, u32[]{:S(2)}, u32[]{:S(2)}) collective-permute-start(bf16[256,640]{1,0:T(8,128)(2,1)S(1)} %collective-permute-done.15.refs_5_.refs_8_), channel_id=1, source_target_pairs={{0,64},{64,0},{128,192},{192,128},{1,65},{65,1},{129,193},{193,129... | collective-permute-start | bytes 983048 | tf_op jit(solution)/shard_map/ppermute | solution.py:480
  75.7 7.6 %collective-permute-start.18 = (bf16[256,640]{1,0:T(8,128)(2,1)S(1)}, bf16[256,640]{1,0:T(8,128)(2,1)S(1)}, u32[]{:S(2)}, u32[]{:S(2)}) collective-permute-start(bf16[256,640]{1,0:T(8,128)(2,1)S(1)} %collective-permute-done.12.refs_3_.refs_10_), channel_id=1, source_target_pairs={{0,8},{8,16},{16,24},{24,32},{32,40},{40,48},{48,56},{56,0},{64,12... | collective-permute-start | bytes 983048 | tf_op jit(solution)/shard_map/ppermute | solution.py:477
  78.7 7.5 %collective-permute-start.21 = (bf16[256,640]{1,0:T(8,128)(2,1)S(1)}, bf16[256,640]{1,0:T(8,128)(2,1)S(1)}, u32[]{:S(2)}, u32[]{:S(2)}) collective-permute-start(bf16[256,640]{1,0:T(8,128)(2,1)S(1)} %collective-permute-done.12.refs_3_.refs_10_), channel_id=1, source_target_pairs={{0,64},{64,0},{128,192},{192,128},{1,65},{65,1},{129,193},{193,129... | collective-permute-start | bytes 983048 | tf_op jit(solution)/shard_map/ppermute | solution.py:480
  78.7 7.5 %collective-permute-start.23 = (bf16[256,640]{1,0:T(8,128)(2,1)S(1)}, bf16[256,640]{1,0:T(8,128)(2,1)S(1)}, u32[]{:S(2)}, u32[]{:S(2)}) collective-permute-start(bf16[256,640]{1,0:T(8,128)(2,1)S(1)} %collective-permute-done.22.refs_5_.refs_8_), channel_id=1, source_target_pairs={{0,64},{64,0},{128,192},{192,128},{1,65},{65,1},{129,193},{193,129... | collective-permute-start | bytes 983048 | tf_op jit(solution)/shard_map/ppermute | solution.py:480
  83.3 4.8 %copy-start.10 = (s32[4]{0:T(128)S(1)}, s32[4]{0:T(128)}, u32[]{:S(2)}) copy-start(s32[4]{0:T(128)} %refs_0_.11) | copy-start | bytes 52
  83.3 4.8 %collective-permute-start.24 = (bf16[256,640]{1,0:T(8,128)(2,1)S(1)}, bf16[256,640]{1,0:T(8,128)(2,1)S(1)}, u32[]{:S(2)}, u32[]{:S(2)}) collective-permute-start(bf16[256,640]{1,0:T(8,128)(2,1)S(1)} %collective-permute-done.18.refs_4_.refs_7_), channel_id=1, source_target_pairs={{0,64},{64,0},{128,192},{192,128},{1,65},{65,1},{129,193},{193,129... | collective-permute-start | bytes 983048 | tf_op jit(solution)/shard_map/ppermute | solution.py:480

commit v7 on v6

--- a/solution.py
+++ b/solution.py
@@ -335,6 +335,15 @@
     q, state, shift = refs[:3]
     blocks = refs[3 : 3 + 4 * pair_count]
     outs = refs[3 + 4 * pair_count :]
+    if end:
+        out, done, semaphores = outs
+
+        def copy_out(head):
+            columns = pl.ds(head * HD, HD)
+            return pltpu.make_async_copy(
+                done.at[:, :, columns], out.at[:, :, columns], semaphores.at[head]
+            )
+
     requests, positions, width = q.shape
     rows = requests * positions
     heads = width // HD
@@ -364,13 +373,13 @@
 
     def emit(head, columns, total, packed):
         if end:
-            result = total[:, :HD] / total[:, HD:]
+            scale = pl.reciprocal(total[:, HD:], approx=True)
+            scale = scale * (2.0 - total[:, HD:] * scale)
+            result = total[:, :HD] * scale
             place = lax.broadcasted_iota(jnp.int32, (positions, HD), 0)
             for r in range(requests):
                 part = result[r * positions : (r + 1) * positions]
-                outs[0][r, :, columns] = jnp.where(place < lengths[r], part, 0.0).astype(
-                    jnp.bfloat16
-                )
+                done[r, :, columns] = jnp.where(place < lengths[r], part, 0.0).astype(jnp.bfloat16)
         else:
             outs[0][head] = total
             outs[1][head] = packed
@@ -380,9 +389,14 @@
         columns = slice(head * HD, (head + 1) * HD)
         total = state[head] + weigh(shifted_scores(head, columns), columns)
         emit(head, columns, total, shift[head])
+        if end:
+            copy_out(head).start()
         largest = jnp.maximum(
             largest, jnp.max(total[:, HD:].reshape(rows // 8, 8, HD), axis=0)
         )
+    if end:
+        for head in range(heads):
+            copy_out(head).wait()
 
     @pl.when(jnp.logical_not(jnp.max(largest) < 1e30))
     def _():
@@ -397,6 +411,11 @@
             return carry
 
         lax.fori_loop(0, heads, one_head, 0)
+        if end:
+            for head in range(heads):
+                copy_out(head).start()
+            for head in range(heads):
+                copy_out(head).wait()
 
 
 def attend_own(q, k, v):
@@ -430,8 +449,14 @@
     if lengths is not None:
         specs = [pl.BlockSpec(memory_space=pltpu.SMEM)] + specs
         operands = [lengths] + operands
-        out_shape, out_specs = jax.ShapeDtypeStruct(q.shape, jnp.bfloat16), vmem
+        out_shape = jax.ShapeDtypeStruct(q.shape, jnp.bfloat16)
+        out_specs = pl.BlockSpec(memory_space=pl.ANY)
+        scratch = [
+            pltpu.VMEM(q.shape, jnp.bfloat16),
+            pltpu.SemaphoreType.DMA((width // HD,)),
+        ]
     else:
+        scratch = []
         out_shape = [jax.ShapeDtypeStruct(array.shape, array.dtype) for array in state]
         out_specs = [vmem] * 2
     key_rows = BLOCK * len(pairs)
@@ -440,6 +465,7 @@
         out_shape=out_shape,
         in_specs=specs,
         out_specs=out_specs,
+        scratch_shapes=scratch,
         compiler_params=pltpu.CompilerParams(vmem_limit_bytes=32 * MIB),
         cost_estimate=pl.CostEstimate(
             flops=4 * rows * key_rows * width,

time: 90.9 us -> 90.9 us (level)
  no operation moved by 1% of the time
where the time goes in v7:
time: 90.9 us; the launch traced here: 90.7 us
  starting transfers between devices  47.7 us (52%)
  Pallas kernels  23.9 us (26%)
  waiting for transfers between devices  15.1 us (17%)
  local copies, waits for them, and re-layouts  3.65 us (4%)
    ppermute x14, starting transfers between devices, step(): return lax.ppermute(array, ('store', 'req'), around)  27 us
    ppermute x10, starting transfers between devices, swap(): return lax.ppermute(array, 'store', across)  17.7 us
    ppermute x14, waiting for transfers between devices, step(): return lax.ppermute(array, ('store', 'req'), around)  10.9 us
    pallas_call x4, Pallas kernels, attend(): pl.pallas_call(functools.partial(stage_kernel, lengths is not None, len(p...  8.58 us
    pallas_call x1, Pallas kernels, attend_own(): pl.pallas_call(own_kernel, out_shape=[jax.ShapeDtypeStruct((heads, rows,...  4.92 us
    pallas_call x1, Pallas kernels, project_rows(): pl.pallas_call(functools.partial(projection_kernel, plan), out_shape=[jax...  4.26 us
    ppermute x1, waiting for transfers between devices, per_device(): mine = merge(row_counts, rows, lax.ppermute(rows, 'store', far))  4.08 us
    unnamed x22, local copies, waits for them, and re-layouts  3.65 us
  transfers between devices with their start and end apart: 25, of which 12 were waited for; matrix products, arithmetic and copies ran while one was open for 0% of the time, Pallas kernels for 21%

profile of v7, /device:TPU:1, one launch (start us, length us, event | category | flops | bytes accessed | tf_op | source)
XLA Modules:
  0.0 90.7 jit_solution(8611002951436757540)
XLA Ops:
  0.0 3.2 %collective-permute-start = (bf16[1024,1152]{1,0:T(8,128)(2,1)}, bf16[1024,1152]{1,0:T(8,128)(2,1)S(1)}, u32[]{:S(2)}, u32[]{:S(2)}) collective-permute-start(bf16[1024,1152]{1,0:T(8,128)(2,1)} %hidden.5), channel_id=1, source_target_pairs={{0,64},{64,0},{128,192},{192,128},{1,65},{65,1},{129,193},{193,129... | collective-permute-start | bytes 7077896 | tf_op jit(solution)/shard_map/ppermute | solution.py:506
  3.2 1.7 %copy-done = bf16[1024,1152]{1,0:T(8,128)(2,1)S(1)} copy-done((bf16[1024,1152]{1,0:T(8,128)(2,1)S(1)}, bf16[1024,1152]{1,0:T(8,128)(2,1)}, u32[]{:S(2)}) %copy-start) | copy-done | bytes 2359320
  4.9 0.7 copy-done.6
  5.6 0.7 copy-done.7
  6.3 0.6 shard_map.100.refs_4_
  6.8 0.1 copy-done.9
  7.0 0.6 shard_map.101.affine
  7.5 0.1 collective-permute-done.hidden_other
  7.6 0.0 copy-done.2
  7.7 0.4 copy-done.3
  8.1 1.8 %shard_map.102 = (bf16[240,640]{1,0:T(8,128)(2,1)S(1)}, f32[8,640]{1,0:T(8,128)S(1)}) custom-call(s32[4]{0:T(128)S(1)} %copy-done.7, bf16[1024,1152]{1,0:T(8,128)(2,1)S(1)} %copy-done, bf16[1024,1152]{1,0:T(8,128)(2,1)S(1)} %collective-permute-done.hidden_other, f32[1152]{0:T(1024)S(1)} %copy-done.6, bf16[48,1152]{1,0:T(8,128)(2,1)S(1)} %shard_map.101.affine, ...), custom_call_target="tpu_custom_call" | custom-call | flops 330301440 | bytes 4194304 | tf_op jit(solution)/shard_map/pallas_call | solution.py:149
  9.9 3.9 %collective-permute-start.1 = (bf16[240,640]{1,0:T(8,128)(2,1)S(1)}, bf16[240,640]{1,0:T(8,128)(2,1)S(1)}, u32[]{:S(2)}, u32[]{:S(2)}) collective-permute-start(bf16[240,640]{1,0:T(8,128)(2,1)S(1)} %get-tuple-element.38), channel_id=1, source_target_pairs={{0,8},{8,16},{16,24},{24,32},{32,40},{40,48},{48,56},{56,0},{64,12... | collective-permute-start | bytes 921608 | tf_op jit(solution)/shard_map/ppermute | solution.py:503
  13.8 1.8 %shard_map.103 = (bf16[240,640]{1,0:T(8,128)(2,1)S(1)}, f32[8,640]{1,0:T(8,128)S(1)}) custom-call(s32[4]{0:T(128)S(1)} %copy-done.7, bf16[1024,1152]{1,0:T(8,128)(2,1)S(1)} %copy-done, bf16[1024,1152]{1,0:T(8,128)(2,1)S(1)} %collective-permute-done.hidden_other, f32[1152]{0:T(1024)S(1)} %copy-done.6, bf16[48,1152]{1,0:T(8,128)(2,1)S(1)} %shard_map.101.affine, ...), custom_call_target="tpu_custom_call" | custom-call | flops 330301440 | bytes 4194304 | tf_op jit(solution)/shard_map/pallas_call | solution.py:149
  15.6 0.8 collective-permute-start.5
  16.4 4.3 %shard_map.104 = (f32[232,640]{1,0:T(8,128)S(1)}, f32[232,640]{1,0:T(8,128)S(1)}, f32[232,640]{1,0:T(8,128)S(1)}, f32[232,640]{1,0:T(8,128)S(1)}, f32[232,640]{1,0:T(8,128)S(1)}, /*index=5*/f32[232,640]{1,0:T(8,128)S(1)}) custom-call(s32[4]{0:T(128)S(1)} %copy-done.7, bf16[1024,1152]{1,0:T(8,128)(2,1)S(1)} %copy-done, ...), custom_call_target="tpu_custom_call" | custom-call | flops 1981808640 | bytes 4194304 | tf_op jit(solution)/shard_map/pallas_call | solution.py:196
  20.7 0.1 shard_map.105
  20.7 0.8 collective-permute-start.2
  21.5 0.1 collective-permute-done.5.received
  21.7 0.1 shard_map.108
  21.7 0.0 copy-start.8
  21.8 2.4 %collective-permute-start.6 = (bf16[240,640]{1,0:T(8,128)(2,1)S(1)}, bf16[240,640]{1,0:T(8,128)(2,1)S(1)}, u32[]{:S(2)}, u32[]{:S(2)}) collective-permute-start(bf16[240,640]{1,0:T(8,128)(2,1)S(1)} %shard_map.108), channel_id=1, source_target_pairs={{0,8},{8,16},{16,24},{24,32},{32,40},{40,48},{48,56},{56,0},{64,12... | collective-permute-start | bytes 921608 | tf_op jit(solution)/shard_map/ppermute | solution.py:503
  24.2 2.6 %collective-permute-done.2.received = bf16[240,640]{1,0:T(8,128)(2,1)S(1)} collective-permute-done((bf16[240,640]{1,0:T(8,128)(2,1)S(1)}, bf16[240,640]{1,0:T(8,128)(2,1)S(1)}, u32[]{:S(2)}, u32[]{:S(2)}) %collective-permute-start.2) | collective-permute-done | bytes 307232 | tf_op jit(solution)/shard_map/ppermute | solution.py:503
  26.8 0.1 shard_map.106
  26.9 0.0 copy-start.1
  26.9 0.0 copy-start.4
  26.9 0.0 copy-start.5
  27.0 1.7 %collective-permute-start.3 = (bf16[240,640]{1,0:T(8,128)(2,1)S(1)}, bf16[240,640]{1,0:T(8,128)(2,1)S(1)}, u32[]{:S(2)}, u32[]{:S(2)}) collective-permute-start(bf16[240,640]{1,0:T(8,128)(2,1)S(1)} %shard_map.106), channel_id=1, source_target_pairs={{0,8},{8,16},{16,24},{24,32},{32,40},{40,48},{48,56},{56,0},{64,12... | collective-permute-start | bytes 921608 | tf_op jit(solution)/shard_map/ppermute | solution.py:503
  28.7 1.4 %collective-permute-done.6.received = bf16[240,640]{1,0:T(8,128)(2,1)S(1)} collective-permute-done((bf16[240,640]{1,0:T(8,128)(2,1)S(1)}, bf16[240,640]{1,0:T(8,128)(2,1)S(1)}, u32[]{:S(2)}, u32[]{:S(2)}) %collective-permute-start.6) | collective-permute-done | bytes 307232 | tf_op jit(solution)/shard_map/ppermute | solution.py:503
  30.1 0.1 shard_map.109
  30.1 2.0 %collective-permute-start.7 = (bf16[240,640]{1,0:T(8,128)(2,1)S(1)}, bf16[240,640]{1,0:T(8,128)(2,1)S(1)}, u32[]{:S(2)}, u32[]{:S(2)}) collective-permute-start(bf16[240,640]{1,0:T(8,128)(2,1)S(1)} %shard_map.109), channel_id=1, source_target_pairs={{0,8},{8,16},{16,24},{24,32},{32,40},{40,48},{48,56},{56,0},{64,12... | collective-permute-start | bytes 921608 | tf_op jit(solution)/shard_map/ppermute | solution.py:503
  32.1 1.3 %collective-permute-done.3.received = bf16[240,640]{1,0:T(8,128)(2,1)S(1)} collective-permute-done((bf16[240,640]{1,0:T(8,128)(2,1)S(1)}, bf16[240,640]{1,0:T(8,128)(2,1)S(1)}, u32[]{:S(2)}, u32[]{:S(2)}) %collective-permute-start.3) | collective-permute-done | bytes 307232 | tf_op jit(solution)/shard_map/ppermute | solution.py:503
  33.4 0.1 shard_map.107
  33.5 2.2 %collective-permute-start.4 = (bf16[240,640]{1,0:T(8,128)(2,1)S(1)}, bf16[240,640]{1,0:T(8,128)(2,1)S(1)}, u32[]{:S(2)}, u32[]{:S(2)}) collective-permute-start(bf16[240,640]{1,0:T(8,128)(2,1)S(1)} %shard_map.107), channel_id=1, source_target_pairs={{0,8},{8,16},{16,24},{24,32},{32,40},{40,48},{48,56},{56,0},{64,12... | collective-permute-start | bytes 921608 | tf_op jit(solution)/shard_map/ppermute | solution.py:503
  35.7 1.0 %collective-permute-done.7 = bf16[240,640]{1,0:T(8,128)(2,1)S(1)} collective-permute-done((bf16[240,640]{1,0:T(8,128)(2,1)S(1)}, bf16[240,640]{1,0:T(8,128)(2,1)S(1)}, u32[]{:S(2)}, u32[]{:S(2)}) %collective-permute-start.7) | collective-permute-done | bytes 307232 | tf_op jit(solution)/shard_map/ppermute | solution.py:503
  36.7 2.2 %collective-permute-start.8 = (bf16[240,640]{1,0:T(8,128)(2,1)S(1)}, bf16[240,640]{1,0:T(8,128)(2,1)S(1)}, u32[]{:S(2)}, u32[]{:S(2)}) collective-permute-start(bf16[240,640]{1,0:T(8,128)(2,1)S(1)} %collective-permute-done.7), channel_id=1, source_target_pairs={{0,64},{64,0},{128,192},{192,128},{1,65},{65,1},{129,193},{193,129... | collective-permute-start | bytes 921608 | tf_op jit(solution)/shard_map/ppermute | solution.py:506
  38.9 1.1 %collective-permute-done.4.ours = bf16[240,640]{1,0:T(8,128)(2,1)S(1)} collective-permute-done((bf16[240,640]{1,0:T(8,128)(2,1)S(1)}, bf16[240,640]{1,0:T(8,128)(2,1)S(1)}, u32[]{:S(2)}, u32[]{:S(2)}) %collective-permute-start.4) | collective-permute-done | bytes 307232 | tf_op jit(solution)/shard_map/ppermute | solution.py:503
  40.0 0.1 collective-permute-done.8.theirs
  40.1 0.4 shard_map.110.rows
  40.5 3.0 %collective-permute-start.9 = (bf16[224,640]{1,0:T(8,128)(2,1)S(1)}, bf16[224,640]{1,0:T(8,128)(2,1)S(1)}, u32[]{:S(2)}, u32[]{:S(2)}) collective-permute-start(bf16[224,640]{1,0:T(8,128)(2,1)S(1)} %shard_map.110.rows), channel_id=1, source_target_pairs={{0,128},{64,192},{128,0},{192,64},{1,129},{65,193},{129,1},{193,65... | collective-permute-start | bytes 860168 | tf_op jit(solution)/shard_map/ppermute | solution.py:531
  43.5 4.1 %collective-permute-done.9.rows_far = bf16[224,640]{1,0:T(8,128)(2,1)S(1)} collective-permute-done((bf16[224,640]{1,0:T(8,128)(2,1)S(1)}, bf16[224,640]{1,0:T(8,128)(2,1)S(1)}, u32[]{:S(2)}, u32[]{:S(2)}) %collective-permute-start.9) | collective-permute-done | bytes 286752 | tf_op jit(solution)/shard_map/ppermute | solution.py:531
  47.6 0.6 shard_map.111.refs_3_.refs_6_
  48.2 4.8 %collective-permute-start.13 = (bf16[256,640]{1,0:T(8,128)(2,1)S(1)}, bf16[256,640]{1,0:T(8,128)(2,1)S(1)}, u32[]{:S(2)}, u32[]{:S(2)}) collective-permute-start(bf16[256,640]{1,0:T(8,128)(2,1)S(1)} %shard_map.111.refs_3_.refs_6_), channel_id=1, source_target_pairs={{0,64},{64,0},{128,192},{192,128},{1,65},{65,1},{129,193},{193,129... | collective-permute-start | bytes 983048 | tf_op jit(solution)/shard_map/ppermute | solution.py:506
  53.0 1.6 %collective-permute-start.10 = (bf16[256,640]{1,0:T(8,128)(2,1)S(1)}, bf16[256,640]{1,0:T(8,128)(2,1)S(1)}, u32[]{:S(2)}, u32[]{:S(2)}) collective-permute-start(bf16[256,640]{1,0:T(8,128)(2,1)S(1)} %shard_map.111.refs_3_.refs_6_), channel_id=1, source_target_pairs={{0,8},{8,16},{16,24},{24,32},{32,40},{40,48},{48,56},{56,0},{64,12... | collective-permute-start | bytes 983048 | tf_op jit(solution)/shard_map/ppermute | solution.py:503
  54.6 0.0 collective-permute-done.13.refs_4_.refs_5_
  54.6 1.3 %collective-permute-start.14 = (bf16[256,640]{1,0:T(8,128)(2,1)S(1)}, bf16[256,640]{1,0:T(8,128)(2,1)S(1)}, u32[]{:S(2)}, u32[]{:S(2)}) collective-permute-start(bf16[256,640]{1,0:T(8,128)(2,1)S(1)} %collective-permute-done.13.refs_4_.refs_5_), channel_id=1, source_target_pairs={{0,8},{8,16},{16,24},{24,32},{32,40},{40,48},{48,56},{56,0},{64,12... | collective-permute-start | bytes 983048 | tf_op jit(solution)/shard_map/ppermute | solution.py:503
  55.9 4.9 %shard_map.112 = (f32[5,512,256]{2,1,0:T(8,128)S(1)}, bf16[5,512,128]{2,1,0:T(8,128)(2,1)S(1)}) custom-call(bf16[4,128,640]{2,1,0:T(8,128)(2,1)S(1)} %copy-done.1, bf16[4,128,640]{2,1,0:T(8,128)(2,1)S(1)} %copy-done.4, bf16[4,128,640]{2,1,0:T(8,128)(2,1)S(1)} %copy-done.5), custom_call_target="tpu_custom_call" | custom-call | flops 167772160 | bytes 6291456 | tf_op jit(solution)/shard_map/pallas_call | solution.py:426
  60.8 0.9 %collective-permute-start.11 = (bf16[256,640]{1,0:T(8,128)(2,1)S(1)}, bf16[256,640]{1,0:T(8,128)(2,1)S(1)}, u32[]{:S(2)}, u32[]{:S(2)}) collective-permute-start(bf16[256,640]{1,0:T(8,128)(2,1)S(1)} %collective-permute-done.10.refs_7_.refs_14_), channel_id=1, source_target_pairs={{0,8},{8,16},{16,24},{24,32},{32,40},{40,48},{48,56},{56,0},{64,12... | collective-permute-start | bytes 983048 | tf_op jit(solution)/shard_map/ppermute | solution.py:503
  61.8 1.0 %collective-permute-done.14.refs_9_.refs_12_ = bf16[256,640]{1,0:T(8,128)(2,1)S(1)} collective-permute-done((bf16[256,640]{1,0:T(8,128)(2,1)S(1)}, bf16[256,640]{1,0:T(8,128)(2,1)S(1)}, u32[]{:S(2)}, u32[]{:S(2)}) %collective-permute-start.14) | collective-permute-done | bytes 327712 | tf_op jit(solution)/shard_map/ppermute | solution.py:503
  62.7 2.5 %collective-permute-start.15 = (bf16[256,640]{1,0:T(8,128)(2,1)S(1)}, bf16[256,640]{1,0:T(8,128)(2,1)S(1)}, u32[]{:S(2)}, u32[]{:S(2)}) collective-permute-start(bf16[256,640]{1,0:T(8,128)(2,1)S(1)} %collective-permute-done.14.refs_9_.refs_12_), channel_id=1, source_target_pairs={{0,8},{8,16},{16,24},{24,32},{32,40},{40,48},{48,56},{56,0},{64,12... | collective-permute-start | bytes 983048 | tf_op jit(solution)/shard_map/ppermute | solution.py:503
  65.3 0.5 collective-permute-start.17
  65.8 1.3 %collective-permute-done.11.refs_3_.refs_10_ = bf16[256,640]{1,0:T(8,128)(2,1)S(1)} collective-permute-done((bf16[256,640]{1,0:T(8,128)(2,1)S(1)}, bf16[256,640]{1,0:T(8,128)(2,1)S(1)}, u32[]{:S(2)}, u32[]{:S(2)}) %collective-permute-start.11) | collective-permute-done | bytes 327712 | tf_op jit(solution)/shard_map/ppermute | solution.py:503
  67.1 1.8 %collective-permute-start.12 = (bf16[256,640]{1,0:T(8,128)(2,1)S(1)}, bf16[256,640]{1,0:T(8,128)(2,1)S(1)}, u32[]{:S(2)}, u32[]{:S(2)}) collective-permute-start(bf16[256,640]{1,0:T(8,128)(2,1)S(1)} %collective-permute-done.11.refs_3_.refs_10_), channel_id=1, source_target_pairs={{0,8},{8,16},{16,24},{24,32},{32,40},{40,48},{48,56},{56,0},{64,12... | collective-permute-start | bytes 983048 | tf_op jit(solution)/shard_map/ppermute | solution.py:503
  68.9 0.8 collective-permute-start.19
  69.7 1.0 %collective-permute-done.15.refs_5_.refs_8_ = bf16[256,640]{1,0:T(8,128)(2,1)S(1)} collective-permute-done((bf16[256,640]{1,0:T(8,128)(2,1)S(1)}, bf16[256,640]{1,0:T(8,128)(2,1)S(1)}, u32[]{:S(2)}, u32[]{:S(2)}) %collective-permute-start.15) | collective-permute-done | bytes 327712 | tf_op jit(solution)/shard_map/ppermute | solution.py:503
  70.6 2.0 %collective-permute-start.22 = (bf16[256,640]{1,0:T(8,128)(2,1)S(1)}, bf16[256,640]{1,0:T(8,128)(2,1)S(1)}, u32[]{:S(2)}, u32[]{:S(2)}) collective-permute-start(bf16[256,640]{1,0:T(8,128)(2,1)S(1)} %collective-permute-done.15.refs_5_.refs_8_), channel_id=1, source_target_pairs={{0,8},{8,16},{16,24},{24,32},{32,40},{40,48},{48,56},{56,0},{64,12... | collective-permute-start | bytes 983048 | tf_op jit(solution)/shard_map/ppermute | solution.py:503
  72.6 0.6 collective-permute-start.20
  73.2 2.5 %shard_map.113 = (f32[5,512,256]{2,1,0:T(8,128)S(1)}, bf16[5,512,128]{2,1,0:T(8,128)(2,1)S(1)}) custom-call(bf16[4,128,640]{2,1,0:T(8,128)(2,1)S(1)} %copy-done.1, f32[5,512,256]{2,1,0:T(8,128)S(1)} %get-tuple-element.50.refs_1_, bf16[5,512,128]{2,1,0:T(8,128)(2,1)S(1)} %get-tuple-element.51.refs_2_, bf16[256,640]{1,0:T(8,128)(2,1)S(1)} %shard_map.111.refs_3_.refs_6_, ...), custom_call_target="tpu_custom_call" | custom-call | flops 1006632960 | bytes 8388608 | tf_op jit(solution)/shard_map/pallas_call | solution.py:463
  75.7 3.0 %collective-permute-start.18 = (bf16[256,640]{1,0:T(8,128)(2,1)S(1)}, bf16[256,640]{1,0:T(8,128)(2,1)S(1)}, u32[]{:S(2)}, u32[]{:S(2)}) collective-permute-start(bf16[256,640]{1,0:T(8,128)(2,1)S(1)} %collective-permute-done.12.refs_3_.refs_10_), channel_id=1, source_target_pairs={{0,8},{8,16},{16,24},{24,32},{32,40},{40,48},{48,56},{56,0},{64,12... | collective-permute-start | bytes 983048 | tf_op jit(solution)/shard_map/ppermute | solution.py:503
  78.7 2.7 %collective-permute-start.23 = (bf16[256,640]{1,0:T(8,128)(2,1)S(1)}, bf16[256,640]{1,0:T(8,128)(2,1)S(1)}, u32[]{:S(2)}, u32[]{:S(2)}) collective-permute-start(bf16[256,640]{1,0:T(8,128)(2,1)S(1)} %collective-permute-done.22.refs_5_.refs_8_), channel_id=1, source_target_pairs={{0,64},{64,0},{128,192},{192,128},{1,65},{65,1},{129,193},{193,129... | collective-permute-start | bytes 983048 | tf_op jit(solution)/shard_map/ppermute | solution.py:506
  81.5 1.8 %shard_map.114 = (f32[5,512,256]{2,1,0:T(8,128)S(1)}, bf16[5,512,128]{2,1,0:T(8,128)(2,1)S(1)}) custom-call(bf16[4,128,640]{2,1,0:T(8,128)(2,1)S(1)} %copy-done.1, f32[5,512,256]{2,1,0:T(8,128)S(1)} %get-tuple-element.55.refs_1_, bf16[5,512,128]{2,1,0:T(8,128)(2,1)S(1)} %get-tuple-element.56.refs_2_, ...), custom_call_target="tpu_custom_call" | custom-call | flops 671088640 | bytes 8388608 | tf_op jit(solution)/shard_map/pallas_call | solution.py:463
  83.3 0.0 copy-start.10
  83.3 2.9 %collective-permute-start.24 = (bf16[256,640]{1,0:T(8,128)(2,1)S(1)}, bf16[256,640]{1,0:T(8,128)(2,1)S(1)}, u32[]{:S(2)}, u32[]{:S(2)}) collective-permute-start(bf16[256,640]{1,0:T(8,128)(2,1)S(1)} %collective-permute-done.18.refs_4_.refs_7_), channel_id=1, source_target_pairs={{0,64},{64,0},{128,192},{192,128},{1,65},{65,1},{129,193},{193,129... | collective-permute-start | bytes 983048 | tf_op jit(solution)/shard_map/ppermute | solution.py:506
  86.3 1.8 %shard_map.115 = (f32[5,512,256]{2,1,0:T(8,128)S(1)}, bf16[5,512,128]{2,1,0:T(8,128)(2,1)S(1)}) custom-call(bf16[4,128,640]{2,1,0:T(8,128)(2,1)S(1)} %copy-done.1, f32[5,512,256]{2,1,0:T(8,128)S(1)} %get-tuple-element.60.refs_1_, bf16[5,512,128]{2,1,0:T(8,128)(2,1)S(1)} %get-tuple-element.61.refs_2_, ...), custom_call_target="tpu_custom_call" | custom-call | flops 671088640 | bytes 8388608 | tf_op jit(solution)/shard_map/pallas_call | solution.py:463
  88.1 2.5 %shard_map.116 = bf16[4,128,640]{2,1,0:T(8,128)(2,1)} custom-call(s32[4]{0:T(128)S(1)} %copy-done.10, bf16[4,128,640]{2,1,0:T(8,128)(2,1)S(1)} %copy-done.1, f32[5,512,256]{2,1,0:T(8,128)S(1)} %get-tuple-element.62.refs_2_, bf16[5,512,128]{2,1,0:T(8,128)(2,1)S(1)} %get-tuple-element.63.refs_3_, bf16[256,640]{1,0:T(8,128)(2,1)S(1)} %collective-permute-done.18.refs_4_.refs_7_, ...), custom_call_target="tpu_custom_call" | custom-call | flops 335544320 | bytes 8388608 | tf_op jit(solution)/shard_map/pallas_call | solution.py:463
  (25 shorter events, 0.1 us)
Async XLA Ops:
  0.0 7.6 %collective-permute-start = (bf16[1024,1152]{1,0:T(8,128)(2,1)}, bf16[1024,1152]{1,0:T(8,128)(2,1)S(1)}, u32[]{:S(2)}, u32[]{:S(2)}) collective-permute-start(bf16[1024,1152]{1,0:T(8,128)(2,1)} %hidden.5), channel_id=1, source_target_pairs={{0,64},{64,0},{128,192},{192,128},{1,65},{65,1},{129,193},{193,129... | collective-permute-start | bytes 7077896 | tf_op jit(solution)/shard_map/ppermute | solution.py:506
  3.2 1.7 %copy-start = (bf16[1024,1152]{1,0:T(8,128)(2,1)S(1)}, bf16[1024,1152]{1,0:T(8,128)(2,1)}, u32[]{:S(2)}) copy-start(bf16[1024,1152]{1,0:T(8,128)(2,1)} %hidden.5) | copy-start | bytes 7077892
  4.9 0.7 copy-start.6
  5.6 0.7 copy-start.7
  6.3 0.7 copy-start.9
  6.3 1.4 %copy-start.2 = (bf16[1152,640]{1,0:T(8,128)(2,1)S(1)}, bf16[1152,640]{1,0:T(8,128)(2,1)}, u32[]{:S(2)}) copy-start(bf16[1152,640]{1,0:T(8,128)(2,1)} %rest_0_.1) | copy-start | bytes 4423684
  6.3 1.8 %copy-start.3 = (bf16[1152,640]{1,0:T(8,128)(2,1)S(1)}, bf16[1152,640]{1,0:T(8,128)(2,1)}, u32[]{:S(2)}) copy-start(bf16[1152,640]{1,0:T(8,128)(2,1)} %rest_1_.1) | copy-start | bytes 4423684
  9.9 10.8 %collective-permute-start.1 = (bf16[240,640]{1,0:T(8,128)(2,1)S(1)}, bf16[240,640]{1,0:T(8,128)(2,1)S(1)}, u32[]{:S(2)}, u32[]{:S(2)}) collective-permute-start(bf16[240,640]{1,0:T(8,128)(2,1)S(1)} %get-tuple-element.38), channel_id=1, source_target_pairs={{0,8},{8,16},{16,24},{24,32},{32,40},{40,48},{48,56},{56,0},{64,12... | collective-permute-start | bytes 921608 | tf_op jit(solution)/shard_map/ppermute | solution.py:503
  15.6 6.1 %collective-permute-start.5 = (bf16[240,640]{1,0:T(8,128)(2,1)S(1)}, bf16[240,640]{1,0:T(8,128)(2,1)S(1)}, u32[]{:S(2)}, u32[]{:S(2)}) collective-permute-start(bf16[240,640]{1,0:T(8,128)(2,1)S(1)} %get-tuple-element.42), channel_id=1, source_target_pairs={{0,8},{8,16},{16,24},{24,32},{32,40},{40,48},{48,56},{56,0},{64,12... | collective-permute-start | bytes 921608 | tf_op jit(solution)/shard_map/ppermute | solution.py:503
  20.7 6.1 %collective-permute-start.2 = (bf16[240,640]{1,0:T(8,128)(2,1)S(1)}, bf16[240,640]{1,0:T(8,128)(2,1)S(1)}, u32[]{:S(2)}, u32[]{:S(2)}) collective-permute-start(bf16[240,640]{1,0:T(8,128)(2,1)S(1)} %shard_map.105), channel_id=1, source_target_pairs={{0,8},{8,16},{16,24},{24,32},{32,40},{40,48},{48,56},{56,0},{64,12... | collective-permute-start | bytes 921608 | tf_op jit(solution)/shard_map/ppermute | solution.py:503
  21.7 25.8 %copy-start.8 = (s32[4]{0:T(128)S(1)}, s32[4]{0:T(128)}, u32[]{:S(2)}) copy-start(s32[4]{0:T(128)} %counts.7) | copy-start | bytes 52
  21.8 8.3 %collective-permute-start.6 = (bf16[240,640]{1,0:T(8,128)(2,1)S(1)}, bf16[240,640]{1,0:T(8,128)(2,1)S(1)}, u32[]{:S(2)}, u32[]{:S(2)}) collective-permute-start(bf16[240,640]{1,0:T(8,128)(2,1)S(1)} %shard_map.108), channel_id=1, source_target_pairs={{0,8},{8,16},{16,24},{24,32},{32,40},{40,48},{48,56},{56,0},{64,12... | collective-permute-start | bytes 921608 | tf_op jit(solution)/shard_map/ppermute | solution.py:503
  26.9 29.0 %copy-start.1 = (bf16[4,128,640]{2,1,0:T(8,128)(2,1)S(1)}, bf16[4,128,640]{2,1,0:T(8,128)(2,1)}, u32[]{:S(2)}) copy-start(bf16[4,128,640]{2,1,0:T(8,128)(2,1)} %refs_1_.5) | copy-start | bytes 1966084
  26.9 29.0 %copy-start.4 = (bf16[4,128,640]{2,1,0:T(8,128)(2,1)S(1)}, bf16[4,128,640]{2,1,0:T(8,128)(2,1)}, u32[]{:S(2)}) copy-start(bf16[4,128,640]{2,1,0:T(8,128)(2,1)} %own_k.1) | copy-start | bytes 1966084
  26.9 29.0 %copy-start.5 = (bf16[4,128,640]{2,1,0:T(8,128)(2,1)S(1)}, bf16[4,128,640]{2,1,0:T(8,128)(2,1)}, u32[]{:S(2)}) copy-start(bf16[4,128,640]{2,1,0:T(8,128)(2,1)} %own_v.1) | copy-start | bytes 1966084
  27.0 6.5 %collective-permute-start.3 = (bf16[240,640]{1,0:T(8,128)(2,1)S(1)}, bf16[240,640]{1,0:T(8,128)(2,1)S(1)}, u32[]{:S(2)}, u32[]{:S(2)}) collective-permute-start(bf16[240,640]{1,0:T(8,128)(2,1)S(1)} %shard_map.106), channel_id=1, source_target_pairs={{0,8},{8,16},{16,24},{24,32},{32,40},{40,48},{48,56},{56,0},{64,12... | collective-permute-start | bytes 921608 | tf_op jit(solution)/shard_map/ppermute | solution.py:503
  30.1 6.6 %collective-permute-start.7 = (bf16[240,640]{1,0:T(8,128)(2,1)S(1)}, bf16[240,640]{1,0:T(8,128)(2,1)S(1)}, u32[]{:S(2)}, u32[]{:S(2)}) collective-permute-start(bf16[240,640]{1,0:T(8,128)(2,1)S(1)} %shard_map.109), channel_id=1, source_target_pairs={{0,8},{8,16},{16,24},{24,32},{32,40},{40,48},{48,56},{56,0},{64,12... | collective-permute-start | bytes 921608 | tf_op jit(solution)/shard_map/ppermute | solution.py:503
  33.5 6.5 %collective-permute-start.4 = (bf16[240,640]{1,0:T(8,128)(2,1)S(1)}, bf16[240,640]{1,0:T(8,128)(2,1)S(1)}, u32[]{:S(2)}, u32[]{:S(2)}) collective-permute-start(bf16[240,640]{1,0:T(8,128)(2,1)S(1)} %shard_map.107), channel_id=1, source_target_pairs={{0,8},{8,16},{16,24},{24,32},{32,40},{40,48},{48,56},{56,0},{64,12... | collective-permute-start | bytes 921608 | tf_op jit(solution)/shard_map/ppermute | solution.py:503
  36.7 3.4 %collective-permute-start.8 = (bf16[240,640]{1,0:T(8,128)(2,1)S(1)}, bf16[240,640]{1,0:T(8,128)(2,1)S(1)}, u32[]{:S(2)}, u32[]{:S(2)}) collective-permute-start(bf16[240,640]{1,0:T(8,128)(2,1)S(1)} %collective-permute-done.7), channel_id=1, source_target_pairs={{0,64},{64,0},{128,192},{192,128},{1,65},{65,1},{129,193},{193,129... | collective-permute-start | bytes 921608 | tf_op jit(solution)/shard_map/ppermute | solution.py:506
  40.5 7.1 %collective-permute-start.9 = (bf16[224,640]{1,0:T(8,128)(2,1)S(1)}, bf16[224,640]{1,0:T(8,128)(2,1)S(1)}, u32[]{:S(2)}, u32[]{:S(2)}) collective-permute-start(bf16[224,640]{1,0:T(8,128)(2,1)S(1)} %shard_map.110.rows), channel_id=1, source_target_pairs={{0,128},{64,192},{128,0},{192,64},{1,129},{65,193},{129,1},{193,65... | collective-permute-start | bytes 860168 | tf_op jit(solution)/shard_map/ppermute | solution.py:531
  48.2 6.4 %collective-permute-start.13 = (bf16[256,640]{1,0:T(8,128)(2,1)S(1)}, bf16[256,640]{1,0:T(8,128)(2,1)S(1)}, u32[]{:S(2)}, u32[]{:S(2)}) collective-permute-start(bf16[256,640]{1,0:T(8,128)(2,1)S(1)} %shard_map.111.refs_3_.refs_6_), channel_id=1, source_target_pairs={{0,64},{64,0},{128,192},{192,128},{1,65},{65,1},{129,193},{193,129... | collective-permute-start | bytes 983048 | tf_op jit(solution)/shard_map/ppermute | solution.py:506
  53.0 7.8 %collective-permute-start.10 = (bf16[256,640]{1,0:T(8,128)(2,1)S(1)}, bf16[256,640]{1,0:T(8,128)(2,1)S(1)}, u32[]{:S(2)}, u32[]{:S(2)}) collective-permute-start(bf16[256,640]{1,0:T(8,128)(2,1)S(1)} %shard_map.111.refs_3_.refs_6_), channel_id=1, source_target_pairs={{0,8},{8,16},{16,24},{24,32},{32,40},{40,48},{48,56},{56,0},{64,12... | collective-permute-start | bytes 983048 | tf_op jit(solution)/shard_map/ppermute | solution.py:503
  54.6 8.1 %collective-permute-start.14 = (bf16[256,640]{1,0:T(8,128)(2,1)S(1)}, bf16[256,640]{1,0:T(8,128)(2,1)S(1)}, u32[]{:S(2)}, u32[]{:S(2)}) collective-permute-start(bf16[256,640]{1,0:T(8,128)(2,1)S(1)} %collective-permute-done.13.refs_4_.refs_5_), channel_id=1, source_target_pairs={{0,8},{8,16},{16,24},{24,32},{32,40},{40,48},{48,56},{56,0},{64,12... | collective-permute-start | bytes 983048 | tf_op jit(solution)/shard_map/ppermute | solution.py:503
  60.8 6.3 %collective-permute-start.11 = (bf16[256,640]{1,0:T(8,128)(2,1)S(1)}, bf16[256,640]{1,0:T(8,128)(2,1)S(1)}, u32[]{:S(2)}, u32[]{:S(2)}) collective-permute-start(bf16[256,640]{1,0:T(8,128)(2,1)S(1)} %collective-permute-done.10.refs_7_.refs_14_), channel_id=1, source_target_pairs={{0,8},{8,16},{16,24},{24,32},{32,40},{40,48},{48,56},{56,0},{64,12... | collective-permute-start | bytes 983048 | tf_op jit(solution)/shard_map/ppermute | solution.py:503
  62.7 7.9 %collective-permute-start.15 = (bf16[256,640]{1,0:T(8,128)(2,1)S(1)}, bf16[256,640]{1,0:T(8,128)(2,1)S(1)}, u32[]{:S(2)}, u32[]{:S(2)}) collective-permute-start(bf16[256,640]{1,0:T(8,128)(2,1)S(1)} %collective-permute-done.14.refs_9_.refs_12_), channel_id=1, source_target_pairs={{0,8},{8,16},{16,24},{24,32},{32,40},{40,48},{48,56},{56,0},{64,12... | collective-permute-start | bytes 983048 | tf_op jit(solution)/shard_map/ppermute | solution.py:503
  65.3 7.4 %collective-permute-start.16 = (bf16[256,640]{1,0:T(8,128)(2,1)S(1)}, bf16[256,640]{1,0:T(8,128)(2,1)S(1)}, u32[]{:S(2)}, u32[]{:S(2)}) collective-permute-start(bf16[256,640]{1,0:T(8,128)(2,1)S(1)} %collective-permute-done.10.refs_7_.refs_14_), channel_id=1, source_target_pairs={{0,64},{64,0},{128,192},{192,128},{1,65},{65,1},{129,193},{193,129... | collective-permute-start | bytes 983048 | tf_op jit(solution)/shard_map/ppermute | solution.py:506
  65.3 7.9 %collective-permute-start.17 = (bf16[256,640]{1,0:T(8,128)(2,1)S(1)}, bf16[256,640]{1,0:T(8,128)(2,1)S(1)}, u32[]{:S(2)}, u32[]{:S(2)}) collective-permute-start(bf16[256,640]{1,0:T(8,128)(2,1)S(1)} %collective-permute-done.14.refs_9_.refs_12_), channel_id=1, source_target_pairs={{0,64},{64,0},{128,192},{192,128},{1,65},{65,1},{129,193},{193,129... | collective-permute-start | bytes 983048 | tf_op jit(solution)/shard_map/ppermute | solution.py:506
  67.1 8.6 %collective-permute-start.12 = (bf16[256,640]{1,0:T(8,128)(2,1)S(1)}, bf16[256,640]{1,0:T(8,128)(2,1)S(1)}, u32[]{:S(2)}, u32[]{:S(2)}) collective-permute-start(bf16[256,640]{1,0:T(8,128)(2,1)S(1)} %collective-permute-done.11.refs_3_.refs_10_), channel_id=1, source_target_pairs={{0,8},{8,16},{16,24},{24,32},{32,40},{40,48},{48,56},{56,0},{64,12... | collective-permute-start | bytes 983048 | tf_op jit(solution)/shard_map/ppermute | solution.py:503
  68.9 12.6 %collective-permute-start.19 = (bf16[256,640]{1,0:T(8,128)(2,1)S(1)}, bf16[256,640]{1,0:T(8,128)(2,1)S(1)}, u32[]{:S(2)}, u32[]{:S(2)}) collective-permute-start(bf16[256,640]{1,0:T(8,128)(2,1)S(1)} %collective-permute-done.11.refs_3_.refs_10_), channel_id=1, source_target_pairs={{0,64},{64,0},{128,192},{192,128},{1,65},{65,1},{129,193},{193,129... | collective-permute-start | bytes 983048 | tf_op jit(solution)/shard_map/ppermute | solution.py:506
  70.6 8.1 %collective-permute-start.22 = (bf16[256,640]{1,0:T(8,128)(2,1)S(1)}, bf16[256,640]{1,0:T(8,128)(2,1)S(1)}, u32[]{:S(2)}, u32[]{:S(2)}) collective-permute-start(bf16[256,640]{1,0:T(8,128)(2,1)S(1)} %collective-permute-done.15.refs_5_.refs_8_), channel_id=1, source_target_pairs={{0,8},{8,16},{16,24},{24,32},{32,40},{40,48},{48,56},{56,0},{64,12... | collective-permute-start | bytes 983048 | tf_op jit(solution)/shard_map/ppermute | solution.py:503
  72.6 8.8 %collective-permute-start.20 = (bf16[256,640]{1,0:T(8,128)(2,1)S(1)}, bf16[256,640]{1,0:T(8,128)(2,1)S(1)}, u32[]{:S(2)}, u32[]{:S(2)}) collective-permute-start(bf16[256,640]{1,0:T(8,128)(2,1)S(1)} %collective-permute-done.15.refs_5_.refs_8_), channel_id=1, source_target_pairs={{0,64},{64,0},{128,192},{192,128},{1,65},{65,1},{129,193},{193,129... | collective-permute-start | bytes 983048 | tf_op jit(solution)/shard_map/ppermute | solution.py:506
  75.7 7.6 %collective-permute-start.18 = (bf16[256,640]{1,0:T(8,128)(2,1)S(1)}, bf16[256,640]{1,0:T(8,128)(2,1)S(1)}, u32[]{:S(2)}, u32[]{:S(2)}) collective-permute-start(bf16[256,640]{1,0:T(8,128)(2,1)S(1)} %collective-permute-done.12.refs_3_.refs_10_), channel_id=1, source_target_pairs={{0,8},{8,16},{16,24},{24,32},{32,40},{40,48},{48,56},{56,0},{64,12... | collective-permute-start | bytes 983048 | tf_op jit(solution)/shard_map/ppermute | solution.py:503
  78.7 7.5 %collective-permute-start.21 = (bf16[256,640]{1,0:T(8,128)(2,1)S(1)}, bf16[256,640]{1,0:T(8,128)(2,1)S(1)}, u32[]{:S(2)}, u32[]{:S(2)}) collective-permute-start(bf16[256,640]{1,0:T(8,128)(2,1)S(1)} %collective-permute-done.12.refs_3_.refs_10_), channel_id=1, source_target_pairs={{0,64},{64,0},{128,192},{192,128},{1,65},{65,1},{129,193},{193,129... | collective-permute-start | bytes 983048 | tf_op jit(solution)/shard_map/ppermute | solution.py:506
  78.7 7.5 %collective-permute-start.23 = (bf16[256,640]{1,0:T(8,128)(2,1)S(1)}, bf16[256,640]{1,0:T(8,128)(2,1)S(1)}, u32[]{:S(2)}, u32[]{:S(2)}) collective-permute-start(bf16[256,640]{1,0:T(8,128)(2,1)S(1)} %collective-permute-done.22.refs_5_.refs_8_), channel_id=1, source_target_pairs={{0,64},{64,0},{128,192},{192,128},{1,65},{65,1},{129,193},{193,129... | collective-permute-start | bytes 983048 | tf_op jit(solution)/shard_map/ppermute | solution.py:506
  83.3 4.8 %copy-start.10 = (s32[4]{0:T(128)S(1)}, s32[4]{0:T(128)}, u32[]{:S(2)}) copy-start(s32[4]{0:T(128)} %refs_0_.11) | copy-start | bytes 52
  83.3 4.8 %collective-permute-start.24 = (bf16[256,640]{1,0:T(8,128)(2,1)S(1)}, bf16[256,640]{1,0:T(8,128)(2,1)S(1)}, u32[]{:S(2)}, u32[]{:S(2)}) collective-permute-start(bf16[256,640]{1,0:T(8,128)(2,1)S(1)} %collective-permute-done.18.refs_4_.refs_7_), channel_id=1, source_target_pairs={{0,64},{64,0},{128,192},{192,128},{1,65},{65,1},{129,193},{193,129... | collective-permute-start | bytes 983048 | tf_op jit(solution)/shard_map/ppermute | solution.py:506
